TPU v7x, 32 devices: a whole 2x2x4 slice. The times are simulated.
32 devices in a mesh: mp: 8 (over y, x, core), replica: 4 (over z).
Axes of the slice: x: 2, y: 2, z: 4, core: 2. Of those that a mesh axis runs over, the one named last changes fastest.
Arguments:
- table: float32 [32768, 128], P('mp'), may hold values from -6 to 6
- accum: float32 [32768, 128], P('mp'), may hold values from 100 to 1000
- lookup_slots: int32 [4096, 32], P('replica', 'mp'), may hold values from 0 to 1023
- lookup_weights: int32 [4096, 32], P('replica', 'mp'), may hold values from 1 to 3
- touched_rows: int32 [8192], P('mp'), may hold values from 0 to 4095, as said below
- pooled_grad: bfloat16 [4096, 128], P(('replica', 'mp')), may hold values from -6 to 6
Outputs:
- pooled: float32 [4096, 128], P(('replica', 'mp'))
- new_table: float32 [32768, 128], P('mp')
- new_accum: float32 [32768, 128], P('mp')
Inputs may be any that keep to these rules, and one draw needn't show every extreme that they name: `touched_rows`: within each shard's block of 1024 entries the row ids are distinct.
All inputs are finite; a program needn't handle non-finite values.
Results may differ from a plain program's by a relative error of at most 0.0029.
Values may be sent and summed in bfloat16 or wider, within the bound.
No kernel may reach another device: no remote copies, remote signals or barrier semaphores. Data moves between devices by JAX's collectives and lax.ppermute only.
A program may use at most 64 MiB of HBM per device.

v0:
```python
import math

import jax
import jax.numpy as jnp
from jax import lax
from jax.sharding import PartitionSpec as P

learn_rate = 0.5


def build_counts(slots, weights, touch_count):
    bag_count = slots.shape[0]
    block_rows = math.gcd(bag_count, 512)
    columns = jnp.arange(touch_count, dtype=jnp.int32)

    def one_block(block_index):
        slot_block = lax.dynamic_slice_in_dim(slots, block_index * block_rows, block_rows, 0)
        weight_block = lax.dynamic_slice_in_dim(weights, block_index * block_rows, block_rows, 0)
        matches = (slot_block[:, :, None] == columns[None, None, :]).astype(jnp.float32)
        return jnp.sum(matches * weight_block[:, :, None].astype(jnp.float32), axis=1).astype(
            jnp.bfloat16
        )

    blocks = lax.map(one_block, jnp.arange(bag_count // block_rows, dtype=jnp.int32))
    return blocks.reshape(bag_count, touch_count)


def adagrad(row_values, history, gradient):
    history_new = history + gradient * gradient
    return (row_values - learn_rate * gradient / jnp.sqrt(history_new), history_new)


def per_device(table, accum, lookup_slots, lookup_weights, touched_rows, pooled_grad):
    touch_count = touched_rows.shape[0]
    feature_dim = table.shape[1]
    bag_local = pooled_grad.shape[0]
    mp_count = lax.axis_size("mp")
    counts = build_counts(lookup_slots, lookup_weights, touch_count)
    row_tile = table[touched_rows]
    tile_low = row_tile.astype(jnp.bfloat16)
    partial_value = jnp.dot(counts, tile_low, preferred_element_type=jnp.float32)
    received = lax.all_to_all(
        partial_value.reshape(mp_count, bag_local, feature_dim),
        "mp",
        split_axis=0,
        concat_axis=0,
        tiled=True,
    )
    pooled = jnp.sum(received, axis=0)
    local_grad = lax.dot_general(
        counts,
        lax.all_gather(pooled_grad, "mp", axis=0, tiled=True),
        (((0,), (0,)), ((), ())),
        preferred_element_type=jnp.float32,
    )
    gradient = lax.psum(local_grad.astype(jnp.bfloat16), "replica").astype(jnp.float32)
    new_rows, new_history = adagrad(row_tile, accum[touched_rows], gradient)
    new_table = table.at[touched_rows].set(new_rows)
    new_accum = accum.at[touched_rows].set(new_history)
    return (pooled, new_table, new_accum)


def solution(mesh):
    placed = (
        P("mp", None),
        P("mp", None),
        P("replica", "mp"),
        P("replica", "mp"),
        P("mp"),
        P(("replica", "mp"), None),
    )
    return jax.shard_map(
        per_device,
        mesh=mesh,
        in_specs=placed,
        out_specs=(P(("replica", "mp"), None), P("mp", None), P("mp", None)),
        check_vma=False,
    )
```

profile of v0, /device:TPU:0, one launch (start us, length us, event | category | flops | bytes accessed | tf_op | source)
XLA Modules:
  0.0 101.4 jit_solution(8591296899414771870)
XLA Ops:
  7.2 0.0 copy-start.1
  7.2 1.7 %copy.23 = f32[4096,128]{1,0:T(8,128)S(1)} copy(f32[4096,128]{1,0:T(8,128)} %param.8) | data formatting | bytes 4194304
  8.9 0.5 copy-done.1
  9.4 0.0 copy-start.3
  9.4 0.0 copy-start.4
  9.4 1.3 %copy.24 = f32[4096,128]{1,0:T(8,128)} copy(f32[4096,128]{1,0:T(8,128)S(1)} %copy-done.1) | data formatting | bytes 4194304
  10.7 0.0 copy-done.3
  10.7 0.0 copy-done.4
  10.7 0.0 copy-start.6
  10.7 7.6 %while.11 = (s32[]{:T(128)}, bf16[2,512,1024]{2,1,0:T(8,128)(2,1)}, s32[2]{0:T(128)S(1)}, s32[1024,4]{0,1:T(4,128)S(1)}, s32[1024,4]{0,1:T(4,128)S(1)}, /*index=5*/s32[]{:T(128)}, s32[1]{0:T(128)}, s32[]{:T(128)}, s32[]{:T(128)}) while((s32[]{:T(128)}, bf16[2,512,1024]{2,1,0:T(8,128)(2,1)}, s32[2]{0:T(128)S(1)}, ...), condition=%wide.region_2.3_spmd.clone, body=%wide.region_0.2_spmd.clone.sunk | while | flops 5769222 | bytes 3195047 | solution.py:24
  10.7 0.7 dynamic_slice.18
  12.1 1.4 %select_reduce_fusion.2 = bf16[512,1024]{1,0:T(8,128)(2,1)S(1)} fusion(f32[512,4]{0,1:T(4,128)S(1)} %get-tuple-element.95, s32[512,4]{0,1:T(4,128)S(1)} %get-tuple-element.96), kind=kLoop, calls=%fused_computation.6.clone.1 | loop fusion | flops 5767168 | bytes 1064960 | tf_op jit(solution)/shard_map/while/body/eval_jaxpr/reduce_sum | solution.py:20
  13.5 1.0 %bitcast_dynamic-update-slice_fusion.2 = bf16[2,512,1024]{2,1,0:T(8,128)(2,1)} fusion(bf16[2,512,1024]{2,1,0:T(8,128)(2,1)} %get-tuple-element.107, s32[]{:T(128)S(6)} %copy.14, bf16[512,1024]{1,0:T(8,128)(2,1)S(1)} %select_reduce_fusion.2), kind=kLoop, calls=%fused_computation.7.clone.1 | loop fusion | bytes 2097156 | tf_op jit(solution)/shard_map/while/body/jit(dynamic_update_index_in_dim)/dynamic_update_slice | solution.py:24
  14.5 0.6 dynamic_slice.18
  15.8 1.4 %select_reduce_fusion.2 = bf16[512,1024]{1,0:T(8,128)(2,1)S(1)} fusion(f32[512,4]{0,1:T(4,128)S(1)} %get-tuple-element.95, s32[512,4]{0,1:T(4,128)S(1)} %get-tuple-element.96), kind=kLoop, calls=%fused_computation.6.clone.1 | loop fusion | flops 5767168 | bytes 1064960 | tf_op jit(solution)/shard_map/while/body/eval_jaxpr/reduce_sum | solution.py:20
  17.3 1.0 %bitcast_dynamic-update-slice_fusion.2 = bf16[2,512,1024]{2,1,0:T(8,128)(2,1)} fusion(bf16[2,512,1024]{2,1,0:T(8,128)(2,1)} %get-tuple-element.107, s32[]{:T(128)S(6)} %copy.14, bf16[512,1024]{1,0:T(8,128)(2,1)S(1)} %select_reduce_fusion.2), kind=kLoop, calls=%fused_computation.7.clone.1 | loop fusion | bytes 2097156 | tf_op jit(solution)/shard_map/while/body/jit(dynamic_update_index_in_dim)/dynamic_update_slice | solution.py:24
  18.3 0.0 copy-done.6
  18.3 2.8 %gather_fusion = f32[1024,128]{1,0:T(8,128)S(1)} fusion(f32[4096,128]{1,0:T(8,128)S(1)} %copy.23, s32[1024]{0:T(1024)S(1)} %get-tuple-element.61), kind=kCustom, calls=%fused_computation | custom fusion | bytes 1052672 | tf_op jit(solution)/shard_map/gather | solution.py:39
  21.1 0.0 copy-start.5
  21.1 3.1 %fusion.11 = f32[8,128,128]{2,1,0:T(8,128)} fusion(bf16[8,128,1024]{2,1,0:T(8,128)(2,1)} %bitcast.15, f32[1024,128]{1,0:T(8,128)S(1)} %gather_fusion), kind=kOutput, calls=%fused_computation.19 | convolution fusion | flops 268566528 | bytes 3145728 | tf_op jit(solution)/shard_map/dot_general | solution.py:41
  24.2 5.2 %all-to-all-start = ((f32[8,128,128]{2,1,0:T(8,128)}), f32[8,128,128]{2,1,0:T(8,128)}, u32[]{:S(2)}, u32[]{:S(2)}) async-start(f32[8,128,128]{2,1,0:T(8,128)} %fusion.11), calls=%async_computation | async-start | bytes 1048576 | tf_op jit(solution)/shard_map/all_to_all | solution.py:42
  29.4 0.0 all-reduce.2.cloned.1.call-start
  29.5 0.0 copy-done.5
  29.5 13.3 %all_gather.3 = bf16[1024,128]{1,0:T(8,128)(2,1)S(1)} all-gather(bf16[128,128]{1,0:T(8,128)(2,1)S(1)} %copy-done.5), channel_id=1, replica_groups=mesh['mp'=8,'replica'=4] {'mp'}, dimensions={0}, use_global_device_ids=true | all-gather | bytes 294912 | tf_op jit(solution)/shard_map/all_gather | solution.py:52
  42.8 3.1 %convolution_convert_fusion = bf16[1024,128]{1,0:T(8,128)(2,1)} fusion(bf16[1024,1024]{1,0:T(8,128)(2,1)} %bitcast.16, bf16[1024,128]{1,0:T(8,128)(2,1)S(1)} %all_gather.3), kind=kOutput, calls=%fused_computation.10 | convolution fusion | flops 268566528 | bytes 2621440 | tf_op jit(solution)/shard_map/dot_general | solution.py:50
  45.9 0.0 all-reduce.2.cloned.1.call-update
  45.9 4.4 %gather_fusion.1 = f32[1024,128]{1,0:T(8,128)S(1)} fusion(f32[4096,128]{1,0:T(8,128)} %copy.24, s32[1024]{0:T(1024)S(1)} %get-tuple-element.61), kind=kCustom, calls=%fused_computation.1 | custom fusion | bytes 1052672 | tf_op jit(solution)/shard_map/gather | solution.py:57
  50.3 31.7 %all-reduce.2.cloned.1.call-done = bf16[1024,128]{1,0:T(8,128)(2,1)} async-done(((bf16[1024,128]{1,0:T(8,128)(2,1)}), bf16[1024,128]{1,0:T(8,128)(2,1)}) %all-reduce.2.cloned.1.call-update) | async-done | bytes 262160 | tf_op jit(solution)/shard_map/psum | solution.py:56
  82.0 0.0 copy-start.2
  82.0 6.4 %scatter_custom_fusion.1 = f32[4096,128]{1,0:T(8,128)} fusion(f32[4096,128]{1,0:T(8,128)} %copy.24, s32[1024]{0:T(1024)S(1)} %get-tuple-element.60, f32[1024,128]{1,0:T(8,128)S(1)} %gather_fusion.1, bf16[1024,128]{1,0:T(8,128)(2,1)} %all-reduce.2.cloned.1.call-done), kind=kCustom, calls=%fused_computation.18 | custom fusion | flops 393216 | bytes 2883584 | tf_op jit(solution)/shard_map/scatter | solution.py:59
  88.4 0.0 copy-done.2
  88.4 4.0 %scatter_custom_fusion = f32[4096,128]{1,0:T(8,128)S(1)} fusion(f32[4096,128]{1,0:T(8,128)S(1)} %copy.23, s32[1024]{0:T(1024)S(1)} %get-tuple-element.60, f32[1024,128]{1,0:T(8,128)S(1)} %gather_fusion, bf16[1024,128]{1,0:T(8,128)(2,1)S(1)} %copy-done.2, f32[1024,128]{1,0:T(8,128)S(1)} %gather_fusion.1, f32[]{:T(128)} %constant.26.clone.1), kind=kCustom, calls=%fused_computation.15 | custom fusion | flops 786432 | bytes 3407876 | tf_op jit(solution)/shard_map/scatter | solution.py:58
  92.4 0.0 copy-start
  92.5 0.0 all-to-all-done
  92.5 2.1 %reduce_sum.18 = f32[128,128]{1,0:T(8,128)} reduce(f32[8,128,128]{2,1,0:T(8,128)} %all-to-all-done, f32[]{:T(128)} %constant.6.clone.1), dimensions={0}, to_apply=%region_3.4 | reduce | flops 114688 | bytes 589828 | tf_op jit(solution)/shard_map/reduce_sum | solution.py:49
  94.6 0.0 copy-done
  (5 shorter events, 0.0 us)
Async XLA Ops:
  7.2 2.2 %copy-start.1 = (f32[4096,128]{1,0:T(8,128)S(1)}, f32[4096,128]{1,0:T(8,128)}, u32[]{:S(2)}) copy-start(f32[4096,128]{1,0:T(8,128)} %param.9) | copy-start | bytes 6291460
  9.4 1.3 %copy-start.3 = (s32[1024,4]{0,1:T(4,128)S(1)}, s32[1024,4]{0,1:T(4,128)}, u32[]{:S(2)}) copy-start(s32[1024,4]{0,1:T(4,128)} %param.10) | copy-start | bytes 49156
  9.4 1.3 %copy-start.4 = (s32[1024,4]{0,1:T(4,128)S(1)}, s32[1024,4]{0,1:T(4,128)}, u32[]{:S(2)}) copy-start(s32[1024,4]{0,1:T(4,128)} %param.11) | copy-start | bytes 49156
  10.7 7.6 %copy-start.6 = (s32[1024]{0:T(1024)S(1)}, s32[1024]{0:T(1024)}, u32[]{:S(2)}) copy-start(s32[1024]{0:T(1024)} %param.12) | copy-start | bytes 12292
  21.1 8.3 %copy-start.5 = (bf16[128,128]{1,0:T(8,128)(2,1)S(1)}, bf16[128,128]{1,0:T(8,128)(2,1)}, u32[]{:S(2)}) copy-start(bf16[128,128]{1,0:T(8,128)(2,1)} %param.13) | copy-start | bytes 98308
  24.2 68.2 %all-to-all-start = ((f32[8,128,128]{2,1,0:T(8,128)}), f32[8,128,128]{2,1,0:T(8,128)}, u32[]{:S(2)}, u32[]{:S(2)}) async-start(f32[8,128,128]{2,1,0:T(8,128)} %fusion.11), calls=%async_computation | async-start | bytes 1048576 | tf_op jit(solution)/shard_map/all_to_all | solution.py:42
  29.4 52.6 %all-reduce.2.cloned.1.call-start = ((), (), s32[]{:S(2)}) async-start(), calls=%async_computation.1 | async-start | bytes 524288 | tf_op jit(solution)/shard_map/psum | solution.py:56
  82.0 6.4 %copy-start.2 = (bf16[1024,128]{1,0:T(8,128)(2,1)S(1)}, bf16[1024,128]{1,0:T(8,128)(2,1)}, u32[]{:S(2)}) copy-start(bf16[1024,128]{1,0:T(8,128)(2,1)} %all-reduce.2.cloned.1.call-done) | copy-start | bytes 786436
  92.4 2.1 %copy-start = (f32[4096,128]{1,0:T(8,128)}, f32[4096,128]{1,0:T(8,128)S(1)}, u32[]{:S(2)}) copy-start(f32[4096,128]{1,0:T(8,128)S(1)} %scatter_custom_fusion) | copy-start | bytes 6291460
Sparse Core Ops, SparseCore 0:
  46.0 35.9 all-reduce.1
where the time goes:
time: 102 us; the launch traced here: 101 us
  waiting for transfers between devices  31.7 us (31%)
  other arithmetic  15.4 us (15%)
  local copies, waits for them, and re-layouts  14.2 us (14%)
  between operations  14.1 us (14%)
  blocking collectives  13.3 us (13%)
  matrix products  6.16 us (6%)
  starting transfers between devices  5.21 us (5%)
  loops' own time  1.33 us (1%)
    psum x1, waiting for transfers between devices, per_device(): lax.psum(local_grad.astype(jnp.bfloat16), 'replica').astype(jnp.float32)  31.7 us
    all_gather x1, blocking collectives, per_device(): lax.all_gather(pooled_grad, 'mp', axis=0, tiled=True)  13.3 us
    scatter x1, other arithmetic, per_device(): new_accum = accum.at[touched_rows].set(new_history)  6.41 us
    all_to_all x1, starting transfers between devices, per_device(): lax.all_to_all(partial_value.reshape(mp_count, bag_local, feature_dim), '...  5.17 us
    gather x1, local copies, waits for them, and re-layouts, per_device(): new_rows, new_history = adagrad(row_tile, accum[touched_rows], gradient)  4.4 us
    scatter x1, other arithmetic, per_device(): new_table = table.at[touched_rows].set(new_rows)  4.01 us
    unnamed x16, local copies, waits for them, and re-layouts  3.56 us
    dot_general x1, matrix products, per_device(): jnp.dot(counts, tile_low, preferred_element_type=jnp.float32)  3.1 us
  transfers between devices with their start and end apart: 2, of which 1 were waited for; matrix products, arithmetic and copies ran while one was open for 18% of the time, Pallas kernels for 0%

commit v1 on v0

--- a/solution.py
+++ b/solution.py
@@ -1,11 +1,16 @@
+import functools
 import math
 
 import jax
 import jax.numpy as jnp
 from jax import lax
+from jax.experimental import pallas as pl
+from jax.experimental.pallas import tpu as pltpu
 from jax.sharding import PartitionSpec as P
 
 learn_rate = 0.5
+LANES = 128
+MIB = 1 << 20
 
 
 def build_counts(slots, weights, touch_count):
@@ -30,7 +35,7 @@
     return (row_values - learn_rate * gradient / jnp.sqrt(history_new), history_new)
 
 
-def per_device(table, accum, lookup_slots, lookup_weights, touched_rows, pooled_grad):
+def per_device_general(table, accum, lookup_slots, lookup_weights, touched_rows, pooled_grad):
     touch_count = touched_rows.shape[0]
     feature_dim = table.shape[1]
     bag_local = pooled_grad.shape[0]
@@ -60,6 +65,291 @@
     return (pooled, new_table, new_accum)
 
 
+def vmem():
+    return pl.BlockSpec(memory_space=pltpu.VMEM)
+
+
+def smem():
+    return pl.BlockSpec(memory_space=pltpu.SMEM)
+
+
+def anywhere():
+    return pl.BlockSpec(memory_space=pl.ANY)
+
+
+def params(mib):
+    return pltpu.CompilerParams(vmem_limit_bytes=mib * MIB)
+
+
+def pack_kernel(grad_ref, slots_ref, weights_ref, out_ref, slot_rows, weight_rows):
+    hots, bags = slots_ref.shape
+    rows = grad_ref.shape[0]
+    blocks = bags // LANES
+    out_ref[pl.ds(0, rows), :] = grad_ref[...]
+    for h in range(hots):
+        for j in range(blocks):
+            slot_rows[pl.ds(h * blocks + j, 1), :] = slots_ref[pl.ds(h, 1), pl.ds(j * LANES, LANES)]
+            weight_rows[pl.ds(h * blocks + j, 1), :] = weights_ref[pl.ds(h, 1), pl.ds(j * LANES, LANES)]
+    slot = slot_rows[...]
+    code = weight_rows[...] * 64 + lax.shift_right_logical(slot, 8)
+    low = jnp.bitwise_and(slot, 255)
+    lookups = hots * blocks
+    out_ref[pl.ds(rows, lookups), :] = low.astype(jnp.float32).astype(jnp.bfloat16)
+    out_ref[pl.ds(rows + lookups, lookups), :] = code.astype(jnp.float32).astype(jnp.bfloat16)
+
+
+def fill_counts(packed_ref, rows, hots, blocks, touch, low_rows, code_rows, write):
+    lookups = hots * blocks
+    low_rows[...] = packed_ref[pl.ds(rows, lookups), :].astype(jnp.float32)
+    code_rows[...] = packed_ref[pl.ds(rows + lookups, lookups), :].astype(jnp.float32)
+    step = min(touch, 256)
+    line = lax.broadcasted_iota(jnp.int32, (step, LANES), 0).astype(jnp.float32).astype(jnp.bfloat16)
+    zero = jnp.zeros((step, LANES), jnp.bfloat16)
+
+    def one(j, carry):
+        lows, highs, weights = [], [], []
+        for h in range(hots):
+            low = low_rows[pl.ds(h * blocks + j, 1), :]
+            code = code_rows[pl.ds(h * blocks + j, 1), :].astype(jnp.int32)
+            lows.append(low)
+            highs.append(jnp.bitwise_and(code, 63))
+            weights.append(lax.shift_right_logical(code, 6).astype(jnp.float32).astype(jnp.bfloat16))
+        for k in range(touch // step):
+            total = None
+            for h in range(hots):
+                at = jnp.where(highs[h] == k, lows[h], -1.0).astype(jnp.bfloat16)
+                at = jnp.broadcast_to(at, (step, LANES))
+                term = jnp.where(at == line, jnp.broadcast_to(weights[h], (step, LANES)), zero)
+                total = term if total is None else total + term
+            write(j, k, total)
+        return carry
+
+    lax.fori_loop(0, blocks, one, 0)
+
+
+def pooled_kernel(hots, mp, touched_ref, packed_ref, table_ref, keep_ref, send_ref, counts_ref,
+                  table_vmem, tile, low_rows, code_rows, sum_t, sem):
+    touch = touched_ref.shape[0]
+    bags = counts_ref.shape[1]
+    rows = bags // mp
+    blocks = bags // LANES
+    me = lax.axis_index("mp")
+    copy = pltpu.make_async_copy(table_ref, table_vmem, sem)
+    copy.start()
+
+    def write(j, k, block):
+        counts_ref[pl.ds(k * block.shape[0], block.shape[0]),
+                   pl.ds(pl.multiple_of(j * LANES, LANES), LANES)] = block
+
+    fill_counts(packed_ref, rows, hots, blocks, touch, low_rows, code_rows, write)
+    copy.wait()
+
+    def gather(i, carry):
+        for u in range(16):
+            t = i * 16 + u
+            tile[pl.ds(t, 1), :] = table_vmem[pl.ds(touched_ref[t], 1), :]
+        return carry
+
+    lax.fori_loop(0, touch // 16, gather, 0)
+    tile_t = tile[...].T.astype(jnp.bfloat16)
+    sum_t[...] = jnp.dot(tile_t, counts_ref[...], preferred_element_type=jnp.float32)
+    for c in range(mp // 2):
+        for odd, ref in ((0, keep_ref), (1, send_ref)):
+            owner = jnp.bitwise_xor(me, 2 * c + odd)
+            block = sum_t[:, pl.ds(pl.multiple_of(owner * rows, rows), rows)]
+            ref[c] = block.T
+
+
+def join_kernel(rows, *refs):
+    out_ref = refs[-1]
+    for d, ref in enumerate(refs[:-1]):
+        out_ref[pl.ds(d * rows, rows), :] = ref[pl.ds(0, rows), :]
+
+
+def counts_kernel(hots, rows, *refs):
+    peers, counts_ref, low_rows, code_rows = refs[:-3], refs[-3], refs[-2], refs[-1]
+    touch = counts_ref.shape[0]
+    bags = counts_ref.shape[1] // len(peers)
+    for d, ref in enumerate(peers):
+
+        def write(j, k, block, d=d):
+            counts_ref[pl.ds(k * block.shape[0], block.shape[0]),
+                       pl.ds(pl.multiple_of(d * bags + j * LANES, LANES), LANES)] = block
+
+        fill_counts(ref, rows, hots, bags // LANES, touch, low_rows, code_rows, write)
+
+
+def update_kernel(mp, replicas, rows, touched_ref, own_ref, rest_ref, *refs):
+    blocks = refs[:mp]
+    table_ref, accum_ref, new_table_ref, new_accum_ref = refs[mp:mp + 4]
+    grads, summed, full, table_vmem, accum_vmem, in_sem, out_sem = refs[mp + 4:]
+    touch = touched_ref.shape[0]
+    total_rows = full.shape[0]
+    bags = mp * rows
+    me = lax.axis_index("mp")
+    loads = [
+        pltpu.make_async_copy(table_ref, table_vmem, in_sem.at[0]),
+        pltpu.make_async_copy(accum_ref, accum_vmem, in_sem.at[1]),
+    ]
+    for load in loads:
+        load.start()
+    full[...] = jnp.zeros_like(full)
+    for m, ref in enumerate(blocks):
+        owner = jnp.bitwise_xor(me, m)
+        for d in range(replicas):
+            place = pl.multiple_of(d * bags + owner * rows, rows)
+            grads[pl.ds(place, rows), :] = ref[pl.ds(d * rows, rows), :]
+    gradient = jnp.dot(own_ref[...], grads[pl.ds(0, bags), :], preferred_element_type=jnp.float32)
+    gradient += jnp.dot(
+        rest_ref[...], grads[pl.ds(bags, bags * (replicas - 1)), :], preferred_element_type=jnp.float32
+    )
+    summed[...] = gradient
+
+    def scatter(i, carry):
+        for u in range(16):
+            t = i * 16 + u
+            full[pl.ds(touched_ref[t], 1), :] = summed[pl.ds(t, 1), :]
+        return carry
+
+    lax.fori_loop(0, touch // 16, scatter, 0)
+    for load in loads:
+        load.wait()
+    chunks = 8
+    size = total_rows // chunks
+    stores = []
+    for c in range(chunks):
+        part = pl.ds(c * size, size)
+        change = full[part, :]
+        history = accum_vmem[part, :] + change * change
+        table_vmem[part, :] = table_vmem[part, :] - learn_rate * change * lax.rsqrt(history)
+        accum_vmem[part, :] = history
+        for held, out, s in ((table_vmem, new_table_ref, 0), (accum_vmem, new_accum_ref, 1)):
+            store = pltpu.make_async_copy(held.at[part, :], out.at[part, :], out_sem.at[s, c])
+            store.start()
+            stores.append(store)
+    for store in stores:
+        store.wait()
+
+
+def per_device_small(table, accum, lookup_slots, lookup_weights, touched_rows, pooled_grad):
+    bags, hots = lookup_slots.shape
+    touch = touched_rows.shape[0]
+    rows, feature = pooled_grad.shape
+    table_rows = table.shape[0]
+    mp = lax.axis_size("mp")
+    replicas = lax.axis_size("replica")
+    lookups = hots * (bags // LANES)
+    low = jnp.bfloat16
+
+    def swap(value, axis, distance):
+        return lax.ppermute(value, axis, [(i, i ^ distance) for i in range(lax.axis_size(axis))])
+
+    packed = pl.pallas_call(
+        pack_kernel,
+        out_shape=jax.ShapeDtypeStruct((rows + 2 * lookups, LANES), low),
+        in_specs=[vmem(), vmem(), vmem()],
+        out_specs=vmem(),
+        scratch_shapes=[pltpu.VMEM((lookups, LANES), jnp.int32)] * 2,
+        compiler_params=params(8),
+        name="pack",
+    )(pooled_grad, lookup_slots.T, lookup_weights.T)
+    peers = [swap(packed, "replica", d) for d in range(1, replicas)]
+
+    keep, send, own_counts = pl.pallas_call(
+        functools.partial(pooled_kernel, hots, mp),
+        out_shape=[
+            jax.ShapeDtypeStruct((mp // 2, rows, feature), jnp.float32),
+            jax.ShapeDtypeStruct((mp // 2, rows, feature), jnp.float32),
+            jax.ShapeDtypeStruct((touch, bags), low),
+        ],
+        in_specs=[smem(), vmem(), anywhere()],
+        out_specs=[vmem(), vmem(), vmem()],
+        scratch_shapes=[
+            pltpu.VMEM((table_rows, feature), jnp.float32),
+            pltpu.VMEM((touch, feature), jnp.float32),
+            pltpu.VMEM((lookups, LANES), jnp.float32),
+            pltpu.VMEM((lookups, LANES), jnp.float32),
+            pltpu.VMEM((feature, bags), jnp.float32),
+            pltpu.SemaphoreType.DMA,
+        ],
+        compiler_params=params(20),
+        cost_estimate=pl.CostEstimate(flops=2 * touch * bags * feature, bytes_accessed=8 * MIB, transcendentals=0),
+        name="pool",
+    )(touched_rows, packed, table)
+    halves = keep + swap(send, "mp", 1)
+
+    joined = pl.pallas_call(
+        functools.partial(join_kernel, rows),
+        out_shape=jax.ShapeDtypeStruct((replicas * rows, feature), low),
+        in_specs=[vmem()] * replicas,
+        out_specs=vmem(),
+        compiler_params=params(8),
+        name="join",
+    )(packed, *peers)
+    far = [swap(joined, "mp", 2 * c) for c in range(1, mp // 2)]
+    same = [joined] + far
+    other = [swap(value, "mp", 1) for value in same]
+    blocks = [value for pair in zip(same, other) for value in pair]
+
+    pooled = halves[0]
+    for c in range(1, mp // 2):
+        pooled = pooled + swap(halves[c], "mp", 2 * c)
+
+    rest_counts = pl.pallas_call(
+        functools.partial(counts_kernel, hots, rows),
+        out_shape=jax.ShapeDtypeStruct((touch, bags * (replicas - 1)), low),
+        in_specs=[vmem()] * (replicas - 1),
+        out_specs=vmem(),
+        scratch_shapes=[pltpu.VMEM((lookups, LANES), jnp.float32)] * 2,
+        compiler_params=params(16),
+        cost_estimate=pl.CostEstimate(flops=0, bytes_accessed=12 * MIB, transcendentals=0),
+        name="count",
+    )(*peers)
+
+    new_table, new_accum = pl.pallas_call(
+        functools.partial(update_kernel, mp, replicas, rows),
+        out_shape=[jax.ShapeDtypeStruct(table.shape, jnp.float32)] * 2,
+        in_specs=[smem()] + [vmem()] * (2 + mp) + [anywhere()] * 2,
+        out_specs=[anywhere()] * 2,
+        scratch_shapes=[
+            pltpu.VMEM((bags * replicas, feature), low),
+            pltpu.VMEM((touch, feature), jnp.float32),
+            pltpu.VMEM((table_rows, feature), jnp.float32),
+            pltpu.VMEM((table_rows, feature), jnp.float32),
+            pltpu.VMEM((table_rows, feature), jnp.float32),
+            pltpu.SemaphoreType.DMA((2,)),
+            pltpu.SemaphoreType.DMA((2, 8)),
+        ],
+        compiler_params=params(32),
+        cost_estimate=pl.CostEstimate(
+            flops=2 * touch * bags * replicas * feature, bytes_accessed=16 * MIB, transcendentals=0
+        ),
+        name="update",
+    )(touched_rows, own_counts, rest_counts, *blocks, table, accum)
+    return (pooled, new_table, new_accum)
+
+
+def fits_small(mesh, table, lookup_slots, touched_rows, pooled_grad):
+    mp, replicas = mesh.shape["mp"], mesh.shape["replica"]
+    powers = all(n >= 2 and n & (n - 1) == 0 for n in (mp, replicas))
+    touch = touched_rows.shape[0] // mp
+    bags = lookup_slots.shape[0] // replicas
+    rows = pooled_grad.shape[0] // (mp * replicas)
+    return (
+        powers
+        and mp <= 8
+        and replicas <= 4
+        and lookup_slots.shape[0] * touch <= 4096 * 1024
+        and touch % 256 == 0
+        and touch <= 16384
+        and bags % LANES == 0
+        and rows % LANES == 0
+        and table.shape[1] == LANES
+        and table.shape[0] // mp <= 4096
+        and table.shape[0] // mp % 64 == 0
+    )
+
+
 def solution(mesh):
     placed = (
         P("mp", None),
@@ -69,10 +359,15 @@
         P("mp"),
         P(("replica", "mp"), None),
     )
-    return jax.shard_map(
-        per_device,
-        mesh=mesh,
-        in_specs=placed,
-        out_specs=(P(("replica", "mp"), None), P("mp", None), P("mp", None)),
-        check_vma=False,
-    )
+
+    def step(table, accum, lookup_slots, lookup_weights, touched_rows, pooled_grad):
+        small = fits_small(mesh, table, lookup_slots, touched_rows, pooled_grad)
+        return jax.shard_map(
+            per_device_small if small else per_device_general,
+            mesh=mesh,
+            in_specs=placed,
+            out_specs=(P(("replica", "mp"), None), P("mp", None), P("mp", None)),
+            check_vma=False,
+        )(table, accum, lookup_slots, lookup_weights, touched_rows, pooled_grad)
+
+    return step

time: 102 us -> 39.8 us (0.39)
  waiting for transfers between devices: 31.7 us -> 5.97 us
  other arithmetic: 15.4 us -> 0.69 us
  Pallas kernels: 0 us -> 13.6 us
  between operations: 14.1 us -> 0.76 us
  blocking collectives: 13.3 us -> 0 us
  local copies, waits for them, and re-layouts: 14.2 us -> 4.49 us
  starting transfers between devices: 5.21 us -> 13.9 us
  matrix products: 6.16 us -> 0 us
  loops' own time: 1.33 us -> 0 us
    psum x1 -> x0, waiting for transfers between devices: 31.7 us -> none  [per_device(): lax.psum(local_grad.astype(jnp.bfloat16), 'replica').astype(jnp.float32)]
    ppermute x0 -> x14, starting transfers between devices: none -> 13.9 us  [swap(): lax.ppermute(value, axis, [(i, i ^ distance) for i in range(lax.axis_size...]
    pallas_call x0 -> x5, Pallas kernels: none -> 13.6 us  [the longest x1 6.7 us: per_device_small(): pl.pallas_call(functools.partial(update_kernel, mp, replicas, rows), out_...]
    all_gather x1 -> x0, blocking collectives: 13.3 us -> none  [per_device(): lax.all_gather(pooled_grad, 'mp', axis=0, tiled=True)]
    scatter x2 -> x0, other arithmetic: 10.4 us -> none  [the longest x1 6.41 us: per_device(): new_accum = accum.at[touched_rows].set(new_history)]
    gather x2 -> x0, local copies, waits for them, and re-layouts: 7.21 us -> none  [the longest x1 4.4 us: per_device(): new_rows, new_history = adagrad(row_tile, accum[touched_rows], gradient)]
    dot_general x2 -> x0, matrix products: 6.16 us -> none  [the longest x1 3.1 us: per_device(): jnp.dot(counts, tile_low, preferred_element_type=jnp.float32)]
    ppermute x0 -> x14, waiting for transfers between devices: none -> 5.97 us  [swap(): lax.ppermute(value, axis, [(i, i ^ distance) for i in range(lax.axis_size...]
  transfers between devices with their start and end apart: 2 -> 14, of which waited for: 1 -> 4; matrix products, arithmetic and copies ran while one was open for 18% -> 0% of each run, Pallas kernels for 0% -> 25%
where the time goes in v1:
time: 39.8 us; the launch traced here: 39.4 us
  starting transfers between devices  13.9 us (35%)
  Pallas kernels  13.6 us (34%)
  waiting for transfers between devices  5.97 us (15%)
  local copies, waits for them, and re-layouts  4.49 us (11%)
  between operations  0.76 us (2%)
  other arithmetic  0.69 us (2%)
    ppermute x14, starting transfers between devices, swap(): lax.ppermute(value, axis, [(i, i ^ distance) for i in range(lax.axis_size...  13.9 us
    pallas_call x1, Pallas kernels, per_device_small(): pl.pallas_call(functools.partial(update_kernel, mp, replicas, rows), out_...  6.7 us
    ppermute x14, waiting for transfers between devices, swap(): lax.ppermute(value, axis, [(i, i ^ distance) for i in range(lax.axis_size...  5.97 us
    unnamed x16, local copies, waits for them, and re-layouts  4.47 us
    pallas_call x1, Pallas kernels, per_device_small(): pl.pallas_call(functools.partial(pooled_kernel, hots, mp), out_shape=[jax...  3.64 us
    pallas_call x1, Pallas kernels, per_device_small(): pl.pallas_call(functools.partial(counts_kernel, hots, rows), out_shape=ja...  3.2 us
  transfers between devices with their start and end apart: 14, of which 4 were waited for; matrix products, arithmetic and copies ran while one was open for 0% of the time, Pallas kernels for 25%

profile of v1, /device:TPU:0, one launch (start us, length us, event | category | flops | bytes accessed | tf_op | source)
XLA Modules:
  0.0 39.4 jit_solution(17716624537876785564)
XLA Ops:
  0.6 0.0 copy-start.3
  0.6 0.7 %copy-done.3 = bf16[128,128]{1,0:T(8,128)(2,1)S(1)} copy-done((bf16[128,128]{1,0:T(8,128)(2,1)S(1)}, bf16[128,128]{1,0:T(8,128)(2,1)}, u32[]{:S(2)}) %copy-start.3) | copy-done | bytes 32792
  1.4 0.0 copy-start.6
  1.4 0.7 %copy-done.6 = s32[1024,4]{0,1:T(4,128)S(1)} copy-done((s32[1024,4]{0,1:T(4,128)S(1)}, s32[1024,4]{0,1:T(4,128)}, u32[]{:S(2)}) %copy-start.6) | copy-done | bytes 16408
  2.1 0.0 copy-start.7
  2.1 0.7 %copy-done.7 = s32[1024,4]{0,1:T(4,128)S(1)} copy-done((s32[1024,4]{0,1:T(4,128)S(1)}, s32[1024,4]{0,1:T(4,128)}, u32[]{:S(2)}) %copy-start.7) | copy-done | bytes 16408
  2.9 0.0 copy-start
  2.9 1.6 %copy-done = f32[4096,128]{1,0:T(8,128)S(1)} copy-done((f32[4096,128]{1,0:T(8,128)S(1)}, f32[4096,128]{1,0:T(8,128)}, u32[]{:S(2)}) %copy-start) | copy-done | bytes 2097176
  4.5 0.0 copy-start.4
  4.5 0.7 %copy-done.4 = s32[1024]{0:T(1024)S(1)} copy-done((s32[1024]{0:T(1024)S(1)}, s32[1024]{0:T(1024)}, u32[]{:S(2)}) %copy-start.4) | copy-done | bytes 4120
  5.1 3.6 %pool.1 = (f32[4,128,128]{2,1,0:T(8,128)S(1)}, f32[4,128,128]{2,1,0:T(8,128)S(1)}, bf16[1024,1024]{1,0:T(8,128)(2,1)S(1)}) custom-call(s32[1024]{0:T(1024)S(1)} %copy-done.4, bf16[192,128]{1,0:T(8,128)(2,1)S(1)} %pack.1.packed_ref.refs_0_, f32[4096,128]{1,0:T(8,128)S(1)} %copy-done), custom_call_target="tpu_custom_call" | custom-call | flops 268435456 | bytes 8388608 | tf_op jit(solution)/shard_map/pool/pallas_call | solution.py:258
  8.8 0.5 %collective-permute-start = (f32[4,128,128]{2,1,0:T(8,128)S(1)}, f32[4,128,128]{2,1,0:T(8,128)S(1)}, u32[]{:S(2)}, u32[]{:S(2)}) collective-permute-start(f32[4,128,128]{2,1,0:T(8,128)S(1)} %get-tuple-element.9), channel_id=1, source_target_pairs={{0,4},{4,0},{8,12},{12,8},{16,20},{20,16},{24,28},{28,24},{1,5},{5... | collective-permute-start | bytes 786440 | tf_op jit(solution)/shard_map/ppermute | solution.py:245
  9.3 4.7 %collective-permute-start.6 = (bf16[192,128]{1,0:T(8,128)(2,1)S(1)}, bf16[192,128]{1,0:T(8,128)(2,1)S(1)}, u32[]{:S(2)}, u32[]{:S(2)}) collective-permute-start(bf16[192,128]{1,0:T(8,128)(2,1)S(1)} %pack.1.packed_ref.refs_0_), channel_id=1, source_target_pairs={{0,3},{1,2},{2,1},{3,0},{4,7},{5,6},{6,5},{7,4},{8,11},{9,10},{10,... | collective-permute-start | bytes 147464 | tf_op jit(solution)/shard_map/ppermute | solution.py:245
  14.0 0.0 collective-permute-start.5
  14.0 0.6 %collective-permute-start.4 = (bf16[192,128]{1,0:T(8,128)(2,1)S(1)}, bf16[192,128]{1,0:T(8,128)(2,1)S(1)}, u32[]{:S(2)}, u32[]{:S(2)}) collective-permute-start(bf16[192,128]{1,0:T(8,128)(2,1)S(1)} %pack.1.packed_ref.refs_0_), channel_id=1, source_target_pairs={{0,1},{1,0},{2,3},{3,2},{4,5},{5,4},{6,7},{7,6},{8,9},{9,8},{10,11... | collective-permute-start | bytes 147464 | tf_op jit(solution)/shard_map/ppermute | solution.py:245
  14.6 1.8 %collective-permute-done.6.refs_2_.refs_3_ = bf16[192,128]{1,0:T(8,128)(2,1)S(1)} collective-permute-done((bf16[192,128]{1,0:T(8,128)(2,1)S(1)}, bf16[192,128]{1,0:T(8,128)(2,1)S(1)}, u32[]{:S(2)}, u32[]{:S(2)}) %collective-permute-start.6) | collective-permute-done | bytes 49184 | tf_op jit(solution)/shard_map/ppermute | solution.py:245
  16.4 2.7 %collective-permute-done.5.refs_1_.refs_2_ = bf16[192,128]{1,0:T(8,128)(2,1)S(1)} collective-permute-done((bf16[192,128]{1,0:T(8,128)(2,1)S(1)}, bf16[192,128]{1,0:T(8,128)(2,1)S(1)}, u32[]{:S(2)}, u32[]{:S(2)}) %collective-permute-start.5) | collective-permute-done | bytes 49184 | tf_op jit(solution)/shard_map/ppermute | solution.py:245
  19.1 0.0 collective-permute-done.4.refs_0_.refs_1_
  19.1 0.0 copy-start.5
  19.2 2.5 %collective-permute-start.12 = (bf16[512,128]{1,0:T(8,128)(2,1)S(1)}, bf16[512,128]{1,0:T(8,128)(2,1)S(1)}, u32[]{:S(2)}, u32[]{:S(2)}) collective-permute-start(bf16[512,128]{1,0:T(8,128)(2,1)S(1)} %join.1.refs_0_), channel_id=1, source_target_pairs={{0,24},{4,28},{8,16},{12,20},{16,8},{20,12},{24,0},{28,4},{1,25},{... | collective-permute-start | bytes 393224 | tf_op jit(solution)/shard_map/ppermute | solution.py:245
  21.7 0.5 %collective-permute-start.10 = (bf16[512,128]{1,0:T(8,128)(2,1)S(1)}, bf16[512,128]{1,0:T(8,128)(2,1)S(1)}, u32[]{:S(2)}, u32[]{:S(2)}) collective-permute-start(bf16[512,128]{1,0:T(8,128)(2,1)S(1)} %join.1.refs_0_), channel_id=1, source_target_pairs={{0,16},{4,20},{8,24},{12,28},{16,0},{20,4},{24,8},{28,12},{1,17},{... | collective-permute-start | bytes 393224 | tf_op jit(solution)/shard_map/ppermute | solution.py:245
  22.2 0.5 %collective-permute-start.8 = (bf16[512,128]{1,0:T(8,128)(2,1)S(1)}, bf16[512,128]{1,0:T(8,128)(2,1)S(1)}, u32[]{:S(2)}, u32[]{:S(2)}) collective-permute-start(bf16[512,128]{1,0:T(8,128)(2,1)S(1)} %join.1.refs_0_), channel_id=1, source_target_pairs={{0,8},{4,12},{8,0},{12,4},{16,24},{20,28},{24,16},{28,20},{1,9},{5... | collective-permute-start | bytes 393224 | tf_op jit(solution)/shard_map/ppermute | solution.py:245
  22.7 0.0 collective-permute-start.7
  22.7 0.0 copy-start.1
  22.7 0.0 copy-start.2
  22.7 3.2 %count.1.rest_ref = bf16[1024,3072]{1,0:T(8,128)(2,1)S(1)} custom-call(bf16[192,128]{1,0:T(8,128)(2,1)S(1)} %collective-permute-done.4.refs_0_.refs_1_, bf16[192,128]{1,0:T(8,128)(2,1)S(1)} %collective-permute-done.5.refs_1_.refs_2_, bf16[192,128]{1,0:T(8,128)(2,1)S(1)} %collective-permute-done.6.refs_2_.refs_3_), custom_call_target="tpu_custom_call" | custom-call | bytes 12582912 | tf_op jit(solution)/shard_map/count/pallas_call | solution.py:298
  25.9 0.0 collective-permute-done.12.refs_6_
  25.9 0.6 %collective-permute-start.13 = (bf16[512,128]{1,0:T(8,128)(2,1)S(1)}, bf16[512,128]{1,0:T(8,128)(2,1)S(1)}, u32[]{:S(2)}, u32[]{:S(2)}) collective-permute-start(bf16[512,128]{1,0:T(8,128)(2,1)S(1)} %collective-permute-done.12.refs_6_), channel_id=1, source_target_pairs={{0,4},{4,0},{8,12},{12,8},{16,20},{20,16},{24,28},{28,24},{1,5},{5... | collective-permute-start | bytes 393224 | tf_op jit(solution)/shard_map/ppermute | solution.py:245
  26.5 1.4 %collective-permute-done.10.refs_4_ = bf16[512,128]{1,0:T(8,128)(2,1)S(1)} collective-permute-done((bf16[512,128]{1,0:T(8,128)(2,1)S(1)}, bf16[512,128]{1,0:T(8,128)(2,1)S(1)}, u32[]{:S(2)}, u32[]{:S(2)}) %collective-permute-start.10) | collective-permute-done | bytes 131104 | tf_op jit(solution)/shard_map/ppermute | solution.py:245
  27.9 0.0 collective-permute-start.11
  27.9 0.1 collective-permute-done.8.refs_2_
  28.0 0.4 %collective-permute-start.9 = (bf16[512,128]{1,0:T(8,128)(2,1)S(1)}, bf16[512,128]{1,0:T(8,128)(2,1)S(1)}, u32[]{:S(2)}, u32[]{:S(2)}) collective-permute-start(bf16[512,128]{1,0:T(8,128)(2,1)S(1)} %collective-permute-done.8.refs_2_), channel_id=1, source_target_pairs={{0,4},{4,0},{8,12},{12,8},{16,20},{20,16},{24,28},{28,24},{1,5},{5... | collective-permute-start | bytes 393224 | tf_op jit(solution)/shard_map/ppermute | solution.py:245
  28.4 0.0 collective-permute-done
  28.5 1.6 %collective-permute-start.1 = (f32[128,128]{1,0:T(8,128)S(1)}, f32[128,128]{1,0:T(8,128)S(1)}, u32[]{:S(2)}, u32[]{:S(2)}) collective-permute-start(f32[128,128]{1,0:T(8,128)S(1)} %get-tuple-element.13), channel_id=1, source_target_pairs={{0,8},{4,12},{8,0},{12,4},{16,24},{20,28},{24,16},{28,20},{1,9},{5... | collective-permute-start | bytes 196616 | tf_op jit(solution)/shard_map/ppermute | solution.py:245
  30.0 0.0 collective-permute-done.7.refs_1_
  30.0 1.5 %collective-permute-start.3 = (f32[128,128]{1,0:T(8,128)S(1)}, f32[128,128]{1,0:T(8,128)S(1)}, u32[]{:S(2)}, u32[]{:S(2)}) collective-permute-start(f32[128,128]{1,0:T(8,128)S(1)} %get-tuple-element.14), channel_id=1, source_target_pairs={{0,24},{4,28},{8,16},{12,20},{16,8},{20,12},{24,0},{28,4},{1,25},{... | collective-permute-start | bytes 196616 | tf_op jit(solution)/shard_map/ppermute | solution.py:245
  31.5 0.0 collective-permute-done.13.refs_7_
  31.5 0.5 %collective-permute-start.2 = (f32[128,128]{1,0:T(8,128)S(1)}, f32[128,128]{1,0:T(8,128)S(1)}, u32[]{:S(2)}, u32[]{:S(2)}) collective-permute-start(f32[128,128]{1,0:T(8,128)S(1)} %get-tuple-element.15), channel_id=1, source_target_pairs={{0,16},{4,20},{8,24},{12,28},{16,0},{20,4},{24,8},{28,12},{1,17},{... | collective-permute-start | bytes 196616 | tf_op jit(solution)/shard_map/ppermute | solution.py:245
  32.0 0.0 collective-permute-done.11.refs_5_
  32.0 0.0 collective-permute-done.9.refs_3_
  32.0 0.0 copy-done.5
  32.0 0.0 copy-done.1
  32.0 0.0 copy-done.2
  32.0 6.7 %update.1 = (f32[4096,128]{1,0:T(8,128)}, f32[4096,128]{1,0:T(8,128)}) custom-call(s32[1024]{0:T(1024)S(1)} %copy-done.5, bf16[1024,1024]{1,0:T(8,128)(2,1)S(1)} %get-tuple-element.10.own_ref, bf16[1024,3072]{1,0:T(8,128)(2,1)S(1)} %count.1.rest_ref, bf16[512,128]{1,0:T(8,128)(2,1)S(1)} %join.1.refs_0_, bf16[512,128]{1,0:T(8,128)(2,1)S(1)} %collective-permute-done.7.refs_1_, ...), custom_call_target="tpu_custom_call" | custom-call | flops 1073741824 | bytes 16777216 | tf_op jit(solution)/shard_map/update/pallas_call | solution.py:309
  38.8 0.0 collective-permute-done.1
  38.8 0.0 collective-permute-done.3
  38.8 0.0 collective-permute-done.2
  38.8 0.6 %fusion.2 = f32[128,128]{1,0:T(8,128)} fusion(f32[128,128]{1,0:T(8,128)S(1)} %collective-permute-done.3, f32[128,128]{1,0:T(8,128)S(1)} %collective-permute-done.2, f32[128,128]{1,0:T(8,128)S(1)} %collective-permute-done.1, f32[4,128,128]{2,1,0:T(8,128)S(1)} %add.12), kind=kLoop, calls=%fused_computation.6 | loop fusion | flops 49152 | bytes 327680 | tf_op jit(solution)/shard_map/add | solution.py:296
  (4 shorter events, 0.1 us)
Async XLA Ops:
  0.6 0.8 %copy-start.3 = (bf16[128,128]{1,0:T(8,128)(2,1)S(1)}, bf16[128,128]{1,0:T(8,128)(2,1)}, u32[]{:S(2)}) copy-start(bf16[128,128]{1,0:T(8,128)(2,1)} %grad_ref.1) | copy-start | bytes 98308
  1.4 0.7 %copy-start.6 = (s32[1024,4]{0,1:T(4,128)S(1)}, s32[1024,4]{0,1:T(4,128)}, u32[]{:S(2)}) copy-start(s32[1024,4]{0,1:T(4,128)} %param.8) | copy-start | bytes 49156
  2.1 0.7 %copy-start.7 = (s32[1024,4]{0,1:T(4,128)S(1)}, s32[1024,4]{0,1:T(4,128)}, u32[]{:S(2)}) copy-start(s32[1024,4]{0,1:T(4,128)} %param.9) | copy-start | bytes 49156
  2.9 1.6 %copy-start = (f32[4096,128]{1,0:T(8,128)S(1)}, f32[4096,128]{1,0:T(8,128)}, u32[]{:S(2)}) copy-start(f32[4096,128]{1,0:T(8,128)} %refs_8_.1) | copy-start | bytes 6291460
  4.5 0.7 %copy-start.4 = (s32[1024]{0:T(1024)S(1)}, s32[1024]{0:T(1024)}, u32[]{:S(2)}) copy-start(s32[1024]{0:T(1024)} %touched_ref.3) | copy-start | bytes 12292
  8.8 19.6 %collective-permute-start = (f32[4,128,128]{2,1,0:T(8,128)S(1)}, f32[4,128,128]{2,1,0:T(8,128)S(1)}, u32[]{:S(2)}, u32[]{:S(2)}) collective-permute-start(f32[4,128,128]{2,1,0:T(8,128)S(1)} %get-tuple-element.9), channel_id=1, source_target_pairs={{0,4},{4,0},{8,12},{12,8},{16,20},{20,16},{24,28},{28,24},{1,5},{5... | collective-permute-start | bytes 786440 | tf_op jit(solution)/shard_map/ppermute | solution.py:245
  9.3 7.1 %collective-permute-start.6 = (bf16[192,128]{1,0:T(8,128)(2,1)S(1)}, bf16[192,128]{1,0:T(8,128)(2,1)S(1)}, u32[]{:S(2)}, u32[]{:S(2)}) collective-permute-start(bf16[192,128]{1,0:T(8,128)(2,1)S(1)} %pack.1.packed_ref.refs_0_), channel_id=1, source_target_pairs={{0,3},{1,2},{2,1},{3,0},{4,7},{5,6},{6,5},{7,4},{8,11},{9,10},{10,... | collective-permute-start | bytes 147464 | tf_op jit(solution)/shard_map/ppermute | solution.py:245
  14.0 5.1 %collective-permute-start.5 = (bf16[192,128]{1,0:T(8,128)(2,1)S(1)}, bf16[192,128]{1,0:T(8,128)(2,1)S(1)}, u32[]{:S(2)}, u32[]{:S(2)}) collective-permute-start(bf16[192,128]{1,0:T(8,128)(2,1)S(1)} %pack.1.packed_ref.refs_0_), channel_id=1, source_target_pairs={{0,2},{1,3},{2,0},{3,1},{4,6},{5,7},{6,4},{7,5},{8,10},{9,11},{10,... | collective-permute-start | bytes 147464 | tf_op jit(solution)/shard_map/ppermute | solution.py:245
  14.0 5.1 %collective-permute-start.4 = (bf16[192,128]{1,0:T(8,128)(2,1)S(1)}, bf16[192,128]{1,0:T(8,128)(2,1)S(1)}, u32[]{:S(2)}, u32[]{:S(2)}) collective-permute-start(bf16[192,128]{1,0:T(8,128)(2,1)S(1)} %pack.1.packed_ref.refs_0_), channel_id=1, source_target_pairs={{0,1},{1,0},{2,3},{3,2},{4,5},{5,4},{6,7},{7,6},{8,9},{9,8},{10,11... | collective-permute-start | bytes 147464 | tf_op jit(solution)/shard_map/ppermute | solution.py:245
  19.1 12.9 %copy-start.5 = (s32[1024]{0:T(1024)S(1)}, s32[1024]{0:T(1024)}, u32[]{:S(2)}) copy-start(s32[1024]{0:T(1024)} %touched_ref.3) | copy-start | bytes 12292
  19.2 6.8 %collective-permute-start.12 = (bf16[512,128]{1,0:T(8,128)(2,1)S(1)}, bf16[512,128]{1,0:T(8,128)(2,1)S(1)}, u32[]{:S(2)}, u32[]{:S(2)}) collective-permute-start(bf16[512,128]{1,0:T(8,128)(2,1)S(1)} %join.1.refs_0_), channel_id=1, source_target_pairs={{0,24},{4,28},{8,16},{12,20},{16,8},{20,12},{24,0},{28,4},{1,25},{... | collective-permute-start | bytes 393224 | tf_op jit(solution)/shard_map/ppermute | solution.py:245
  21.7 6.2 %collective-permute-start.10 = (bf16[512,128]{1,0:T(8,128)(2,1)S(1)}, bf16[512,128]{1,0:T(8,128)(2,1)S(1)}, u32[]{:S(2)}, u32[]{:S(2)}) collective-permute-start(bf16[512,128]{1,0:T(8,128)(2,1)S(1)} %join.1.refs_0_), channel_id=1, source_target_pairs={{0,16},{4,20},{8,24},{12,28},{16,0},{20,4},{24,8},{28,12},{1,17},{... | collective-permute-start | bytes 393224 | tf_op jit(solution)/shard_map/ppermute | solution.py:245
  22.2 5.8 %collective-permute-start.8 = (bf16[512,128]{1,0:T(8,128)(2,1)S(1)}, bf16[512,128]{1,0:T(8,128)(2,1)S(1)}, u32[]{:S(2)}, u32[]{:S(2)}) collective-permute-start(bf16[512,128]{1,0:T(8,128)(2,1)S(1)} %join.1.refs_0_), channel_id=1, source_target_pairs={{0,8},{4,12},{8,0},{12,4},{16,24},{20,28},{24,16},{28,20},{1,9},{5... | collective-permute-start | bytes 393224 | tf_op jit(solution)/shard_map/ppermute | solution.py:245
  22.7 7.3 %collective-permute-start.7 = (bf16[512,128]{1,0:T(8,128)(2,1)S(1)}, bf16[512,128]{1,0:T(8,128)(2,1)S(1)}, u32[]{:S(2)}, u32[]{:S(2)}) collective-permute-start(bf16[512,128]{1,0:T(8,128)(2,1)S(1)} %join.1.refs_0_), channel_id=1, source_target_pairs={{0,4},{4,0},{8,12},{12,8},{16,20},{20,16},{24,28},{28,24},{1,5},{5... | collective-permute-start | bytes 393224 | tf_op jit(solution)/shard_map/ppermute | solution.py:245
  22.7 9.3 %copy-start.1 = (f32[4096,128]{1,0:T(8,128)S(1)}, f32[4096,128]{1,0:T(8,128)}, u32[]{:S(2)}) copy-start(f32[4096,128]{1,0:T(8,128)} %refs_8_.1) | copy-start | bytes 6291460
  22.7 9.3 %copy-start.2 = (f32[4096,128]{1,0:T(8,128)S(1)}, f32[4096,128]{1,0:T(8,128)}, u32[]{:S(2)}) copy-start(f32[4096,128]{1,0:T(8,128)} %refs_9_.1) | copy-start | bytes 6291460
  25.9 5.6 %collective-permute-start.13 = (bf16[512,128]{1,0:T(8,128)(2,1)S(1)}, bf16[512,128]{1,0:T(8,128)(2,1)S(1)}, u32[]{:S(2)}, u32[]{:S(2)}) collective-permute-start(bf16[512,128]{1,0:T(8,128)(2,1)S(1)} %collective-permute-done.12.refs_6_), channel_id=1, source_target_pairs={{0,4},{4,0},{8,12},{12,8},{16,20},{20,16},{24,28},{28,24},{1,5},{5... | collective-permute-start | bytes 393224 | tf_op jit(solution)/shard_map/ppermute | solution.py:245
  27.9 4.1 %collective-permute-start.11 = (bf16[512,128]{1,0:T(8,128)(2,1)S(1)}, bf16[512,128]{1,0:T(8,128)(2,1)S(1)}, u32[]{:S(2)}, u32[]{:S(2)}) collective-permute-start(bf16[512,128]{1,0:T(8,128)(2,1)S(1)} %collective-permute-done.10.refs_4_), channel_id=1, source_target_pairs={{0,4},{4,0},{8,12},{12,8},{16,20},{20,16},{24,28},{28,24},{1,5},{5... | collective-permute-start | bytes 393224 | tf_op jit(solution)/shard_map/ppermute | solution.py:245
  28.0 4.1 %collective-permute-start.9 = (bf16[512,128]{1,0:T(8,128)(2,1)S(1)}, bf16[512,128]{1,0:T(8,128)(2,1)S(1)}, u32[]{:S(2)}, u32[]{:S(2)}) collective-permute-start(bf16[512,128]{1,0:T(8,128)(2,1)S(1)} %collective-permute-done.8.refs_2_), channel_id=1, source_target_pairs={{0,4},{4,0},{8,12},{12,8},{16,20},{20,16},{24,28},{28,24},{1,5},{5... | collective-permute-start | bytes 393224 | tf_op jit(solution)/shard_map/ppermute | solution.py:245
  28.5 10.3 %collective-permute-start.1 = (f32[128,128]{1,0:T(8,128)S(1)}, f32[128,128]{1,0:T(8,128)S(1)}, u32[]{:S(2)}, u32[]{:S(2)}) collective-permute-start(f32[128,128]{1,0:T(8,128)S(1)} %get-tuple-element.13), channel_id=1, source_target_pairs={{0,8},{4,12},{8,0},{12,4},{16,24},{20,28},{24,16},{28,20},{1,9},{5... | collective-permute-start | bytes 196616 | tf_op jit(solution)/shard_map/ppermute | solution.py:245
  30.0 8.8 %collective-permute-start.3 = (f32[128,128]{1,0:T(8,128)S(1)}, f32[128,128]{1,0:T(8,128)S(1)}, u32[]{:S(2)}, u32[]{:S(2)}) collective-permute-start(f32[128,128]{1,0:T(8,128)S(1)} %get-tuple-element.14), channel_id=1, source_target_pairs={{0,24},{4,28},{8,16},{12,20},{16,8},{20,12},{24,0},{28,4},{1,25},{... | collective-permute-start | bytes 196616 | tf_op jit(solution)/shard_map/ppermute | solution.py:245
  31.5 7.3 %collective-permute-start.2 = (f32[128,128]{1,0:T(8,128)S(1)}, f32[128,128]{1,0:T(8,128)S(1)}, u32[]{:S(2)}, u32[]{:S(2)}) collective-permute-start(f32[128,128]{1,0:T(8,128)S(1)} %get-tuple-element.15), channel_id=1, source_target_pairs={{0,16},{4,20},{8,24},{12,28},{16,0},{20,4},{24,8},{28,12},{1,17},{... | collective-permute-start | bytes 196616 | tf_op jit(solution)/shard_map/ppermute | solution.py:245

commit v2 on v1

--- a/solution.py
+++ b/solution.py
@@ -73,19 +73,31 @@
     return pl.BlockSpec(memory_space=pltpu.SMEM)
 
 
-def anywhere():
-    return pl.BlockSpec(memory_space=pl.ANY)
+def hbm():
+    return pl.BlockSpec(memory_space=pltpu.HBM)
+
+
+def in_hbm(value):
+    return pltpu.with_memory_space_constraint(value, pltpu.HBM)
 
 
 def params(mib):
     return pltpu.CompilerParams(vmem_limit_bytes=mib * MIB)
 
 
-def pack_kernel(grad_ref, slots_ref, weights_ref, out_ref, slot_rows, weight_rows):
+def pack_kernel(grad_hbm, slots_hbm, weights_hbm, out_ref, slots_ref, weights_ref, slot_rows, weight_rows, sem):
     hots, bags = slots_ref.shape
-    rows = grad_ref.shape[0]
+    rows = grad_hbm.shape[0]
     blocks = bags // LANES
-    out_ref[pl.ds(0, rows), :] = grad_ref[...]
+    loads = [
+        pltpu.make_async_copy(slots_hbm, slots_ref, sem.at[0]),
+        pltpu.make_async_copy(weights_hbm, weights_ref, sem.at[1]),
+        pltpu.make_async_copy(grad_hbm, out_ref.at[pl.ds(0, rows), :], sem.at[2]),
+    ]
+    for load in loads:
+        load.start()
+    for load in loads:
+        load.wait()
     for h in range(hots):
         for j in range(blocks):
             slot_rows[pl.ds(h * blocks + j, 1), :] = slots_ref[pl.ds(h, 1), pl.ds(j * LANES, LANES)]
@@ -127,22 +139,29 @@
     lax.fori_loop(0, blocks, one, 0)
 
 
-def pooled_kernel(hots, mp, touched_ref, packed_ref, table_ref, keep_ref, send_ref, counts_ref,
-                  table_vmem, tile, low_rows, code_rows, sum_t, sem):
+def pooled_kernel(hots, mp, touched_hbm, packed_ref, peer_ref, table_hbm, keep_ref, send_ref, counts_ref,
+                  table_vmem, tile, low_rows, code_rows, sum_t, touched_ref, sem):
     touch = touched_ref.shape[0]
-    bags = counts_ref.shape[1]
+    bags = counts_ref.shape[1] // 2
     rows = bags // mp
     blocks = bags // LANES
     me = lax.axis_index("mp")
-    copy = pltpu.make_async_copy(table_ref, table_vmem, sem)
-    copy.start()
-
-    def write(j, k, block):
-        counts_ref[pl.ds(k * block.shape[0], block.shape[0]),
-                   pl.ds(pl.multiple_of(j * LANES, LANES), LANES)] = block
-
-    fill_counts(packed_ref, rows, hots, blocks, touch, low_rows, code_rows, write)
-    copy.wait()
+    loads = [
+        pltpu.make_async_copy(touched_hbm, touched_ref, sem.at[0]),
+        pltpu.make_async_copy(table_hbm, table_vmem, sem.at[1]),
+    ]
+    for load in loads:
+        load.start()
+
+    for d, ref in enumerate((packed_ref, peer_ref)):
+
+        def write(j, k, block, d=d):
+            counts_ref[pl.ds(k * block.shape[0], block.shape[0]),
+                       pl.ds(pl.multiple_of(d * bags + j * LANES, LANES), LANES)] = block
+
+        fill_counts(ref, rows, hots, blocks, touch, low_rows, code_rows, write)
+    for load in loads:
+        load.wait()
 
     def gather(i, carry):
         for u in range(16):
@@ -152,7 +171,7 @@
 
     lax.fori_loop(0, touch // 16, gather, 0)
     tile_t = tile[...].T.astype(jnp.bfloat16)
-    sum_t[...] = jnp.dot(tile_t, counts_ref[...], preferred_element_type=jnp.float32)
+    sum_t[...] = jnp.dot(tile_t, counts_ref[:, pl.ds(0, bags)], preferred_element_type=jnp.float32)
     for c in range(mp // 2):
         for odd, ref in ((0, keep_ref), (1, send_ref)):
             owner = jnp.bitwise_xor(me, 2 * c + odd)
@@ -179,31 +198,33 @@
         fill_counts(ref, rows, hots, bags // LANES, touch, low_rows, code_rows, write)
 
 
-def update_kernel(mp, replicas, rows, touched_ref, own_ref, rest_ref, *refs):
-    blocks = refs[:mp]
-    table_ref, accum_ref, new_table_ref, new_accum_ref = refs[mp:mp + 4]
-    grads, summed, full, table_vmem, accum_vmem, in_sem, out_sem = refs[mp + 4:]
-    touch = touched_ref.shape[0]
-    total_rows = full.shape[0]
+def halves_kernel(keep_ref, got_ref, *outs):
+    for c, out_ref in enumerate(outs):
+        out_ref[...] = keep_ref[c] + got_ref[c]
+
+
+def grad_kernel(mp, replicas, rows, near_ref, rest_ref, *refs):
+    blocks, sum_ref = refs[:mp], refs[mp]
+    grads = refs[mp + 1]
     bags = mp * rows
     me = lax.axis_index("mp")
-    loads = [
-        pltpu.make_async_copy(table_ref, table_vmem, in_sem.at[0]),
-        pltpu.make_async_copy(accum_ref, accum_vmem, in_sem.at[1]),
-    ]
-    for load in loads:
-        load.start()
-    full[...] = jnp.zeros_like(full)
     for m, ref in enumerate(blocks):
         owner = jnp.bitwise_xor(me, m)
         for d in range(replicas):
             place = pl.multiple_of(d * bags + owner * rows, rows)
             grads[pl.ds(place, rows), :] = ref[pl.ds(d * rows, rows), :]
-    gradient = jnp.dot(own_ref[...], grads[pl.ds(0, bags), :], preferred_element_type=jnp.float32)
-    gradient += jnp.dot(
-        rest_ref[...], grads[pl.ds(bags, bags * (replicas - 1)), :], preferred_element_type=jnp.float32
-    )
-    summed[...] = gradient
+    near = near_ref.shape[1]
+    total = jnp.dot(near_ref[...], grads[pl.ds(0, near), :], preferred_element_type=jnp.float32)
+    total += jnp.dot(rest_ref[...], grads[pl.ds(near, rest_ref.shape[1]), :], preferred_element_type=jnp.float32)
+    sum_ref[...] = total
+
+
+def update_kernel(parts, touched_ref, summed, table_ref, accum_ref, *refs):
+    pooled_parts = refs[:parts]
+    new_table_ref, new_accum_ref, pooled_ref, full, table_vmem, accum_vmem, out_sem = refs[parts:]
+    touch = touched_ref.shape[0]
+    total_rows = full.shape[0]
+    full[...] = jnp.zeros_like(full)
 
     def scatter(i, carry):
         for u in range(16):
@@ -212,21 +233,23 @@
         return carry
 
     lax.fori_loop(0, touch // 16, scatter, 0)
-    for load in loads:
-        load.wait()
     chunks = 8
     size = total_rows // chunks
     stores = []
     for c in range(chunks):
         part = pl.ds(c * size, size)
         change = full[part, :]
-        history = accum_vmem[part, :] + change * change
-        table_vmem[part, :] = table_vmem[part, :] - learn_rate * change * lax.rsqrt(history)
+        history = accum_ref[part, :] + change * change
+        table_vmem[part, :] = table_ref[part, :] - learn_rate * change * lax.rsqrt(history)
         accum_vmem[part, :] = history
         for held, out, s in ((table_vmem, new_table_ref, 0), (accum_vmem, new_accum_ref, 1)):
             store = pltpu.make_async_copy(held.at[part, :], out.at[part, :], out_sem.at[s, c])
             store.start()
             stores.append(store)
+    pooled = pooled_parts[0][...]
+    for part in pooled_parts[1:]:
+        pooled = pooled + part[...]
+    pooled_ref[...] = pooled
     for store in stores:
         store.wait()
 
@@ -247,22 +270,24 @@
     packed = pl.pallas_call(
         pack_kernel,
         out_shape=jax.ShapeDtypeStruct((rows + 2 * lookups, LANES), low),
-        in_specs=[vmem(), vmem(), vmem()],
+        in_specs=[hbm()] * 3,
         out_specs=vmem(),
-        scratch_shapes=[pltpu.VMEM((lookups, LANES), jnp.int32)] * 2,
+        scratch_shapes=[pltpu.VMEM((hots, bags), jnp.int32)] * 2
+        + [pltpu.VMEM((lookups, LANES), jnp.int32)] * 2
+        + [pltpu.SemaphoreType.DMA((3,))],
         compiler_params=params(8),
         name="pack",
-    )(pooled_grad, lookup_slots.T, lookup_weights.T)
+    )(in_hbm(pooled_grad), in_hbm(lookup_slots.T), in_hbm(lookup_weights.T))
     peers = [swap(packed, "replica", d) for d in range(1, replicas)]
 
-    keep, send, own_counts = pl.pallas_call(
+    keep, send, near_counts = pl.pallas_call(
         functools.partial(pooled_kernel, hots, mp),
         out_shape=[
             jax.ShapeDtypeStruct((mp // 2, rows, feature), jnp.float32),
             jax.ShapeDtypeStruct((mp // 2, rows, feature), jnp.float32),
-            jax.ShapeDtypeStruct((touch, bags), low),
+            jax.ShapeDtypeStruct((touch, 2 * bags), low),
         ],
-        in_specs=[smem(), vmem(), anywhere()],
+        in_specs=[hbm(), vmem(), vmem(), hbm()],
         out_specs=[vmem(), vmem(), vmem()],
         scratch_shapes=[
             pltpu.VMEM((table_rows, feature), jnp.float32),
@@ -270,13 +295,14 @@
             pltpu.VMEM((lookups, LANES), jnp.float32),
             pltpu.VMEM((lookups, LANES), jnp.float32),
             pltpu.VMEM((feature, bags), jnp.float32),
-            pltpu.SemaphoreType.DMA,
+            pltpu.SMEM((touch,), jnp.int32),
+            pltpu.SemaphoreType.DMA((2,)),
         ],
         compiler_params=params(20),
         cost_estimate=pl.CostEstimate(flops=2 * touch * bags * feature, bytes_accessed=8 * MIB, transcendentals=0),
         name="pool",
-    )(touched_rows, packed, table)
-    halves = keep + swap(send, "mp", 1)
+    )(in_hbm(touched_rows), packed, peers[0], in_hbm(table))
+    got = swap(send, "mp", 1)
 
     joined = pl.pallas_call(
         functools.partial(join_kernel, rows),
@@ -291,54 +317,67 @@
     other = [swap(value, "mp", 1) for value in same]
     blocks = [value for pair in zip(same, other) for value in pair]
 
-    pooled = halves[0]
-    for c in range(1, mp // 2):
-        pooled = pooled + swap(halves[c], "mp", 2 * c)
+    halves = pl.pallas_call(
+        halves_kernel,
+        out_shape=[jax.ShapeDtypeStruct((rows, feature), jnp.float32)] * (mp // 2),
+        in_specs=[vmem()] * 2,
+        out_specs=[vmem()] * (mp // 2),
+        compiler_params=params(8),
+        name="halves",
+    )(keep, got)
+    pooled_parts = [halves[0]] + [swap(halves[c], "mp", 2 * c) for c in range(1, mp // 2)]
 
     rest_counts = pl.pallas_call(
         functools.partial(counts_kernel, hots, rows),
-        out_shape=jax.ShapeDtypeStruct((touch, bags * (replicas - 1)), low),
-        in_specs=[vmem()] * (replicas - 1),
+        out_shape=jax.ShapeDtypeStruct((touch, bags * (replicas - 2)), low),
+        in_specs=[vmem()] * (replicas - 2),
         out_specs=vmem(),
         scratch_shapes=[pltpu.VMEM((lookups, LANES), jnp.float32)] * 2,
         compiler_params=params(16),
-        cost_estimate=pl.CostEstimate(flops=0, bytes_accessed=12 * MIB, transcendentals=0),
+        cost_estimate=pl.CostEstimate(flops=0, bytes_accessed=8 * MIB, transcendentals=0),
         name="count",
-    )(*peers)
-
-    new_table, new_accum = pl.pallas_call(
-        functools.partial(update_kernel, mp, replicas, rows),
-        out_shape=[jax.ShapeDtypeStruct(table.shape, jnp.float32)] * 2,
-        in_specs=[smem()] + [vmem()] * (2 + mp) + [anywhere()] * 2,
-        out_specs=[anywhere()] * 2,
+    )(*peers[1:])
+
+    gradient = pl.pallas_call(
+        functools.partial(grad_kernel, mp, replicas, rows),
+        out_shape=jax.ShapeDtypeStruct((touch, feature), jnp.float32),
+        in_specs=[vmem()] * (2 + mp),
+        out_specs=vmem(),
+        scratch_shapes=[pltpu.VMEM((bags * replicas, feature), low)],
+        compiler_params=params(24),
+        cost_estimate=pl.CostEstimate(flops=0, bytes_accessed=MIB, transcendentals=0),
+        name="gradient",
+    )(near_counts, rest_counts, *blocks)
+
+    new_table, new_accum, pooled = pl.pallas_call(
+        functools.partial(update_kernel, len(pooled_parts)),
+        out_shape=[jax.ShapeDtypeStruct(table.shape, jnp.float32)] * 2
+        + [jax.ShapeDtypeStruct((rows, feature), jnp.float32)],
+        in_specs=[smem()] + [vmem()] * (3 + len(pooled_parts)),
+        out_specs=[hbm()] * 2 + [vmem()],
         scratch_shapes=[
-            pltpu.VMEM((bags * replicas, feature), low),
-            pltpu.VMEM((touch, feature), jnp.float32),
             pltpu.VMEM((table_rows, feature), jnp.float32),
             pltpu.VMEM((table_rows, feature), jnp.float32),
             pltpu.VMEM((table_rows, feature), jnp.float32),
-            pltpu.SemaphoreType.DMA((2,)),
             pltpu.SemaphoreType.DMA((2, 8)),
         ],
-        compiler_params=params(32),
-        cost_estimate=pl.CostEstimate(
-            flops=2 * touch * bags * replicas * feature, bytes_accessed=16 * MIB, transcendentals=0
-        ),
+        compiler_params=params(24),
+        cost_estimate=pl.CostEstimate(flops=0, bytes_accessed=MIB, transcendentals=0),
         name="update",
-    )(touched_rows, own_counts, rest_counts, *blocks, table, accum)
+    )(touched_rows, gradient, table, accum, *pooled_parts)
     return (pooled, new_table, new_accum)
 
 
 def fits_small(mesh, table, lookup_slots, touched_rows, pooled_grad):
     mp, replicas = mesh.shape["mp"], mesh.shape["replica"]
-    powers = all(n >= 2 and n & (n - 1) == 0 for n in (mp, replicas))
+    powers = all(n & (n - 1) == 0 for n in (mp, replicas))
     touch = touched_rows.shape[0] // mp
     bags = lookup_slots.shape[0] // replicas
     rows = pooled_grad.shape[0] // (mp * replicas)
     return (
         powers
-        and mp <= 8
-        and replicas <= 4
+        and 2 <= mp <= 8
+        and replicas == 4
         and lookup_slots.shape[0] * touch <= 4096 * 1024
         and touch % 256 == 0
         and touch <= 16384

time: 39.8 us -> 34.6 us (0.87)
  local copies, waits for them, and re-layouts: 4.49 us -> 0.02 us
  other arithmetic: 0.69 us -> 0 us
  starting transfers between devices: 13.9 us -> 13.3 us
  Pallas kernels: 13.6 us -> 14.1 us
    unnamed x16 -> x6, local copies, waits for them, and re-layouts: 4.47 us -> 0.02 us
    pallas_call x1, Pallas kernels: 3.2 us -> 2.13 us  [per_device_small(): pl.pallas_call(functools.partial(counts_kernel, hots, rows), out_shape=ja...]
    pallas_call x1, Pallas kernels: 0.04 us -> 0.85 us  [per_device_small(): pl.pallas_call(pack_kernel, out_shape=jax.ShapeDtypeStruct((rows + 2 * lo...]
    add x2 -> x0, other arithmetic: 0.69 us -> none  [the longest x1 0.65 us: per_device_small(): pooled = pooled + swap(halves[c], 'mp', 2 * c)]
    ppermute x14, starting transfers between devices: 13.9 us -> 13.3 us  [swap(): lax.ppermute(value, axis, [(i, i ^ distance) for i in range(lax.axis_size...]
    pallas_call x1 -> x3, Pallas kernels: 6.7 us -> 7.1 us  [the longest x1 4.67 us: per_device_small(): pl.pallas_call(functools.partial(update_kernel, len(pooled_parts)), out_s...]
where the time goes in v2:
time: 34.6 us; the launch traced here: 34.4 us
  Pallas kernels  14.1 us (41%)
  starting transfers between devices  13.3 us (38%)
  waiting for transfers between devices  6.22 us (18%)
  between operations  0.78 us (2%)
    ppermute x14, starting transfers between devices, swap(): lax.ppermute(value, axis, [(i, i ^ distance) for i in range(lax.axis_size...  13.3 us
    ppermute x14, waiting for transfers between devices, swap(): lax.ppermute(value, axis, [(i, i ^ distance) for i in range(lax.axis_size...  6.22 us
    pallas_call x1, Pallas kernels, per_device_small(): pl.pallas_call(functools.partial(update_kernel, len(pooled_parts)), out_s...  4.67 us
    pallas_call x1, Pallas kernels, per_device_small(): pl.pallas_call(functools.partial(pooled_kernel, hots, mp), out_shape=[jax...  3.97 us
    pallas_call x1, Pallas kernels, per_device_small(): pl.pallas_call(functools.partial(grad_kernel, mp, replicas, rows), out_sh...  2.4 us
    pallas_call x1, Pallas kernels, per_device_small(): pl.pallas_call(functools.partial(counts_kernel, hots, rows), out_shape=ja...  2.13 us
    pallas_call x1, Pallas kernels, per_device_small(): pl.pallas_call(pack_kernel, out_shape=jax.ShapeDtypeStruct((rows + 2 * lo...  0.85 us
  transfers between devices with their start and end apart: 14, of which 4 were waited for; matrix products, arithmetic and copies ran while one was open for 0% of the time, Pallas kernels for 25%

profile of v2, /device:TPU:0, one launch (start us, length us, event | category | flops | bytes accessed | tf_op | source)
XLA Modules:
  0.0 34.4 jit_solution(5103527543025742756)
XLA Ops:
  0.6 0.9 %pack.1.packed_ref.refs_0_ = bf16[192,128]{1,0:T(8,128)(2,1)S(1)} custom-call(bf16[128,128]{1,0:T(8,128)(2,1)} %grad_hbm.1, s32[4,1024]{1,0:T(4,128)} %bitcast.2, s32[4,1024]{1,0:T(4,128)} %bitcast.3), custom_call_target="tpu_custom_call" | custom-call | tf_op jit(solution)/shard_map/pack/pallas_call | solution.py:270
  1.5 3.1 %collective-permute-start = (bf16[192,128]{1,0:T(8,128)(2,1)S(1)}, bf16[192,128]{1,0:T(8,128)(2,1)S(1)}, u32[]{:S(2)}, u32[]{:S(2)}) collective-permute-start(bf16[192,128]{1,0:T(8,128)(2,1)S(1)} %pack.1.packed_ref.refs_0_), channel_id=1, source_target_pairs={{0,1},{1,0},{2,3},{3,2},{4,5},{5,4},{6,7},{7,6},{8,9},{9,8},{10,11... | collective-permute-start | bytes 147464 | tf_op jit(solution)/shard_map/ppermute | solution.py:268
  4.6 2.5 %collective-permute-start.2 = (bf16[192,128]{1,0:T(8,128)(2,1)S(1)}, bf16[192,128]{1,0:T(8,128)(2,1)S(1)}, u32[]{:S(2)}, u32[]{:S(2)}) collective-permute-start(bf16[192,128]{1,0:T(8,128)(2,1)S(1)} %pack.1.packed_ref.refs_0_), channel_id=1, source_target_pairs={{0,3},{1,2},{2,1},{3,0},{4,7},{5,6},{6,5},{7,4},{8,11},{9,10},{10,... | collective-permute-start | bytes 147464 | tf_op jit(solution)/shard_map/ppermute | solution.py:268
  7.1 0.1 collective-permute-start.1
  7.2 0.0 collective-permute-done.peer_ref.refs_1_
  7.2 4.0 %pool.1 = (f32[4,128,128]{2,1,0:T(8,128)S(1)}, f32[4,128,128]{2,1,0:T(8,128)S(1)}, bf16[1024,2048]{1,0:T(8,128)(2,1)S(1)}) custom-call(s32[1024]{0:T(1024)} %touched_ref.1, bf16[192,128]{1,0:T(8,128)(2,1)S(1)} %pack.1.packed_ref.refs_0_, bf16[192,128]{1,0:T(8,128)(2,1)S(1)} %collective-permute-done.peer_ref.refs_1_, f32[4096,128]{1,0:T(8,128)} %table_ref.1), custom_call_target="tpu_custom_call" | custom-call | flops 268435456 | bytes 8388608 | tf_op jit(solution)/shard_map/pool/pallas_call | solution.py:283
  11.1 0.1 collective-permute-start.10
  11.2 0.0 collective-permute-done.2.refs_1_.refs_3_
  11.2 1.3 %collective-permute-done.1.refs_0_.refs_2_ = bf16[192,128]{1,0:T(8,128)(2,1)S(1)} collective-permute-done((bf16[192,128]{1,0:T(8,128)(2,1)S(1)}, bf16[192,128]{1,0:T(8,128)(2,1)S(1)}, u32[]{:S(2)}, u32[]{:S(2)}) %collective-permute-start.1) | collective-permute-done | bytes 49184 | tf_op jit(solution)/shard_map/ppermute | solution.py:268
  12.6 2.5 %collective-permute-start.8 = (bf16[512,128]{1,0:T(8,128)(2,1)S(1)}, bf16[512,128]{1,0:T(8,128)(2,1)S(1)}, u32[]{:S(2)}, u32[]{:S(2)}) collective-permute-start(bf16[512,128]{1,0:T(8,128)(2,1)S(1)} %join.1.refs_0_), channel_id=1, source_target_pairs={{0,24},{4,28},{8,16},{12,20},{16,8},{20,12},{24,0},{28,4},{1,25},{... | collective-permute-start | bytes 393224 | tf_op jit(solution)/shard_map/ppermute | solution.py:268
  15.1 0.5 %collective-permute-start.6 = (bf16[512,128]{1,0:T(8,128)(2,1)S(1)}, bf16[512,128]{1,0:T(8,128)(2,1)S(1)}, u32[]{:S(2)}, u32[]{:S(2)}) collective-permute-start(bf16[512,128]{1,0:T(8,128)(2,1)S(1)} %join.1.refs_0_), channel_id=1, source_target_pairs={{0,16},{4,20},{8,24},{12,28},{16,0},{20,4},{24,8},{28,12},{1,17},{... | collective-permute-start | bytes 393224 | tf_op jit(solution)/shard_map/ppermute | solution.py:268
  15.6 0.5 %collective-permute-start.4 = (bf16[512,128]{1,0:T(8,128)(2,1)S(1)}, bf16[512,128]{1,0:T(8,128)(2,1)S(1)}, u32[]{:S(2)}, u32[]{:S(2)}) collective-permute-start(bf16[512,128]{1,0:T(8,128)(2,1)S(1)} %join.1.refs_0_), channel_id=1, source_target_pairs={{0,8},{4,12},{8,0},{12,4},{16,24},{20,28},{24,16},{28,20},{1,9},{5... | collective-permute-start | bytes 393224 | tf_op jit(solution)/shard_map/ppermute | solution.py:268
  16.1 0.0 collective-permute-start.3
  16.1 3.2 %collective-permute-done.8.refs_6_ = bf16[512,128]{1,0:T(8,128)(2,1)S(1)} collective-permute-done((bf16[512,128]{1,0:T(8,128)(2,1)S(1)}, bf16[512,128]{1,0:T(8,128)(2,1)S(1)}, u32[]{:S(2)}, u32[]{:S(2)}) %collective-permute-start.8) | collective-permute-done | bytes 131104 | tf_op jit(solution)/shard_map/ppermute | solution.py:268
  19.3 0.0 collective-permute-start.9
  19.3 1.6 %collective-permute-done.6.refs_4_ = bf16[512,128]{1,0:T(8,128)(2,1)S(1)} collective-permute-done((bf16[512,128]{1,0:T(8,128)(2,1)S(1)}, bf16[512,128]{1,0:T(8,128)(2,1)S(1)}, u32[]{:S(2)}, u32[]{:S(2)}) %collective-permute-start.6) | collective-permute-done | bytes 131104 | tf_op jit(solution)/shard_map/ppermute | solution.py:268
  20.9 0.0 collective-permute-start.7
  20.9 0.1 collective-permute-done.4.refs_2_
  21.0 0.4 %collective-permute-start.5 = (bf16[512,128]{1,0:T(8,128)(2,1)S(1)}, bf16[512,128]{1,0:T(8,128)(2,1)S(1)}, u32[]{:S(2)}, u32[]{:S(2)}) collective-permute-start(bf16[512,128]{1,0:T(8,128)(2,1)S(1)} %collective-permute-done.4.refs_2_), channel_id=1, source_target_pairs={{0,4},{4,0},{8,12},{12,8},{16,20},{20,16},{24,28},{28,24},{1,5},{5... | collective-permute-start | bytes 393224 | tf_op jit(solution)/shard_map/ppermute | solution.py:268
  21.4 0.0 collective-permute-done.10.got_ref
  21.5 1.6 %collective-permute-start.11 = (f32[128,128]{1,0:T(8,128)S(1)}, f32[128,128]{1,0:T(8,128)S(1)}, u32[]{:S(2)}, u32[]{:S(2)}) collective-permute-start(f32[128,128]{1,0:T(8,128)S(1)} %get-tuple-element.17), channel_id=1, source_target_pairs={{0,8},{4,12},{8,0},{12,4},{16,24},{20,28},{24,16},{28,20},{1,9},{5... | collective-permute-start | bytes 196616 | tf_op jit(solution)/shard_map/ppermute | solution.py:268
  23.0 0.0 collective-permute-done.3.refs_1_
  23.0 0.8 %collective-permute-start.12 = (f32[128,128]{1,0:T(8,128)S(1)}, f32[128,128]{1,0:T(8,128)S(1)}, u32[]{:S(2)}, u32[]{:S(2)}) collective-permute-start(f32[128,128]{1,0:T(8,128)S(1)} %get-tuple-element.18), channel_id=1, source_target_pairs={{0,16},{4,20},{8,24},{12,28},{16,0},{20,4},{24,8},{28,12},{1,17},{... | collective-permute-start | bytes 196616 | tf_op jit(solution)/shard_map/ppermute | solution.py:268
  23.9 0.0 collective-permute-done.9.refs_7_
  23.9 1.2 %collective-permute-start.13 = (f32[128,128]{1,0:T(8,128)S(1)}, f32[128,128]{1,0:T(8,128)S(1)}, u32[]{:S(2)}, u32[]{:S(2)}) collective-permute-start(f32[128,128]{1,0:T(8,128)S(1)} %get-tuple-element.19), channel_id=1, source_target_pairs={{0,24},{4,28},{8,16},{12,20},{16,8},{20,12},{24,0},{28,4},{1,25},{... | collective-permute-start | bytes 196616 | tf_op jit(solution)/shard_map/ppermute | solution.py:268
  25.0 2.1 %count.1.rest_ref = bf16[1024,2048]{1,0:T(8,128)(2,1)S(1)} custom-call(bf16[192,128]{1,0:T(8,128)(2,1)S(1)} %collective-permute-done.1.refs_0_.refs_2_, bf16[192,128]{1,0:T(8,128)(2,1)S(1)} %collective-permute-done.2.refs_1_.refs_3_), custom_call_target="tpu_custom_call" | custom-call | bytes 8388608 | tf_op jit(solution)/shard_map/count/pallas_call | solution.py:330
  27.2 0.0 collective-permute-done.7.refs_5_
  27.2 0.0 collective-permute-done.5.refs_3_
  27.2 0.0 copy-start
  27.2 0.0 copy-start.1
  27.2 0.0 copy-start.2
  27.2 2.4 %gradient.1.summed = f32[1024,128]{1,0:T(8,128)S(1)} custom-call(bf16[1024,2048]{1,0:T(8,128)(2,1)S(1)} %get-tuple-element.13.near_ref, bf16[1024,2048]{1,0:T(8,128)(2,1)S(1)} %count.1.rest_ref, bf16[512,128]{1,0:T(8,128)(2,1)S(1)} %join.1.refs_0_, bf16[512,128]{1,0:T(8,128)(2,1)S(1)} %collective-permute-done.3.refs_1_, ...), custom_call_target="tpu_custom_call" | custom-call | bytes 1048576 | tf_op jit(solution)/shard_map/gradient/pallas_call | solution.py:341
  29.6 0.0 collective-permute-done.11.refs_1_
  29.6 0.0 collective-permute-done.12.refs_2_
  29.7 0.0 collective-permute-done.13.refs_3_
  29.7 0.0 copy-done
  29.7 0.0 copy-done.1
  29.7 0.0 copy-done.2
  29.7 4.7 %update.1 = (f32[4096,128]{1,0:T(8,128)}, f32[4096,128]{1,0:T(8,128)}, f32[128,128]{1,0:T(8,128)}) custom-call(s32[1024]{0:T(1024)S(1)} %copy-done.2, f32[1024,128]{1,0:T(8,128)S(1)} %gradient.1.summed, f32[4096,128]{1,0:T(8,128)S(1)} %copy-done, f32[4096,128]{1,0:T(8,128)S(1)} %copy-done.1, f32[128,128]{1,0:T(8,128)S(1)} %get-tuple-element.16.refs_0_, ...), custom_call_target="tpu_custom_call" | custom-call | bytes 1048576 | tf_op jit(solution)/shard_map/update/pallas_call | solution.py:352
  (2 shorter events, 0.0 us)
Async XLA Ops:
  1.5 5.7 %collective-permute-start = (bf16[192,128]{1,0:T(8,128)(2,1)S(1)}, bf16[192,128]{1,0:T(8,128)(2,1)S(1)}, u32[]{:S(2)}, u32[]{:S(2)}) collective-permute-start(bf16[192,128]{1,0:T(8,128)(2,1)S(1)} %pack.1.packed_ref.refs_0_), channel_id=1, source_target_pairs={{0,1},{1,0},{2,3},{3,2},{4,5},{5,4},{6,7},{7,6},{8,9},{9,8},{10,11... | collective-permute-start | bytes 147464 | tf_op jit(solution)/shard_map/ppermute | solution.py:268
  4.6 6.7 %collective-permute-start.2 = (bf16[192,128]{1,0:T(8,128)(2,1)S(1)}, bf16[192,128]{1,0:T(8,128)(2,1)S(1)}, u32[]{:S(2)}, u32[]{:S(2)}) collective-permute-start(bf16[192,128]{1,0:T(8,128)(2,1)S(1)} %pack.1.packed_ref.refs_0_), channel_id=1, source_target_pairs={{0,3},{1,2},{2,1},{3,0},{4,7},{5,6},{6,5},{7,4},{8,11},{9,10},{10,... | collective-permute-start | bytes 147464 | tf_op jit(solution)/shard_map/ppermute | solution.py:268
  7.1 5.5 %collective-permute-start.1 = (bf16[192,128]{1,0:T(8,128)(2,1)S(1)}, bf16[192,128]{1,0:T(8,128)(2,1)S(1)}, u32[]{:S(2)}, u32[]{:S(2)}) collective-permute-start(bf16[192,128]{1,0:T(8,128)(2,1)S(1)} %pack.1.packed_ref.refs_0_), channel_id=1, source_target_pairs={{0,2},{1,3},{2,0},{3,1},{4,6},{5,7},{6,4},{7,5},{8,10},{9,11},{10,... | collective-permute-start | bytes 147464 | tf_op jit(solution)/shard_map/ppermute | solution.py:268
  11.1 10.3 %collective-permute-start.10 = (f32[4,128,128]{2,1,0:T(8,128)S(1)}, f32[4,128,128]{2,1,0:T(8,128)S(1)}, u32[]{:S(2)}, u32[]{:S(2)}) collective-permute-start(f32[4,128,128]{2,1,0:T(8,128)S(1)} %get-tuple-element.15), channel_id=1, source_target_pairs={{0,4},{4,0},{8,12},{12,8},{16,20},{20,16},{24,28},{28,24},{1,5},{5... | collective-permute-start | bytes 786440 | tf_op jit(solution)/shard_map/ppermute | solution.py:268
  12.6 6.8 %collective-permute-start.8 = (bf16[512,128]{1,0:T(8,128)(2,1)S(1)}, bf16[512,128]{1,0:T(8,128)(2,1)S(1)}, u32[]{:S(2)}, u32[]{:S(2)}) collective-permute-start(bf16[512,128]{1,0:T(8,128)(2,1)S(1)} %join.1.refs_0_), channel_id=1, source_target_pairs={{0,24},{4,28},{8,16},{12,20},{16,8},{20,12},{24,0},{28,4},{1,25},{... | collective-permute-start | bytes 393224 | tf_op jit(solution)/shard_map/ppermute | solution.py:268
  15.1 5.8 %collective-permute-start.6 = (bf16[512,128]{1,0:T(8,128)(2,1)S(1)}, bf16[512,128]{1,0:T(8,128)(2,1)S(1)}, u32[]{:S(2)}, u32[]{:S(2)}) collective-permute-start(bf16[512,128]{1,0:T(8,128)(2,1)S(1)} %join.1.refs_0_), channel_id=1, source_target_pairs={{0,16},{4,20},{8,24},{12,28},{16,0},{20,4},{24,8},{28,12},{1,17},{... | collective-permute-start | bytes 393224 | tf_op jit(solution)/shard_map/ppermute | solution.py:268
  15.6 5.4 %collective-permute-start.4 = (bf16[512,128]{1,0:T(8,128)(2,1)S(1)}, bf16[512,128]{1,0:T(8,128)(2,1)S(1)}, u32[]{:S(2)}, u32[]{:S(2)}) collective-permute-start(bf16[512,128]{1,0:T(8,128)(2,1)S(1)} %join.1.refs_0_), channel_id=1, source_target_pairs={{0,8},{4,12},{8,0},{12,4},{16,24},{20,28},{24,16},{28,20},{1,9},{5... | collective-permute-start | bytes 393224 | tf_op jit(solution)/shard_map/ppermute | solution.py:268
  16.1 6.9 %collective-permute-start.3 = (bf16[512,128]{1,0:T(8,128)(2,1)S(1)}, bf16[512,128]{1,0:T(8,128)(2,1)S(1)}, u32[]{:S(2)}, u32[]{:S(2)}) collective-permute-start(bf16[512,128]{1,0:T(8,128)(2,1)S(1)} %join.1.refs_0_), channel_id=1, source_target_pairs={{0,4},{4,0},{8,12},{12,8},{16,20},{20,16},{24,28},{28,24},{1,5},{5... | collective-permute-start | bytes 393224 | tf_op jit(solution)/shard_map/ppermute | solution.py:268
  19.3 4.5 %collective-permute-start.9 = (bf16[512,128]{1,0:T(8,128)(2,1)S(1)}, bf16[512,128]{1,0:T(8,128)(2,1)S(1)}, u32[]{:S(2)}, u32[]{:S(2)}) collective-permute-start(bf16[512,128]{1,0:T(8,128)(2,1)S(1)} %collective-permute-done.8.refs_6_), channel_id=1, source_target_pairs={{0,4},{4,0},{8,12},{12,8},{16,20},{20,16},{24,28},{28,24},{1,5},{5... | collective-permute-start | bytes 393224 | tf_op jit(solution)/shard_map/ppermute | solution.py:268
  20.9 6.3 %collective-permute-start.7 = (bf16[512,128]{1,0:T(8,128)(2,1)S(1)}, bf16[512,128]{1,0:T(8,128)(2,1)S(1)}, u32[]{:S(2)}, u32[]{:S(2)}) collective-permute-start(bf16[512,128]{1,0:T(8,128)(2,1)S(1)} %collective-permute-done.6.refs_4_), channel_id=1, source_target_pairs={{0,4},{4,0},{8,12},{12,8},{16,20},{20,16},{24,28},{28,24},{1,5},{5... | collective-permute-start | bytes 393224 | tf_op jit(solution)/shard_map/ppermute | solution.py:268
  21.0 6.2 %collective-permute-start.5 = (bf16[512,128]{1,0:T(8,128)(2,1)S(1)}, bf16[512,128]{1,0:T(8,128)(2,1)S(1)}, u32[]{:S(2)}, u32[]{:S(2)}) collective-permute-start(bf16[512,128]{1,0:T(8,128)(2,1)S(1)} %collective-permute-done.4.refs_2_), channel_id=1, source_target_pairs={{0,4},{4,0},{8,12},{12,8},{16,20},{20,16},{24,28},{28,24},{1,5},{5... | collective-permute-start | bytes 393224 | tf_op jit(solution)/shard_map/ppermute | solution.py:268
  21.5 8.2 %collective-permute-start.11 = (f32[128,128]{1,0:T(8,128)S(1)}, f32[128,128]{1,0:T(8,128)S(1)}, u32[]{:S(2)}, u32[]{:S(2)}) collective-permute-start(f32[128,128]{1,0:T(8,128)S(1)} %get-tuple-element.17), channel_id=1, source_target_pairs={{0,8},{4,12},{8,0},{12,4},{16,24},{20,28},{24,16},{28,20},{1,9},{5... | collective-permute-start | bytes 196616 | tf_op jit(solution)/shard_map/ppermute | solution.py:268
  23.0 6.6 %collective-permute-start.12 = (f32[128,128]{1,0:T(8,128)S(1)}, f32[128,128]{1,0:T(8,128)S(1)}, u32[]{:S(2)}, u32[]{:S(2)}) collective-permute-start(f32[128,128]{1,0:T(8,128)S(1)} %get-tuple-element.18), channel_id=1, source_target_pairs={{0,16},{4,20},{8,24},{12,28},{16,0},{20,4},{24,8},{28,12},{1,17},{... | collective-permute-start | bytes 196616 | tf_op jit(solution)/shard_map/ppermute | solution.py:268
  23.9 5.8 %collective-permute-start.13 = (f32[128,128]{1,0:T(8,128)S(1)}, f32[128,128]{1,0:T(8,128)S(1)}, u32[]{:S(2)}, u32[]{:S(2)}) collective-permute-start(f32[128,128]{1,0:T(8,128)S(1)} %get-tuple-element.19), channel_id=1, source_target_pairs={{0,24},{4,28},{8,16},{12,20},{16,8},{20,12},{24,0},{28,4},{1,25},{... | collective-permute-start | bytes 196616 | tf_op jit(solution)/shard_map/ppermute | solution.py:268
  27.2 2.5 %copy-start = (f32[4096,128]{1,0:T(8,128)S(1)}, f32[4096,128]{1,0:T(8,128)}, u32[]{:S(2)}) copy-start(f32[4096,128]{1,0:T(8,128)} %table_ref.1) | copy-start | bytes 6291460
  27.2 2.5 %copy-start.1 = (f32[4096,128]{1,0:T(8,128)S(1)}, f32[4096,128]{1,0:T(8,128)}, u32[]{:S(2)}) copy-start(f32[4096,128]{1,0:T(8,128)} %accum_ref.1) | copy-start | bytes 6291460
  27.2 2.5 %copy-start.2 = (s32[1024]{0:T(1024)S(1)}, s32[1024]{0:T(1024)}, u32[]{:S(2)}) copy-start(s32[1024]{0:T(1024)} %touched_ref.1) | copy-start | bytes 12292

commit v3 on v2

--- a/solution.py
+++ b/solution.py
@@ -110,8 +110,11 @@
     out_ref[pl.ds(rows + lookups, lookups), :] = code.astype(jnp.float32).astype(jnp.bfloat16)
 
 
-def fill_counts(packed_ref, rows, hots, blocks, touch, low_rows, code_rows, write):
-    lookups = hots * blocks
+def fill_counts(packed_ref, counts_ref, first, me, mp, hots, low_rows, code_rows):
+    touch = counts_ref.shape[0]
+    lookups = low_rows.shape[0]
+    rows = packed_ref.shape[0] - 2 * lookups
+    blocks = lookups // hots
     low_rows[...] = packed_ref[pl.ds(rows, lookups), :].astype(jnp.float32)
     code_rows[...] = packed_ref[pl.ds(rows + lookups, lookups), :].astype(jnp.float32)
     step = min(touch, 256)
@@ -119,6 +122,10 @@
     zero = jnp.zeros((step, LANES), jnp.bfloat16)
 
     def one(j, carry):
+        distance = jnp.bitwise_xor(j * LANES // rows, me)
+        half = jnp.bitwise_and(distance, 1) * (blocks * LANES // 2)
+        at_column = half + lax.shift_right_logical(distance, 1) * rows + j * LANES % rows + first
+        columns = pl.ds(pl.multiple_of(at_column, LANES), LANES)
         lows, highs, weights = [], [], []
         for h in range(hots):
             low = low_rows[pl.ds(h * blocks + j, 1), :]
@@ -133,7 +140,7 @@
                 at = jnp.broadcast_to(at, (step, LANES))
                 term = jnp.where(at == line, jnp.broadcast_to(weights[h], (step, LANES)), zero)
                 total = term if total is None else total + term
-            write(j, k, total)
+            counts_ref[pl.ds(k * step, step), columns] = total
         return carry
 
     lax.fori_loop(0, blocks, one, 0)
@@ -154,12 +161,7 @@
         load.start()
 
     for d, ref in enumerate((packed_ref, peer_ref)):
-
-        def write(j, k, block, d=d):
-            counts_ref[pl.ds(k * block.shape[0], block.shape[0]),
-                       pl.ds(pl.multiple_of(d * bags + j * LANES, LANES), LANES)] = block
-
-        fill_counts(ref, rows, hots, blocks, touch, low_rows, code_rows, write)
+        fill_counts(ref, counts_ref, d * bags, me, mp, hots, low_rows, code_rows)
     for load in loads:
         load.wait()
 
@@ -172,83 +174,126 @@
     lax.fori_loop(0, touch // 16, gather, 0)
     tile_t = tile[...].T.astype(jnp.bfloat16)
     sum_t[...] = jnp.dot(tile_t, counts_ref[:, pl.ds(0, bags)], preferred_element_type=jnp.float32)
-    for c in range(mp // 2):
-        for odd, ref in ((0, keep_ref), (1, send_ref)):
-            owner = jnp.bitwise_xor(me, 2 * c + odd)
-            block = sum_t[:, pl.ds(pl.multiple_of(owner * rows, rows), rows)]
-            ref[c] = block.T
-
-
-def join_kernel(rows, *refs):
-    out_ref = refs[-1]
-    for d, ref in enumerate(refs[:-1]):
-        out_ref[pl.ds(d * rows, rows), :] = ref[pl.ds(0, rows), :]
-
-
-def counts_kernel(hots, rows, *refs):
-    peers, counts_ref, low_rows, code_rows = refs[:-3], refs[-3], refs[-2], refs[-1]
-    touch = counts_ref.shape[0]
+    for half, ref in ((0, keep_ref), (bags // 2, send_ref)):
+        for c in range(mp // 2):
+            ref[c] = sum_t[:, pl.ds(half + c * rows, rows)].T
+
+
+def join_kernel(rows, replicas, keep_ref, send_ref, *refs):
+    packed, outs = refs[:replicas], refs[replicas:]
+    for c, out_ref in enumerate(outs):
+        for d, ref in enumerate(packed):
+            out_ref[pl.ds(d * rows, rows), :] = ref[pl.ds(0, rows), :]
+        out_ref[pl.ds(replicas * rows, rows), :] = keep_ref[c].astype(jnp.bfloat16)
+        out_ref[pl.ds((replicas + 1) * rows, rows), :] = send_ref[c].astype(jnp.bfloat16)
+
+
+def counts_kernel(hots, mp, touched_hbm, touched_rows_ref, accum_hbm, *refs):
+    peers, refs = refs[:-8], refs[-8:]
+    counts_ref, accum_ref, history_ref, spread_ref, low_rows, code_rows, touched_ref, sem = refs
+    loads = [
+        pltpu.make_async_copy(touched_hbm, touched_ref, sem.at[0]),
+        pltpu.make_async_copy(accum_hbm, accum_ref, sem.at[1]),
+    ]
+    for load in loads:
+        load.start()
     bags = counts_ref.shape[1] // len(peers)
+    me = lax.axis_index("mp")
     for d, ref in enumerate(peers):
-
-        def write(j, k, block, d=d):
-            counts_ref[pl.ds(k * block.shape[0], block.shape[0]),
-                       pl.ds(pl.multiple_of(d * bags + j * LANES, LANES), LANES)] = block
-
-        fill_counts(ref, rows, hots, bags // LANES, touch, low_rows, code_rows, write)
-
-
-def halves_kernel(keep_ref, got_ref, *outs):
-    for c, out_ref in enumerate(outs):
-        out_ref[...] = keep_ref[c] + got_ref[c]
-
-
-def grad_kernel(mp, replicas, rows, near_ref, rest_ref, *refs):
-    blocks, sum_ref = refs[:mp], refs[mp]
-    grads = refs[mp + 1]
-    bags = mp * rows
-    me = lax.axis_index("mp")
-    for m, ref in enumerate(blocks):
-        owner = jnp.bitwise_xor(me, m)
-        for d in range(replicas):
-            place = pl.multiple_of(d * bags + owner * rows, rows)
-            grads[pl.ds(place, rows), :] = ref[pl.ds(d * rows, rows), :]
-    near = near_ref.shape[1]
-    total = jnp.dot(near_ref[...], grads[pl.ds(0, near), :], preferred_element_type=jnp.float32)
-    total += jnp.dot(rest_ref[...], grads[pl.ds(near, rest_ref.shape[1]), :], preferred_element_type=jnp.float32)
-    sum_ref[...] = total
-
-
-def update_kernel(parts, touched_ref, summed, table_ref, accum_ref, *refs):
-    pooled_parts = refs[:parts]
-    new_table_ref, new_accum_ref, pooled_ref, full, table_vmem, accum_vmem, out_sem = refs[parts:]
-    touch = touched_ref.shape[0]
-    total_rows = full.shape[0]
-    full[...] = jnp.zeros_like(full)
-
-    def scatter(i, carry):
+        fill_counts(ref, counts_ref, d * bags, me, mp, hots, low_rows, code_rows)
+
+    step = 256
+    line = lax.broadcasted_iota(jnp.int32, (step, LANES), 0).astype(jnp.float32).astype(jnp.bfloat16)
+    one, zero = jnp.ones((step, LANES), jnp.bfloat16), jnp.zeros((step, LANES), jnp.bfloat16)
+
+    def spread(j, carry):
+        row = touched_rows_ref[pl.ds(j, 1), :]
+        high = lax.shift_right_logical(row, 8)
+        low = jnp.bitwise_and(row, 255).astype(jnp.float32)
+        columns = pl.ds(pl.multiple_of(j * LANES, LANES), LANES)
+        for k in range(spread_ref.shape[0] // step):
+            at = jnp.where(high == k, low, -1.0).astype(jnp.bfloat16)
+            spread_ref[pl.ds(k * step, step), columns] = jnp.where(
+                jnp.broadcast_to(at, (step, LANES)) == line, one, zero
+            )
+        return carry
+
+    lax.fori_loop(0, spread_ref.shape[1] // LANES, spread, 0)
+    for load in loads:
+        load.wait()
+
+    def gather(i, carry):
         for u in range(16):
             t = i * 16 + u
-            full[pl.ds(touched_ref[t], 1), :] = summed[pl.ds(t, 1), :]
+            history_ref[pl.ds(t, 1), :] = accum_ref[pl.ds(touched_ref[t], 1), :]
         return carry
 
-    lax.fori_loop(0, touch // 16, scatter, 0)
+    lax.fori_loop(0, history_ref.shape[0] // 16, gather, 0)
+
+
+def hold_kernel(*refs):
+    del refs
+
+
+def hold(values, others):
+    n = len(values)
+    return pl.pallas_call(
+        hold_kernel,
+        out_shape=[jax.ShapeDtypeStruct(v.shape, v.dtype) for v in values],
+        in_specs=[pl.BlockSpec(memory_space=pl.ANY)] * (n + len(others)),
+        out_specs=[pl.BlockSpec(memory_space=pl.ANY)] * n,
+        input_output_aliases={i: i for i in range(n)},
+        compiler_params=params(1),
+        name="hold",
+    )(*values, *others)
+
+
+def parity_sum(odd, rows, replicas, near_ref, rest_ref, blocks, grads):
+    span = len(blocks) * rows
+    for c, ref in enumerate(blocks):
+        for d in range(replicas):
+            grads[pl.ds(d * span + c * rows, rows), :] = ref[pl.ds(d * rows, rows), :]
+    total = None
+    for d in range(replicas):
+        held, place = (near_ref, d) if d < replicas // 2 else (rest_ref, d - replicas // 2)
+        columns = pl.ds((2 * place + odd) * span, span)
+        term = jnp.dot(held[:, columns], grads[pl.ds(d * span, span), :], preferred_element_type=jnp.float32)
+        total = term if total is None else total + term
+    return total
+
+
+def grad_kernel(rows, replicas, near_ref, rest_ref, *refs):
+    blocks, sum_ref, grads = refs[:-2], refs[-2], refs[-1]
+    sum_ref[...] = parity_sum(0, rows, replicas, near_ref, rest_ref, blocks, grads)
+
+
+def update_kernel(parts, rows, replicas, near_ref, rest_ref, first_ref, history_ref, spread_ref, table_ref, accum_ref,
+                  keep_ref, *refs):
+    far, blocks, refs = refs[:parts - 1], refs[parts - 1:2 * parts - 1], refs[2 * parts - 1:]
+    new_table_ref, new_accum_ref, pooled_ref, grads, change, table_vmem, accum_vmem, out_sem = refs
+    width = first_ref.shape[1]
+    gradient = first_ref[...] + parity_sum(1, rows, replicas, near_ref, rest_ref, blocks, grads)
+    square = gradient * gradient
+    step = learn_rate * gradient * lax.rsqrt(history_ref[...] + square)
+    change[:, pl.ds(0, width)] = step.astype(jnp.bfloat16)
+    change[:, pl.ds(width, width)] = square.astype(jnp.bfloat16)
     chunks = 8
-    size = total_rows // chunks
+    size = table_vmem.shape[0] // chunks
     stores = []
     for c in range(chunks):
         part = pl.ds(c * size, size)
-        change = full[part, :]
-        history = accum_ref[part, :] + change * change
-        table_vmem[part, :] = table_ref[part, :] - learn_rate * change * lax.rsqrt(history)
-        accum_vmem[part, :] = history
+        full = jnp.dot(spread_ref[part, :], change[...], preferred_element_type=jnp.float32)
+        table_vmem[part, :] = table_ref[part, :] - full[:, :width]
+        accum_vmem[part, :] = accum_ref[part, :] + full[:, width:]
         for held, out, s in ((table_vmem, new_table_ref, 0), (accum_vmem, new_accum_ref, 1)):
             store = pltpu.make_async_copy(held.at[part, :], out.at[part, :], out_sem.at[s, c])
             store.start()
             stores.append(store)
-    pooled = pooled_parts[0][...]
-    for part in pooled_parts[1:]:
-        pooled = pooled + part[...]
+    pooled = keep_ref[0]
+    for ref in far:
+        pooled = pooled + ref[pl.ds(replicas * rows, rows), :].astype(jnp.float32)
+    for ref in blocks:
+        pooled = pooled + ref[pl.ds((replicas + 1) * rows, rows), :].astype(jnp.float32)
     pooled_ref[...] = pooled
     for store in stores:
         store.wait()
@@ -280,17 +325,17 @@
     )(in_hbm(pooled_grad), in_hbm(lookup_slots.T), in_hbm(lookup_weights.T))
     peers = [swap(packed, "replica", d) for d in range(1, replicas)]
 
-    keep, send, near_counts = pl.pallas_call(
+    keep, send, near_counts, table_held = pl.pallas_call(
         functools.partial(pooled_kernel, hots, mp),
         out_shape=[
             jax.ShapeDtypeStruct((mp // 2, rows, feature), jnp.float32),
             jax.ShapeDtypeStruct((mp // 2, rows, feature), jnp.float32),
             jax.ShapeDtypeStruct((touch, 2 * bags), low),
+            jax.ShapeDtypeStruct((table_rows, feature), jnp.float32),
         ],
         in_specs=[hbm(), vmem(), vmem(), hbm()],
-        out_specs=[vmem(), vmem(), vmem()],
+        out_specs=[vmem()] * 4,
         scratch_shapes=[
-            pltpu.VMEM((table_rows, feature), jnp.float32),
             pltpu.VMEM((touch, feature), jnp.float32),
             pltpu.VMEM((lookups, LANES), jnp.float32),
             pltpu.VMEM((lookups, LANES), jnp.float32),
@@ -302,61 +347,58 @@
         cost_estimate=pl.CostEstimate(flops=2 * touch * bags * feature, bytes_accessed=8 * MIB, transcendentals=0),
         name="pool",
     )(in_hbm(touched_rows), packed, peers[0], in_hbm(table))
-    got = swap(send, "mp", 1)
-
-    joined = pl.pallas_call(
-        functools.partial(join_kernel, rows),
-        out_shape=jax.ShapeDtypeStruct((replicas * rows, feature), low),
-        in_specs=[vmem()] * replicas,
-        out_specs=vmem(),
+
+    parts = mp // 2
+    payloads = pl.pallas_call(
+        functools.partial(join_kernel, rows, replicas),
+        out_shape=[jax.ShapeDtypeStruct(((replicas + 2) * rows, feature), low)] * parts,
+        in_specs=[vmem()] * (2 + replicas),
+        out_specs=[vmem()] * parts,
         compiler_params=params(8),
         name="join",
-    )(packed, *peers)
-    far = [swap(joined, "mp", 2 * c) for c in range(1, mp // 2)]
-    same = [joined] + far
+    )(keep, send, packed, *peers)
+    far = [swap(payloads[c], "mp", 2 * c) for c in range(1, parts)]
+
+    rest_counts, accum_held, history, spread = pl.pallas_call(
+        functools.partial(counts_kernel, hots, mp),
+        out_shape=[
+            jax.ShapeDtypeStruct((touch, bags * (replicas - 2)), low),
+            jax.ShapeDtypeStruct((table_rows, feature), jnp.float32),
+            jax.ShapeDtypeStruct((touch, feature), jnp.float32),
+            jax.ShapeDtypeStruct((table_rows, touch), low),
+        ],
+        in_specs=[hbm(), vmem(), hbm()] + [vmem()] * (replicas - 2),
+        out_specs=[vmem()] * 4,
+        scratch_shapes=[pltpu.VMEM((lookups, LANES), jnp.float32)] * 2
+        + [pltpu.SMEM((touch,), jnp.int32), pltpu.SemaphoreType.DMA((2,))],
+        compiler_params=params(24),
+        cost_estimate=pl.CostEstimate(flops=0, bytes_accessed=1024, transcendentals=0),
+        name="count",
+    )(in_hbm(touched_rows), touched_rows.reshape(touch // LANES, LANES), in_hbm(accum), *peers[1:])
+
+    same = [payloads[0], *hold(far, [rest_counts])]
     other = [swap(value, "mp", 1) for value in same]
-    blocks = [value for pair in zip(same, other) for value in pair]
-
-    halves = pl.pallas_call(
-        halves_kernel,
-        out_shape=[jax.ShapeDtypeStruct((rows, feature), jnp.float32)] * (mp // 2),
-        in_specs=[vmem()] * 2,
-        out_specs=[vmem()] * (mp // 2),
-        compiler_params=params(8),
-        name="halves",
-    )(keep, got)
-    pooled_parts = [halves[0]] + [swap(halves[c], "mp", 2 * c) for c in range(1, mp // 2)]
-
-    rest_counts = pl.pallas_call(
-        functools.partial(counts_kernel, hots, rows),
-        out_shape=jax.ShapeDtypeStruct((touch, bags * (replicas - 2)), low),
-        in_specs=[vmem()] * (replicas - 2),
+
+    first = pl.pallas_call(
+        functools.partial(grad_kernel, rows, replicas),
+        out_shape=jax.ShapeDtypeStruct((touch, feature), jnp.float32),
+        in_specs=[vmem()] * (2 + mp // 2),
         out_specs=vmem(),
-        scratch_shapes=[pltpu.VMEM((lookups, LANES), jnp.float32)] * 2,
+        scratch_shapes=[pltpu.VMEM((bags * replicas // 2, feature), low)],
         compiler_params=params(16),
-        cost_estimate=pl.CostEstimate(flops=0, bytes_accessed=8 * MIB, transcendentals=0),
-        name="count",
-    )(*peers[1:])
-
-    gradient = pl.pallas_call(
-        functools.partial(grad_kernel, mp, replicas, rows),
-        out_shape=jax.ShapeDtypeStruct((touch, feature), jnp.float32),
-        in_specs=[vmem()] * (2 + mp),
-        out_specs=vmem(),
-        scratch_shapes=[pltpu.VMEM((bags * replicas, feature), low)],
-        compiler_params=params(24),
-        cost_estimate=pl.CostEstimate(flops=0, bytes_accessed=MIB, transcendentals=0),
+        cost_estimate=pl.CostEstimate(flops=0, bytes_accessed=1024, transcendentals=0),
         name="gradient",
-    )(near_counts, rest_counts, *blocks)
+    )(near_counts, rest_counts, *same)
 
     new_table, new_accum, pooled = pl.pallas_call(
-        functools.partial(update_kernel, len(pooled_parts)),
+        functools.partial(update_kernel, parts, rows, replicas),
         out_shape=[jax.ShapeDtypeStruct(table.shape, jnp.float32)] * 2
         + [jax.ShapeDtypeStruct((rows, feature), jnp.float32)],
-        in_specs=[smem()] + [vmem()] * (3 + len(pooled_parts)),
+        in_specs=[vmem()] * (7 + 2 * parts),
         out_specs=[hbm()] * 2 + [vmem()],
         scratch_shapes=[
-            pltpu.VMEM((table_rows, feature), jnp.float32),
+            pltpu.VMEM((bags * replicas // 2, feature), low),
+            pltpu.VMEM((touch, 2 * feature), low),
             pltpu.VMEM((table_rows, feature), jnp.float32),
             pltpu.VMEM((table_rows, feature), jnp.float32),
             pltpu.SemaphoreType.DMA((2, 8)),
@@ -364,7 +406,7 @@
         compiler_params=params(24),
         cost_estimate=pl.CostEstimate(flops=0, bytes_accessed=MIB, transcendentals=0),
         name="update",
-    )(touched_rows, gradient, table, accum, *pooled_parts)
+    )(near_counts, rest_counts, first, history, spread, table_held, accum_held, keep, *same[1:], *other)
     return (pooled, new_table, new_accum)
 
 
@@ -385,7 +427,8 @@
         and rows % LANES == 0
         and table.shape[1] == LANES
         and table.shape[0] // mp <= 4096
-        and table.shape[0] // mp % 64 == 0
+        and table.shape[0] // mp % 256 == 0
+        and touch % LANES == 0
     )
 
 

time: 34.6 us -> 31.6 us (0.913)
  Pallas kernels: 14.1 us -> 17.8 us
  starting transfers between devices: 13.3 us -> 9.81 us
  waiting for transfers between devices: 6.22 us -> 3.07 us
    pallas_call x5, Pallas kernels: 9.24 us -> 13.1 us  [the longest x1 6.21 us: per_device_small(): pl.pallas_call(functools.partial(counts_kernel, hots, mp), out_shape=[jax...]
    ppermute x14 -> x10, starting transfers between devices: 13.3 us -> 9.81 us  [swap(): lax.ppermute(value, axis, [(i, i ^ distance) for i in range(lax.axis_size...]
    ppermute x14 -> x10, waiting for transfers between devices: 6.22 us -> 3.07 us  [swap(): lax.ppermute(value, axis, [(i, i ^ distance) for i in range(lax.axis_size...]
  transfers between devices with their start and end apart: 14 -> 10, of which waited for: 4 -> 4; matrix products, arithmetic and copies ran while one was open for 0% -> 0% of each run, Pallas kernels for 25% -> 36%
where the time goes in v3:
time: 31.6 us; the launch traced here: 31.3 us
  Pallas kernels  17.8 us (56%)
  starting transfers between devices  9.81 us (31%)
  waiting for transfers between devices  3.07 us (10%)
  between operations  0.7 us (2%)
    ppermute x10, starting transfers between devices, swap(): lax.ppermute(value, axis, [(i, i ^ distance) for i in range(lax.axis_size...  9.81 us
    pallas_call x1, Pallas kernels, per_device_small(): pl.pallas_call(functools.partial(counts_kernel, hots, mp), out_shape=[jax...  6.21 us
    pallas_call x1, Pallas kernels, per_device_small(): pl.pallas_call(functools.partial(update_kernel, parts, rows, replicas), o...  5.48 us
    pallas_call x1, Pallas kernels, per_device_small(): pl.pallas_call(functools.partial(pooled_kernel, hots, mp), out_shape=[jax...  3.83 us
    ppermute x10, waiting for transfers between devices, swap(): lax.ppermute(value, axis, [(i, i ^ distance) for i in range(lax.axis_size...  3.07 us
    pallas_call x1, Pallas kernels, per_device_small(): pl.pallas_call(functools.partial(grad_kernel, rows, replicas), out_shape=...  1.32 us
    pallas_call x1, Pallas kernels, per_device_small(): pl.pallas_call(pack_kernel, out_shape=jax.ShapeDtypeStruct((rows + 2 * lo...  0.85 us
  transfers between devices with their start and end apart: 10, of which 4 were waited for; matrix products, arithmetic and copies ran while one was open for 0% of the time, Pallas kernels for 36%

profile of v3, /device:TPU:0, one launch (start us, length us, event | category | flops | bytes accessed | tf_op | source)
XLA Modules:
  0.0 31.3 jit_solution(6043032097829301260)
XLA Ops:
  0.6 0.9 %pack.1.packed_ref.refs_0_ = bf16[192,128]{1,0:T(8,128)(2,1)S(1)} custom-call(bf16[128,128]{1,0:T(8,128)(2,1)} %grad_hbm.1, s32[4,1024]{1,0:T(4,128)} %bitcast.4, s32[4,1024]{1,0:T(4,128)} %bitcast.5), custom_call_target="tpu_custom_call" | custom-call | tf_op jit(solution)/shard_map/pack/pallas_call | solution.py:315
  1.5 3.1 %collective-permute-start = (bf16[192,128]{1,0:T(8,128)(2,1)S(1)}, bf16[192,128]{1,0:T(8,128)(2,1)S(1)}, u32[]{:S(2)}, u32[]{:S(2)}) collective-permute-start(bf16[192,128]{1,0:T(8,128)(2,1)S(1)} %pack.1.packed_ref.refs_0_), channel_id=1, source_target_pairs={{0,1},{1,0},{2,3},{3,2},{4,5},{5,4},{6,7},{7,6},{8,9},{9,8},{10,11... | collective-permute-start | bytes 147464 | tf_op jit(solution)/shard_map/ppermute | solution.py:313
  4.6 2.5 %collective-permute-start.2 = (bf16[192,128]{1,0:T(8,128)(2,1)S(1)}, bf16[192,128]{1,0:T(8,128)(2,1)S(1)}, u32[]{:S(2)}, u32[]{:S(2)}) collective-permute-start(bf16[192,128]{1,0:T(8,128)(2,1)S(1)} %pack.1.packed_ref.refs_0_), channel_id=1, source_target_pairs={{0,3},{1,2},{2,1},{3,0},{4,7},{5,6},{6,5},{7,4},{8,11},{9,10},{10,... | collective-permute-start | bytes 147464 | tf_op jit(solution)/shard_map/ppermute | solution.py:313
  7.1 0.1 collective-permute-start.1
  7.2 0.0 collective-permute-done.peer_ref.refs_1_
  7.2 3.8 %pool.1 = (f32[4,128,128]{2,1,0:T(8,128)S(1)}, f32[4,128,128]{2,1,0:T(8,128)S(1)}, bf16[1024,2048]{1,0:T(8,128)(2,1)S(1)}, f32[4096,128]{1,0:T(8,128)S(1)}) custom-call(s32[1024]{0:T(1024)} %touched_hbm.3, bf16[192,128]{1,0:T(8,128)(2,1)S(1)} %pack.1.packed_ref.refs_0_, bf16[192,128]{1,0:T(8,128)(2,1)S(1)} %collective-permute-done.peer_ref.refs_1_, ...), custom_call_target="tpu_custom_call" | custom-call | flops 268435456 | bytes 8388608 | tf_op jit(solution)/shard_map/pool/pallas_call | solution.py:328
  11.0 0.1 collective-permute-done.2.refs_1_.refs_3_
  11.1 1.5 %collective-permute-done.1.refs_0_.refs_2_ = bf16[192,128]{1,0:T(8,128)(2,1)S(1)} collective-permute-done((bf16[192,128]{1,0:T(8,128)(2,1)S(1)}, bf16[192,128]{1,0:T(8,128)(2,1)S(1)}, u32[]{:S(2)}, u32[]{:S(2)}) %collective-permute-start.1) | collective-permute-done | bytes 49184 | tf_op jit(solution)/shard_map/ppermute | solution.py:313
  12.6 0.1 join.1
  12.7 1.6 %collective-permute-start.3 = (bf16[768,128]{1,0:T(8,128)(2,1)S(1)}, bf16[768,128]{1,0:T(8,128)(2,1)S(1)}, u32[]{:S(2)}, u32[]{:S(2)}) collective-permute-start(bf16[768,128]{1,0:T(8,128)(2,1)S(1)} %get-tuple-element.26), channel_id=1, source_target_pairs={{0,8},{4,12},{8,0},{12,4},{16,24},{20,28},{24,16},{28,20},{1,9},{5... | collective-permute-start | bytes 589832 | tf_op jit(solution)/shard_map/ppermute | solution.py:313
  14.2 1.5 %collective-permute-start.4 = (bf16[768,128]{1,0:T(8,128)(2,1)S(1)}, bf16[768,128]{1,0:T(8,128)(2,1)S(1)}, u32[]{:S(2)}, u32[]{:S(2)}) collective-permute-start(bf16[768,128]{1,0:T(8,128)(2,1)S(1)} %get-tuple-element.27), channel_id=1, source_target_pairs={{0,16},{4,20},{8,24},{12,28},{16,0},{20,4},{24,8},{28,12},{1,17},{... | collective-permute-start | bytes 589832 | tf_op jit(solution)/shard_map/ppermute | solution.py:313
  15.7 0.5 %collective-permute-start.5 = (bf16[768,128]{1,0:T(8,128)(2,1)S(1)}, bf16[768,128]{1,0:T(8,128)(2,1)S(1)}, u32[]{:S(2)}, u32[]{:S(2)}) collective-permute-start(bf16[768,128]{1,0:T(8,128)(2,1)S(1)} %get-tuple-element.28), channel_id=1, source_target_pairs={{0,24},{4,28},{8,16},{12,20},{16,8},{20,12},{24,0},{28,4},{1,25},{... | collective-permute-start | bytes 589832 | tf_op jit(solution)/shard_map/ppermute | solution.py:313
  16.2 0.0 collective-permute-start.6
  16.2 6.2 %count.1 = (bf16[1024,2048]{1,0:T(8,128)(2,1)S(1)}, f32[4096,128]{1,0:T(8,128)S(1)}, f32[1024,128]{1,0:T(8,128)S(1)}, bf16[4096,1024]{1,0:T(8,128)(2,1)S(1)}) custom-call(s32[1024]{0:T(1024)} %touched_hbm.3, s32[8,128]{1,0:T(8,128)} %bitcast.3, f32[4096,128]{1,0:T(8,128)} %accum_hbm.1, bf16[192,128]{1,0:T(8,128)(2,1)S(1)} %collective-permute-done.1.refs_0_.refs_2_, ...), custom_call_target="tpu_custom_call" | custom-call | bytes 1024 | tf_op jit(solution)/shard_map/count/pallas_call | solution.py:362
  22.4 0.0 collective-permute-done.3.refs_0_
  22.4 1.4 %collective-permute-done.4.refs_1_ = bf16[768,128]{1,0:T(8,128)(2,1)S(1)} collective-permute-done((bf16[768,128]{1,0:T(8,128)(2,1)S(1)}, bf16[768,128]{1,0:T(8,128)(2,1)S(1)}, u32[]{:S(2)}, u32[]{:S(2)}) %collective-permute-start.4) | collective-permute-done | bytes 196640 | tf_op jit(solution)/shard_map/ppermute | solution.py:313
  23.9 0.0 collective-permute-done.5.refs_2_
  23.9 0.0 collective-permute-start.7
  23.9 0.5 %collective-permute-start.8 = (bf16[768,128]{1,0:T(8,128)(2,1)S(1)}, bf16[768,128]{1,0:T(8,128)(2,1)S(1)}, u32[]{:S(2)}, u32[]{:S(2)}) collective-permute-start(bf16[768,128]{1,0:T(8,128)(2,1)S(1)} %get-tuple-element.30.refs_2_.refs_1_), channel_id=1, source_target_pairs={{0,4},{4,0},{8,12},{12,8},{16,20},{20,16},{24,28},{28,24},{1,5},{5... | collective-permute-start | bytes 589832 | tf_op jit(solution)/shard_map/ppermute | solution.py:313
  24.4 0.1 collective-permute-start.9
  24.4 1.3 %gradient.1.first_ref = f32[1024,128]{1,0:T(8,128)S(1)} custom-call(bf16[1024,2048]{1,0:T(8,128)(2,1)S(1)} %get-tuple-element.21.near_ref, bf16[1024,2048]{1,0:T(8,128)(2,1)S(1)} %get-tuple-element.22.refs_3_.rest_ref, bf16[768,128]{1,0:T(8,128)(2,1)S(1)} %get-tuple-element.25.refs_0_, bf16[768,128]{1,0:T(8,128)(2,1)S(1)} %get-tuple-element.29.refs_1_.refs_0_, ...), custom_call_target="tpu_custom_call" | custom-call | bytes 1024 | tf_op jit(solution)/shard_map/gradient/pallas_call | solution.py:382
  25.8 0.0 collective-permute-done.6.refs_3_
  25.8 0.0 collective-permute-done.7.refs_4_
  25.8 0.0 collective-permute-done.8.refs_5_
  25.8 0.1 collective-permute-done.9.refs_6_
  25.9 5.5 %update.1 = (f32[4096,128]{1,0:T(8,128)}, f32[4096,128]{1,0:T(8,128)}, f32[128,128]{1,0:T(8,128)}) custom-call(bf16[1024,2048]{1,0:T(8,128)(2,1)S(1)} %get-tuple-element.21.near_ref, bf16[1024,2048]{1,0:T(8,128)(2,1)S(1)} %get-tuple-element.22.refs_3_.rest_ref, f32[1024,128]{1,0:T(8,128)S(1)} %gradient.1.first_ref, ...), custom_call_target="tpu_custom_call" | custom-call | bytes 1048576 | tf_op jit(solution)/shard_map/update/pallas_call | solution.py:393
  (1 shorter events, 0.0 us)
Async XLA Ops:
  1.5 5.7 %collective-permute-start = (bf16[192,128]{1,0:T(8,128)(2,1)S(1)}, bf16[192,128]{1,0:T(8,128)(2,1)S(1)}, u32[]{:S(2)}, u32[]{:S(2)}) collective-permute-start(bf16[192,128]{1,0:T(8,128)(2,1)S(1)} %pack.1.packed_ref.refs_0_), channel_id=1, source_target_pairs={{0,1},{1,0},{2,3},{3,2},{4,5},{5,4},{6,7},{7,6},{8,9},{9,8},{10,11... | collective-permute-start | bytes 147464 | tf_op jit(solution)/shard_map/ppermute | solution.py:313
  4.6 6.5 %collective-permute-start.2 = (bf16[192,128]{1,0:T(8,128)(2,1)S(1)}, bf16[192,128]{1,0:T(8,128)(2,1)S(1)}, u32[]{:S(2)}, u32[]{:S(2)}) collective-permute-start(bf16[192,128]{1,0:T(8,128)(2,1)S(1)} %pack.1.packed_ref.refs_0_), channel_id=1, source_target_pairs={{0,3},{1,2},{2,1},{3,0},{4,7},{5,6},{6,5},{7,4},{8,11},{9,10},{10,... | collective-permute-start | bytes 147464 | tf_op jit(solution)/shard_map/ppermute | solution.py:313
  7.1 5.5 %collective-permute-start.1 = (bf16[192,128]{1,0:T(8,128)(2,1)S(1)}, bf16[192,128]{1,0:T(8,128)(2,1)S(1)}, u32[]{:S(2)}, u32[]{:S(2)}) collective-permute-start(bf16[192,128]{1,0:T(8,128)(2,1)S(1)} %pack.1.packed_ref.refs_0_), channel_id=1, source_target_pairs={{0,2},{1,3},{2,0},{3,1},{4,6},{5,7},{6,4},{7,5},{8,10},{9,11},{10,... | collective-permute-start | bytes 147464 | tf_op jit(solution)/shard_map/ppermute | solution.py:313
  12.7 9.8 %collective-permute-start.3 = (bf16[768,128]{1,0:T(8,128)(2,1)S(1)}, bf16[768,128]{1,0:T(8,128)(2,1)S(1)}, u32[]{:S(2)}, u32[]{:S(2)}) collective-permute-start(bf16[768,128]{1,0:T(8,128)(2,1)S(1)} %get-tuple-element.26), channel_id=1, source_target_pairs={{0,8},{4,12},{8,0},{12,4},{16,24},{20,28},{24,16},{28,20},{1,9},{5... | collective-permute-start | bytes 589832 | tf_op jit(solution)/shard_map/ppermute | solution.py:313
  14.2 9.7 %collective-permute-start.4 = (bf16[768,128]{1,0:T(8,128)(2,1)S(1)}, bf16[768,128]{1,0:T(8,128)(2,1)S(1)}, u32[]{:S(2)}, u32[]{:S(2)}) collective-permute-start(bf16[768,128]{1,0:T(8,128)(2,1)S(1)} %get-tuple-element.27), channel_id=1, source_target_pairs={{0,16},{4,20},{8,24},{12,28},{16,0},{20,4},{24,8},{28,12},{1,17},{... | collective-permute-start | bytes 589832 | tf_op jit(solution)/shard_map/ppermute | solution.py:313
  15.7 8.1 %collective-permute-start.5 = (bf16[768,128]{1,0:T(8,128)(2,1)S(1)}, bf16[768,128]{1,0:T(8,128)(2,1)S(1)}, u32[]{:S(2)}, u32[]{:S(2)}) collective-permute-start(bf16[768,128]{1,0:T(8,128)(2,1)S(1)} %get-tuple-element.28), channel_id=1, source_target_pairs={{0,24},{4,28},{8,16},{12,20},{16,8},{20,12},{24,0},{28,4},{1,25},{... | collective-permute-start | bytes 589832 | tf_op jit(solution)/shard_map/ppermute | solution.py:313
  16.2 9.6 %collective-permute-start.6 = (bf16[768,128]{1,0:T(8,128)(2,1)S(1)}, bf16[768,128]{1,0:T(8,128)(2,1)S(1)}, u32[]{:S(2)}, u32[]{:S(2)}) collective-permute-start(bf16[768,128]{1,0:T(8,128)(2,1)S(1)} %get-tuple-element.25.refs_0_), channel_id=1, source_target_pairs={{0,4},{4,0},{8,12},{12,8},{16,20},{20,16},{24,28},{28,24},{1,5},{5... | collective-permute-start | bytes 589832 | tf_op jit(solution)/shard_map/ppermute | solution.py:313
  23.9 1.9 %collective-permute-start.7 = (bf16[768,128]{1,0:T(8,128)(2,1)S(1)}, bf16[768,128]{1,0:T(8,128)(2,1)S(1)}, u32[]{:S(2)}, u32[]{:S(2)}) collective-permute-start(bf16[768,128]{1,0:T(8,128)(2,1)S(1)} %get-tuple-element.29.refs_1_.refs_0_), channel_id=1, source_target_pairs={{0,4},{4,0},{8,12},{12,8},{16,20},{20,16},{24,28},{28,24},{1,5},{5... | collective-permute-start | bytes 589832 | tf_op jit(solution)/shard_map/ppermute | solution.py:313
  23.9 1.9 %collective-permute-start.8 = (bf16[768,128]{1,0:T(8,128)(2,1)S(1)}, bf16[768,128]{1,0:T(8,128)(2,1)S(1)}, u32[]{:S(2)}, u32[]{:S(2)}) collective-permute-start(bf16[768,128]{1,0:T(8,128)(2,1)S(1)} %get-tuple-element.30.refs_2_.refs_1_), channel_id=1, source_target_pairs={{0,4},{4,0},{8,12},{12,8},{16,20},{20,16},{24,28},{28,24},{1,5},{5... | collective-permute-start | bytes 589832 | tf_op jit(solution)/shard_map/ppermute | solution.py:313
  24.4 1.5 %collective-permute-start.9 = (bf16[768,128]{1,0:T(8,128)(2,1)S(1)}, bf16[768,128]{1,0:T(8,128)(2,1)S(1)}, u32[]{:S(2)}, u32[]{:S(2)}) collective-permute-start(bf16[768,128]{1,0:T(8,128)(2,1)S(1)} %get-tuple-element.31.refs_3_.refs_2_), channel_id=1, source_target_pairs={{0,4},{4,0},{8,12},{12,8},{16,20},{20,16},{24,28},{28,24},{1,5},{5... | collective-permute-start | bytes 589832 | tf_op jit(solution)/shard_map/ppermute | solution.py:313

commit v4 on v3

--- a/solution.py
+++ b/solution.py
@@ -110,7 +110,7 @@
     out_ref[pl.ds(rows + lookups, lookups), :] = code.astype(jnp.float32).astype(jnp.bfloat16)
 
 
-def fill_counts(packed_ref, counts_ref, first, me, mp, hots, low_rows, code_rows):
+def fill_counts(packed_ref, counts_ref, place, me, hots, low_rows, code_rows):
     touch = counts_ref.shape[0]
     lookups = low_rows.shape[0]
     rows = packed_ref.shape[0] - 2 * lookups
@@ -123,8 +123,8 @@
 
     def one(j, carry):
         distance = jnp.bitwise_xor(j * LANES // rows, me)
-        half = jnp.bitwise_and(distance, 1) * (blocks * LANES // 2)
-        at_column = half + lax.shift_right_logical(distance, 1) * rows + j * LANES % rows + first
+        half = jnp.bitwise_and(distance, 1) * (counts_ref.shape[1] // 2) + place * (blocks * LANES // 2)
+        at_column = half + lax.shift_right_logical(distance, 1) * rows + j * LANES % rows
         columns = pl.ds(pl.multiple_of(at_column, LANES), LANES)
         lows, highs, weights = [], [], []
         for h in range(hots):
@@ -146,10 +146,10 @@
     lax.fori_loop(0, blocks, one, 0)
 
 
-def pooled_kernel(hots, mp, touched_hbm, packed_ref, peer_ref, table_hbm, keep_ref, send_ref, counts_ref,
+def pooled_kernel(hots, mp, touched_hbm, packed_ref, table_hbm, keep_ref, send_ref, counts_ref,
                   table_vmem, tile, low_rows, code_rows, sum_t, touched_ref, sem):
     touch = touched_ref.shape[0]
-    bags = counts_ref.shape[1] // 2
+    bags = counts_ref.shape[1]
     rows = bags // mp
     blocks = bags // LANES
     me = lax.axis_index("mp")
@@ -160,8 +160,7 @@
     for load in loads:
         load.start()
 
-    for d, ref in enumerate((packed_ref, peer_ref)):
-        fill_counts(ref, counts_ref, d * bags, me, mp, hots, low_rows, code_rows)
+    fill_counts(packed_ref, counts_ref, 0, me, hots, low_rows, code_rows)
     for load in loads:
         load.wait()
 
@@ -173,7 +172,10 @@
 
     lax.fori_loop(0, touch // 16, gather, 0)
     tile_t = tile[...].T.astype(jnp.bfloat16)
-    sum_t[...] = jnp.dot(tile_t, counts_ref[:, pl.ds(0, bags)], preferred_element_type=jnp.float32)
+    for half in (0, 1):
+        sum_t[:, pl.ds(half * (bags // 2), bags // 2)] = jnp.dot(
+            tile_t, counts_ref[:, pl.ds(half * (bags // 2), bags // 2)], preferred_element_type=jnp.float32
+        )
     for half, ref in ((0, keep_ref), (bags // 2, send_ref)):
         for c in range(mp // 2):
             ref[c] = sum_t[:, pl.ds(half + c * rows, rows)].T
@@ -184,11 +186,11 @@
     for c, out_ref in enumerate(outs):
         for d, ref in enumerate(packed):
             out_ref[pl.ds(d * rows, rows), :] = ref[pl.ds(0, rows), :]
-        out_ref[pl.ds(replicas * rows, rows), :] = keep_ref[c].astype(jnp.bfloat16)
-        out_ref[pl.ds((replicas + 1) * rows, rows), :] = send_ref[c].astype(jnp.bfloat16)
-
-
-def counts_kernel(hots, mp, touched_hbm, touched_rows_ref, accum_hbm, *refs):
+        out_ref[pl.ds(replicas * rows, rows), :] = send_ref[c].astype(jnp.bfloat16)
+        out_ref[pl.ds((replicas + 1) * rows, rows), :] = keep_ref[c].astype(jnp.bfloat16)
+
+
+def counts_kernel(hots, touched_hbm, touched_rows_ref, accum_hbm, *refs):
     peers, refs = refs[:-8], refs[-8:]
     counts_ref, accum_ref, history_ref, spread_ref, low_rows, code_rows, touched_ref, sem = refs
     loads = [
@@ -197,10 +199,9 @@
     ]
     for load in loads:
         load.start()
-    bags = counts_ref.shape[1] // len(peers)
     me = lax.axis_index("mp")
     for d, ref in enumerate(peers):
-        fill_counts(ref, counts_ref, d * bags, me, mp, hots, low_rows, code_rows)
+        fill_counts(ref, counts_ref, d, me, hots, low_rows, code_rows)
 
     step = 256
     line = lax.broadcasted_iota(jnp.int32, (step, LANES), 0).astype(jnp.float32).astype(jnp.bfloat16)
@@ -231,70 +232,71 @@
     lax.fori_loop(0, history_ref.shape[0] // 16, gather, 0)
 
 
-def hold_kernel(*refs):
-    del refs
-
-
-def hold(values, others):
-    n = len(values)
-    return pl.pallas_call(
-        hold_kernel,
-        out_shape=[jax.ShapeDtypeStruct(v.shape, v.dtype) for v in values],
-        in_specs=[pl.BlockSpec(memory_space=pl.ANY)] * (n + len(others)),
-        out_specs=[pl.BlockSpec(memory_space=pl.ANY)] * n,
-        input_output_aliases={i: i for i in range(n)},
-        compiler_params=params(1),
-        name="hold",
-    )(*values, *others)
-
-
-def parity_sum(odd, rows, replicas, near_ref, rest_ref, blocks, grads):
-    span = len(blocks) * rows
+def merge_kernel(rows, keep_ref, waited_ref, *refs):
+    del waited_ref
+    blocks, merged_ref, pooled_ref = refs[:-2], refs[-2], refs[-1]
+    span = merged_ref.shape[0] // len(blocks)
+    total = keep_ref[0]
     for c, ref in enumerate(blocks):
+        merged_ref[pl.ds(c * span, span), :] = ref[pl.ds(0, span), :]
+        if c:
+            total = total + ref[pl.ds(span, rows), :].astype(jnp.float32)
+    pooled_ref[...] = total
+
+
+def parity_sum(odd, parts, rows, near_ref, rest_ref, blocks, grads):
+    span = parts * rows
+    replicas = grads.shape[0] // span
+    for c in range(parts):
         for d in range(replicas):
-            grads[pl.ds(d * span + c * rows, rows), :] = ref[pl.ds(d * rows, rows), :]
-    total = None
-    for d in range(replicas):
-        held, place = (near_ref, d) if d < replicas // 2 else (rest_ref, d - replicas // 2)
-        columns = pl.ds((2 * place + odd) * span, span)
-        term = jnp.dot(held[:, columns], grads[pl.ds(d * span, span), :], preferred_element_type=jnp.float32)
-        total = term if total is None else total + term
-    return total
-
-
-def grad_kernel(rows, replicas, near_ref, rest_ref, *refs):
-    blocks, sum_ref, grads = refs[:-2], refs[-2], refs[-1]
-    sum_ref[...] = parity_sum(0, rows, replicas, near_ref, rest_ref, blocks, grads)
-
-
-def update_kernel(parts, rows, replicas, near_ref, rest_ref, first_ref, history_ref, spread_ref, table_ref, accum_ref,
-                  keep_ref, *refs):
-    far, blocks, refs = refs[:parts - 1], refs[parts - 1:2 * parts - 1], refs[2 * parts - 1:]
-    new_table_ref, new_accum_ref, pooled_ref, grads, change, table_vmem, accum_vmem, out_sem = refs
+            grads[pl.ds(d * span + c * rows, rows), :] = blocks[pl.ds((c * (replicas + 1) + d) * rows, rows), :]
+    near = near_ref.shape[1] // 2
+    rest = rest_ref.shape[1] // 2
+    return jnp.dot(
+        near_ref[:, pl.ds(odd * near, near)], grads[pl.ds(0, near), :], preferred_element_type=jnp.float32
+    ) + jnp.dot(
+        rest_ref[:, pl.ds(odd * rest, rest)], grads[pl.ds(near, rest), :], preferred_element_type=jnp.float32
+    )
+
+
+def grad_kernel(parts, rows, near_ref, rest_ref, blocks, sum_ref, grads):
+    sum_ref[...] = parity_sum(0, parts, rows, near_ref, rest_ref, blocks, grads)
+
+
+def update_kernel(parts, rows, near_ref, rest_ref, first_ref, history_ref, spread_ref, table_ref, accum_ref,
+                  sum_ref, blocks, new_table_ref, new_accum_ref, pooled_ref, grads, change, table_vmem, accum_vmem,
+                  pooled_vmem, out_sem):
     width = first_ref.shape[1]
-    gradient = first_ref[...] + parity_sum(1, rows, replicas, near_ref, rest_ref, blocks, grads)
+    chunks = 8
+    pooled = sum_ref[...]
+    span = blocks.shape[0] // parts
+    for c in range(parts):
+        pooled = pooled + blocks[pl.ds((c + 1) * span - rows, rows), :].astype(jnp.float32)
+    pooled_vmem[...] = pooled
+    stores = [pltpu.make_async_copy(pooled_vmem, pooled_ref, out_sem.at[2, 0])]
+    stores[0].start()
+    gradient = first_ref[...] + parity_sum(1, parts, rows, near_ref, rest_ref, blocks, grads)
     square = gradient * gradient
     step = learn_rate * gradient * lax.rsqrt(history_ref[...] + square)
     change[:, pl.ds(0, width)] = step.astype(jnp.bfloat16)
     change[:, pl.ds(width, width)] = square.astype(jnp.bfloat16)
-    chunks = 8
     size = table_vmem.shape[0] // chunks
-    stores = []
+
+    def spread(c):
+        return jnp.dot(spread_ref[pl.ds(c * size, size), :], change[...], preferred_element_type=jnp.float32)
+
+    ahead = spread(0)
     for c in range(chunks):
         part = pl.ds(c * size, size)
-        full = jnp.dot(spread_ref[part, :], change[...], preferred_element_type=jnp.float32)
+        full = ahead
+        if c + 1 < chunks:
+            ahead = spread(c + 1)
         table_vmem[part, :] = table_ref[part, :] - full[:, :width]
         accum_vmem[part, :] = accum_ref[part, :] + full[:, width:]
         for held, out, s in ((table_vmem, new_table_ref, 0), (accum_vmem, new_accum_ref, 1)):
             store = pltpu.make_async_copy(held.at[part, :], out.at[part, :], out_sem.at[s, c])
             store.start()
             stores.append(store)
-    pooled = keep_ref[0]
-    for ref in far:
-        pooled = pooled + ref[pl.ds(replicas * rows, rows), :].astype(jnp.float32)
-    for ref in blocks:
-        pooled = pooled + ref[pl.ds((replicas + 1) * rows, rows), :].astype(jnp.float32)
-    pooled_ref[...] = pooled
     for store in stores:
         store.wait()
 
@@ -330,10 +332,10 @@
         out_shape=[
             jax.ShapeDtypeStruct((mp // 2, rows, feature), jnp.float32),
             jax.ShapeDtypeStruct((mp // 2, rows, feature), jnp.float32),
-            jax.ShapeDtypeStruct((touch, 2 * bags), low),
+            jax.ShapeDtypeStruct((touch, bags), low),
             jax.ShapeDtypeStruct((table_rows, feature), jnp.float32),
         ],
-        in_specs=[hbm(), vmem(), vmem(), hbm()],
+        in_specs=[hbm(), vmem(), hbm()],
         out_specs=[vmem()] * 4,
         scratch_shapes=[
             pltpu.VMEM((touch, feature), jnp.float32),
@@ -346,7 +348,7 @@
         compiler_params=params(20),
         cost_estimate=pl.CostEstimate(flops=2 * touch * bags * feature, bytes_accessed=8 * MIB, transcendentals=0),
         name="pool",
-    )(in_hbm(touched_rows), packed, peers[0], in_hbm(table))
+    )(in_hbm(touched_rows), packed, in_hbm(table))
 
     parts = mp // 2
     payloads = pl.pallas_call(
@@ -360,53 +362,64 @@
     far = [swap(payloads[c], "mp", 2 * c) for c in range(1, parts)]
 
     rest_counts, accum_held, history, spread = pl.pallas_call(
-        functools.partial(counts_kernel, hots, mp),
+        functools.partial(counts_kernel, hots),
         out_shape=[
-            jax.ShapeDtypeStruct((touch, bags * (replicas - 2)), low),
+            jax.ShapeDtypeStruct((touch, bags * (replicas - 1)), low),
             jax.ShapeDtypeStruct((table_rows, feature), jnp.float32),
             jax.ShapeDtypeStruct((touch, feature), jnp.float32),
             jax.ShapeDtypeStruct((table_rows, touch), low),
         ],
-        in_specs=[hbm(), vmem(), hbm()] + [vmem()] * (replicas - 2),
+        in_specs=[hbm(), vmem(), hbm()] + [vmem()] * (replicas - 1),
         out_specs=[vmem()] * 4,
         scratch_shapes=[pltpu.VMEM((lookups, LANES), jnp.float32)] * 2
         + [pltpu.SMEM((touch,), jnp.int32), pltpu.SemaphoreType.DMA((2,))],
         compiler_params=params(24),
         cost_estimate=pl.CostEstimate(flops=0, bytes_accessed=1024, transcendentals=0),
         name="count",
-    )(in_hbm(touched_rows), touched_rows.reshape(touch // LANES, LANES), in_hbm(accum), *peers[1:])
-
-    same = [payloads[0], *hold(far, [rest_counts])]
-    other = [swap(value, "mp", 1) for value in same]
+    )(in_hbm(touched_rows), touched_rows.reshape(touch // LANES, LANES), in_hbm(accum), *peers)
+
+    same, pooled_sum = pl.pallas_call(
+        functools.partial(merge_kernel, rows),
+        out_shape=[
+            jax.ShapeDtypeStruct((parts * (replicas + 1) * rows, feature), low),
+            jax.ShapeDtypeStruct((rows, feature), jnp.float32),
+        ],
+        in_specs=[vmem(), pl.BlockSpec(memory_space=pl.ANY)] + [vmem()] * parts,
+        out_specs=[vmem()] * 2,
+        compiler_params=params(8),
+        name="merge",
+    )(keep, rest_counts, payloads[0], *far)
+    other = swap(same, "mp", 1)
 
     first = pl.pallas_call(
-        functools.partial(grad_kernel, rows, replicas),
+        functools.partial(grad_kernel, parts, rows),
         out_shape=jax.ShapeDtypeStruct((touch, feature), jnp.float32),
-        in_specs=[vmem()] * (2 + mp // 2),
+        in_specs=[vmem()] * 3,
         out_specs=vmem(),
         scratch_shapes=[pltpu.VMEM((bags * replicas // 2, feature), low)],
         compiler_params=params(16),
         cost_estimate=pl.CostEstimate(flops=0, bytes_accessed=1024, transcendentals=0),
         name="gradient",
-    )(near_counts, rest_counts, *same)
+    )(near_counts, rest_counts, same)
 
     new_table, new_accum, pooled = pl.pallas_call(
-        functools.partial(update_kernel, parts, rows, replicas),
+        functools.partial(update_kernel, parts, rows),
         out_shape=[jax.ShapeDtypeStruct(table.shape, jnp.float32)] * 2
         + [jax.ShapeDtypeStruct((rows, feature), jnp.float32)],
-        in_specs=[vmem()] * (7 + 2 * parts),
-        out_specs=[hbm()] * 2 + [vmem()],
+        in_specs=[vmem()] * 9,
+        out_specs=[hbm()] * 3,
         scratch_shapes=[
             pltpu.VMEM((bags * replicas // 2, feature), low),
             pltpu.VMEM((touch, 2 * feature), low),
             pltpu.VMEM((table_rows, feature), jnp.float32),
             pltpu.VMEM((table_rows, feature), jnp.float32),
-            pltpu.SemaphoreType.DMA((2, 8)),
+            pltpu.VMEM((rows, feature), jnp.float32),
+            pltpu.SemaphoreType.DMA((3, 8)),
         ],
         compiler_params=params(24),
         cost_estimate=pl.CostEstimate(flops=0, bytes_accessed=MIB, transcendentals=0),
         name="update",
-    )(near_counts, rest_counts, first, history, spread, table_held, accum_held, keep, *same[1:], *other)
+    )(near_counts, rest_counts, first, history, spread, table_held, accum_held, pooled_sum, other)
     return (pooled, new_table, new_accum)
 
 

time: 31.6 us -> 30.5 us (0.965)
  waiting for transfers between devices: 3.07 us -> 2.34 us
  starting transfers between devices: 9.81 us -> 9.38 us
    ppermute x10 -> x7, waiting for transfers between devices: 3.07 us -> 2.34 us  [swap(): lax.ppermute(value, axis, [(i, i ^ distance) for i in range(lax.axis_size...]
    pallas_call x4, Pallas kernels: 13 us -> 13.6 us  [the longest x1 7.28 us: per_device_small(): pl.pallas_call(functools.partial(counts_kernel, hots), out_shape=[jax.Sha...]
    pallas_call x1, Pallas kernels: 3.83 us -> 3.28 us  [per_device_small(): pl.pallas_call(functools.partial(pooled_kernel, hots, mp), out_shape=[jax...]
    ppermute x10 -> x7, starting transfers between devices: 9.81 us -> 9.38 us  [swap(): lax.ppermute(value, axis, [(i, i ^ distance) for i in range(lax.axis_size...]
  transfers between devices with their start and end apart: 10 -> 7, of which waited for: 4 -> 3; matrix products, arithmetic and copies ran while one was open for 0% -> 0% of each run, Pallas kernels for 36% -> 39%
where the time goes in v4:
time: 30.5 us; the launch traced here: 30.2 us
  Pallas kernels  17.8 us (58%)
  starting transfers between devices  9.38 us (31%)
  waiting for transfers between devices  2.34 us (8%)
  between operations  0.7 us (2%)
    ppermute x7, starting transfers between devices, swap(): lax.ppermute(value, axis, [(i, i ^ distance) for i in range(lax.axis_size...  9.38 us
    pallas_call x1, Pallas kernels, per_device_small(): pl.pallas_call(functools.partial(counts_kernel, hots), out_shape=[jax.Sha...  7.28 us
    pallas_call x1, Pallas kernels, per_device_small(): pl.pallas_call(functools.partial(update_kernel, parts, rows), out_shape=[...  4.92 us
    pallas_call x1, Pallas kernels, per_device_small(): pl.pallas_call(functools.partial(pooled_kernel, hots, mp), out_shape=[jax...  3.28 us
    ppermute x7, waiting for transfers between devices, swap(): lax.ppermute(value, axis, [(i, i ^ distance) for i in range(lax.axis_size...  2.34 us
    pallas_call x1, Pallas kernels, per_device_small(): pl.pallas_call(functools.partial(grad_kernel, parts, rows), out_shape=jax...  1.31 us
    pallas_call x1, Pallas kernels, per_device_small(): pl.pallas_call(pack_kernel, out_shape=jax.ShapeDtypeStruct((rows + 2 * lo...  0.85 us
  transfers between devices with their start and end apart: 7, of which 3 were waited for; matrix products, arithmetic and copies ran while one was open for 0% of the time, Pallas kernels for 39%

profile of v4, /device:TPU:0, one launch (start us, length us, event | category | flops | bytes accessed | tf_op | source)
XLA Modules:
  0.0 30.2 jit_solution(12254838878572111000)
XLA Ops:
  0.6 0.9 %pack.1.packed_ref.refs_0_ = bf16[192,128]{1,0:T(8,128)(2,1)S(1)} custom-call(bf16[128,128]{1,0:T(8,128)(2,1)} %grad_hbm.1, s32[4,1024]{1,0:T(4,128)} %bitcast.4, s32[4,1024]{1,0:T(4,128)} %bitcast.5), custom_call_target="tpu_custom_call" | custom-call | tf_op jit(solution)/shard_map/pack/pallas_call | solution.py:317
  1.5 5.1 %collective-permute-start.2 = (bf16[192,128]{1,0:T(8,128)(2,1)S(1)}, bf16[192,128]{1,0:T(8,128)(2,1)S(1)}, u32[]{:S(2)}, u32[]{:S(2)}) collective-permute-start(bf16[192,128]{1,0:T(8,128)(2,1)S(1)} %pack.1.packed_ref.refs_0_), channel_id=1, source_target_pairs={{0,3},{1,2},{2,1},{3,0},{4,7},{5,6},{6,5},{7,4},{8,11},{9,10},{10,... | collective-permute-start | bytes 147464 | tf_op jit(solution)/shard_map/ppermute | solution.py:315
  6.6 0.0 collective-permute-start.1
  6.6 0.6 %collective-permute-start = (bf16[192,128]{1,0:T(8,128)(2,1)S(1)}, bf16[192,128]{1,0:T(8,128)(2,1)S(1)}, u32[]{:S(2)}, u32[]{:S(2)}) collective-permute-start(bf16[192,128]{1,0:T(8,128)(2,1)S(1)} %pack.1.packed_ref.refs_0_), channel_id=1, source_target_pairs={{0,1},{1,0},{2,3},{3,2},{4,5},{5,4},{6,7},{7,6},{8,9},{9,8},{10,11... | collective-permute-start | bytes 147464 | tf_op jit(solution)/shard_map/ppermute | solution.py:315
  7.2 3.3 %pool.1 = (f32[4,128,128]{2,1,0:T(8,128)S(1)}, f32[4,128,128]{2,1,0:T(8,128)S(1)}, bf16[1024,1024]{1,0:T(8,128)(2,1)S(1)}, f32[4096,128]{1,0:T(8,128)S(1)}) custom-call(s32[1024]{0:T(1024)} %touched_hbm.3, bf16[192,128]{1,0:T(8,128)(2,1)S(1)} %pack.1.packed_ref.refs_0_, f32[4096,128]{1,0:T(8,128)} %table_hbm.1), custom_call_target="tpu_custom_call" | custom-call | flops 268435456 | bytes 8388608 | tf_op jit(solution)/shard_map/pool/pallas_call | solution.py:330
  10.5 0.0 collective-permute-done.2.refs_2_.refs_3_
  10.5 1.1 %collective-permute-done.1.refs_1_.refs_2_ = bf16[192,128]{1,0:T(8,128)(2,1)S(1)} collective-permute-done((bf16[192,128]{1,0:T(8,128)(2,1)S(1)}, bf16[192,128]{1,0:T(8,128)(2,1)S(1)}, u32[]{:S(2)}, u32[]{:S(2)}) %collective-permute-start.1) | collective-permute-done | bytes 49184 | tf_op jit(solution)/shard_map/ppermute | solution.py:315
  11.6 0.0 collective-permute-done.refs_0_.refs_1_
  11.6 0.1 join.1
  11.7 1.6 %collective-permute-start.3 = (bf16[768,128]{1,0:T(8,128)(2,1)S(1)}, bf16[768,128]{1,0:T(8,128)(2,1)S(1)}, u32[]{:S(2)}, u32[]{:S(2)}) collective-permute-start(bf16[768,128]{1,0:T(8,128)(2,1)S(1)} %get-tuple-element.25), channel_id=1, source_target_pairs={{0,8},{4,12},{8,0},{12,4},{16,24},{20,28},{24,16},{28,20},{1,9},{5... | collective-permute-start | bytes 589832 | tf_op jit(solution)/shard_map/ppermute | solution.py:315
  13.2 1.5 %collective-permute-start.4 = (bf16[768,128]{1,0:T(8,128)(2,1)S(1)}, bf16[768,128]{1,0:T(8,128)(2,1)S(1)}, u32[]{:S(2)}, u32[]{:S(2)}) collective-permute-start(bf16[768,128]{1,0:T(8,128)(2,1)S(1)} %get-tuple-element.26), channel_id=1, source_target_pairs={{0,16},{4,20},{8,24},{12,28},{16,0},{20,4},{24,8},{28,12},{1,17},{... | collective-permute-start | bytes 589832 | tf_op jit(solution)/shard_map/ppermute | solution.py:315
  14.8 0.5 %collective-permute-start.5 = (bf16[768,128]{1,0:T(8,128)(2,1)S(1)}, bf16[768,128]{1,0:T(8,128)(2,1)S(1)}, u32[]{:S(2)}, u32[]{:S(2)}) collective-permute-start(bf16[768,128]{1,0:T(8,128)(2,1)S(1)} %get-tuple-element.27), channel_id=1, source_target_pairs={{0,24},{4,28},{8,16},{12,20},{16,8},{20,12},{24,0},{28,4},{1,25},{... | collective-permute-start | bytes 589832 | tf_op jit(solution)/shard_map/ppermute | solution.py:315
  15.2 7.3 %count.1 = (bf16[1024,3072]{1,0:T(8,128)(2,1)S(1)}, f32[4096,128]{1,0:T(8,128)S(1)}, f32[1024,128]{1,0:T(8,128)S(1)}, bf16[4096,1024]{1,0:T(8,128)(2,1)S(1)}) custom-call(s32[1024]{0:T(1024)} %touched_hbm.3, s32[8,128]{1,0:T(8,128)} %bitcast.3, f32[4096,128]{1,0:T(8,128)} %accum_hbm.1, bf16[192,128]{1,0:T(8,128)(2,1)S(1)} %collective-permute-done.refs_0_.refs_1_, ...), custom_call_target="tpu_custom_call" | custom-call | bytes 1024 | tf_op jit(solution)/shard_map/count/pallas_call | solution.py:364
  22.5 0.0 collective-permute-done.3.refs_1_
  22.5 0.5 %collective-permute-done.4.refs_2_ = bf16[768,128]{1,0:T(8,128)(2,1)S(1)} collective-permute-done((bf16[768,128]{1,0:T(8,128)(2,1)S(1)}, bf16[768,128]{1,0:T(8,128)(2,1)S(1)}, u32[]{:S(2)}, u32[]{:S(2)}) %collective-permute-start.4) | collective-permute-done | bytes 196640 | tf_op jit(solution)/shard_map/ppermute | solution.py:315
  23.0 0.0 collective-permute-done.5.refs_3_
  23.0 0.1 merge.1
  23.1 0.1 collective-permute-start.6
  23.2 1.3 %gradient.1.first_ref = f32[1024,128]{1,0:T(8,128)S(1)} custom-call(bf16[1024,1024]{1,0:T(8,128)(2,1)S(1)} %get-tuple-element.20.near_ref, bf16[1024,3072]{1,0:T(8,128)(2,1)S(1)} %get-tuple-element.21.waited_ref.rest_ref, bf16[2560,128]{1,0:T(8,128)(2,1)S(1)} %get-tuple-element.28.blocks), custom_call_target="tpu_custom_call" | custom-call | bytes 1024 | tf_op jit(solution)/shard_map/gradient/pallas_call | solution.py:394
  24.5 0.8 %collective-permute-done.6.blocks = bf16[2560,128]{1,0:T(8,128)(2,1)S(1)} collective-permute-done((bf16[2560,128]{1,0:T(8,128)(2,1)S(1)}, bf16[2560,128]{1,0:T(8,128)(2,1)S(1)}, u32[]{:S(2)}, u32[]{:S(2)}) %collective-permute-start.6) | collective-permute-done | bytes 655392 | tf_op jit(solution)/shard_map/ppermute | solution.py:315
  25.3 4.9 %update.1 = (f32[4096,128]{1,0:T(8,128)}, f32[4096,128]{1,0:T(8,128)}, f32[128,128]{1,0:T(8,128)}) custom-call(bf16[1024,1024]{1,0:T(8,128)(2,1)S(1)} %get-tuple-element.20.near_ref, bf16[1024,3072]{1,0:T(8,128)(2,1)S(1)} %get-tuple-element.21.waited_ref.rest_ref, f32[1024,128]{1,0:T(8,128)S(1)} %gradient.1.first_ref, ...), custom_call_target="tpu_custom_call" | custom-call | bytes 1048576 | tf_op jit(solution)/shard_map/update/pallas_call | solution.py:405
Async XLA Ops:
  1.5 9.0 %collective-permute-start.2 = (bf16[192,128]{1,0:T(8,128)(2,1)S(1)}, bf16[192,128]{1,0:T(8,128)(2,1)S(1)}, u32[]{:S(2)}, u32[]{:S(2)}) collective-permute-start(bf16[192,128]{1,0:T(8,128)(2,1)S(1)} %pack.1.packed_ref.refs_0_), channel_id=1, source_target_pairs={{0,3},{1,2},{2,1},{3,0},{4,7},{5,6},{6,5},{7,4},{8,11},{9,10},{10,... | collective-permute-start | bytes 147464 | tf_op jit(solution)/shard_map/ppermute | solution.py:315
  6.6 5.0 %collective-permute-start.1 = (bf16[192,128]{1,0:T(8,128)(2,1)S(1)}, bf16[192,128]{1,0:T(8,128)(2,1)S(1)}, u32[]{:S(2)}, u32[]{:S(2)}) collective-permute-start(bf16[192,128]{1,0:T(8,128)(2,1)S(1)} %pack.1.packed_ref.refs_0_), channel_id=1, source_target_pairs={{0,2},{1,3},{2,0},{3,1},{4,6},{5,7},{6,4},{7,5},{8,10},{9,11},{10,... | collective-permute-start | bytes 147464 | tf_op jit(solution)/shard_map/ppermute | solution.py:315
  6.6 5.0 %collective-permute-start = (bf16[192,128]{1,0:T(8,128)(2,1)S(1)}, bf16[192,128]{1,0:T(8,128)(2,1)S(1)}, u32[]{:S(2)}, u32[]{:S(2)}) collective-permute-start(bf16[192,128]{1,0:T(8,128)(2,1)S(1)} %pack.1.packed_ref.refs_0_), channel_id=1, source_target_pairs={{0,1},{1,0},{2,3},{3,2},{4,5},{5,4},{6,7},{7,6},{8,9},{9,8},{10,11... | collective-permute-start | bytes 147464 | tf_op jit(solution)/shard_map/ppermute | solution.py:315
  11.7 10.8 %collective-permute-start.3 = (bf16[768,128]{1,0:T(8,128)(2,1)S(1)}, bf16[768,128]{1,0:T(8,128)(2,1)S(1)}, u32[]{:S(2)}, u32[]{:S(2)}) collective-permute-start(bf16[768,128]{1,0:T(8,128)(2,1)S(1)} %get-tuple-element.25), channel_id=1, source_target_pairs={{0,8},{4,12},{8,0},{12,4},{16,24},{20,28},{24,16},{28,20},{1,9},{5... | collective-permute-start | bytes 589832 | tf_op jit(solution)/shard_map/ppermute | solution.py:315
  13.2 9.8 %collective-permute-start.4 = (bf16[768,128]{1,0:T(8,128)(2,1)S(1)}, bf16[768,128]{1,0:T(8,128)(2,1)S(1)}, u32[]{:S(2)}, u32[]{:S(2)}) collective-permute-start(bf16[768,128]{1,0:T(8,128)(2,1)S(1)} %get-tuple-element.26), channel_id=1, source_target_pairs={{0,16},{4,20},{8,24},{12,28},{16,0},{20,4},{24,8},{28,12},{1,17},{... | collective-permute-start | bytes 589832 | tf_op jit(solution)/shard_map/ppermute | solution.py:315
  14.8 8.3 %collective-permute-start.5 = (bf16[768,128]{1,0:T(8,128)(2,1)S(1)}, bf16[768,128]{1,0:T(8,128)(2,1)S(1)}, u32[]{:S(2)}, u32[]{:S(2)}) collective-permute-start(bf16[768,128]{1,0:T(8,128)(2,1)S(1)} %get-tuple-element.27), channel_id=1, source_target_pairs={{0,24},{4,28},{8,16},{12,20},{16,8},{20,12},{24,0},{28,4},{1,25},{... | collective-permute-start | bytes 589832 | tf_op jit(solution)/shard_map/ppermute | solution.py:315
  23.1 2.2 %collective-permute-start.6 = (bf16[2560,128]{1,0:T(8,128)(2,1)S(1)}, bf16[2560,128]{1,0:T(8,128)(2,1)S(1)}, u32[]{:S(2)}, u32[]{:S(2)}) collective-permute-start(bf16[2560,128]{1,0:T(8,128)(2,1)S(1)} %get-tuple-element.28.blocks), channel_id=1, source_target_pairs={{0,4},{4,0},{8,12},{12,8},{16,20},{20,16},{24,28},{28,24},{1,5},{5... | collective-permute-start | bytes 1966088 | tf_op jit(solution)/shard_map/ppermute | solution.py:315

commit v5 on v4

--- a/solution.py
+++ b/solution.py
@@ -181,67 +181,59 @@
             ref[c] = sum_t[:, pl.ds(half + c * rows, rows)].T
 
 
-def join_kernel(rows, replicas, keep_ref, send_ref, *refs):
-    packed, outs = refs[:replicas], refs[replicas:]
-    for c, out_ref in enumerate(outs):
-        for d, ref in enumerate(packed):
-            out_ref[pl.ds(d * rows, rows), :] = ref[pl.ds(0, rows), :]
-        out_ref[pl.ds(replicas * rows, rows), :] = send_ref[c].astype(jnp.bfloat16)
-        out_ref[pl.ds((replicas + 1) * rows, rows), :] = keep_ref[c].astype(jnp.bfloat16)
-
-
-def counts_kernel(hots, touched_hbm, touched_rows_ref, accum_hbm, *refs):
-    peers, refs = refs[:-8], refs[-8:]
-    counts_ref, accum_ref, history_ref, spread_ref, low_rows, code_rows, touched_ref, sem = refs
-    loads = [
-        pltpu.make_async_copy(touched_hbm, touched_ref, sem.at[0]),
-        pltpu.make_async_copy(accum_hbm, accum_ref, sem.at[1]),
-    ]
-    for load in loads:
-        load.start()
+def join_kernel(rows, *refs):
+    out_ref = refs[-1]
+    for d, ref in enumerate(refs[:-1]):
+        out_ref[pl.ds(d * rows, rows), :] = ref[pl.ds(0, rows), :]
+
+
+def halves_kernel(rows, keep_ref, got_ref, own_ref, next_ref, out_ref):
+    own_ref[...] = keep_ref[0] + got_ref[0]
+    next_ref[...] = keep_ref[2] + got_ref[2]
+    for place, c in ((0, 1), (1, 3)):
+        out_ref[pl.ds(place * rows, rows), :] = (keep_ref[c] + got_ref[c]).astype(jnp.bfloat16)
+
+
+def fold_kernel(rows, own_ref, next_ref, got_ref, own_out, next_out):
+    own_out[...] = own_ref[...] + got_ref[pl.ds(0, rows), :].astype(jnp.float32)
+    next_out[...] = next_ref[...] + got_ref[pl.ds(rows, rows), :].astype(jnp.float32)
+
+
+def counts_kernel(hots, accum_hbm, *refs):
+    peers, (counts_ref, accum_ref, low_rows, code_rows, sem) = refs[:-5], refs[-5:]
+    load = pltpu.make_async_copy(accum_hbm, accum_ref, sem)
+    load.start()
     me = lax.axis_index("mp")
     for d, ref in enumerate(peers):
         fill_counts(ref, counts_ref, d, me, hots, low_rows, code_rows)
 
-    step = 256
-    line = lax.broadcasted_iota(jnp.int32, (step, LANES), 0).astype(jnp.float32).astype(jnp.bfloat16)
-    one, zero = jnp.ones((step, LANES), jnp.bfloat16), jnp.zeros((step, LANES), jnp.bfloat16)
-
-    def spread(j, carry):
-        row = touched_rows_ref[pl.ds(j, 1), :]
-        high = lax.shift_right_logical(row, 8)
-        low = jnp.bitwise_and(row, 255).astype(jnp.float32)
-        columns = pl.ds(pl.multiple_of(j * LANES, LANES), LANES)
-        for k in range(spread_ref.shape[0] // step):
-            at = jnp.where(high == k, low, -1.0).astype(jnp.bfloat16)
-            spread_ref[pl.ds(k * step, step), columns] = jnp.where(
-                jnp.broadcast_to(at, (step, LANES)) == line, one, zero
-            )
-        return carry
-
-    lax.fori_loop(0, spread_ref.shape[1] // LANES, spread, 0)
-    for load in loads:
-        load.wait()
-
-    def gather(i, carry):
-        for u in range(16):
-            t = i * 16 + u
-            history_ref[pl.ds(t, 1), :] = accum_ref[pl.ds(touched_ref[t], 1), :]
-        return carry
-
-    lax.fori_loop(0, history_ref.shape[0] // 16, gather, 0)
-
-
-def merge_kernel(rows, keep_ref, waited_ref, *refs):
+    load.wait()
+
+
+def merge_kernel(waited_ref, *refs):
     del waited_ref
-    blocks, merged_ref, pooled_ref = refs[:-2], refs[-2], refs[-1]
+    blocks, merged_ref = refs[:-1], refs[-1]
     span = merged_ref.shape[0] // len(blocks)
-    total = keep_ref[0]
     for c, ref in enumerate(blocks):
-        merged_ref[pl.ds(c * span, span), :] = ref[pl.ds(0, span), :]
-        if c:
-            total = total + ref[pl.ds(span, rows), :].astype(jnp.float32)
-    pooled_ref[...] = total
+        merged_ref[pl.ds(c * span, span), :] = ref[...]
+
+
+def hold_kernel(*refs):
+    del refs
+
+
+def hold(values, others, flops=0):
+    n = len(values)
+    return pl.pallas_call(
+        hold_kernel,
+        out_shape=[jax.ShapeDtypeStruct(v.shape, v.dtype) for v in values],
+        in_specs=[pl.BlockSpec(memory_space=pl.ANY)] * (n + len(others)),
+        out_specs=[pl.BlockSpec(memory_space=pl.ANY)] * n,
+        input_output_aliases={i: i for i in range(n)},
+        compiler_params=params(1),
+        cost_estimate=pl.CostEstimate(flops=flops, bytes_accessed=0, transcendentals=0),
+        name="hold",
+    )(*values, *others)
 
 
 def parity_sum(odd, parts, rows, near_ref, rest_ref, blocks, grads):
@@ -249,7 +241,7 @@
     replicas = grads.shape[0] // span
     for c in range(parts):
         for d in range(replicas):
-            grads[pl.ds(d * span + c * rows, rows), :] = blocks[pl.ds((c * (replicas + 1) + d) * rows, rows), :]
+            grads[pl.ds(d * span + c * rows, rows), :] = blocks[pl.ds((c * replicas + d) * rows, rows), :]
     near = near_ref.shape[1] // 2
     rest = rest_ref.shape[1] // 2
     return jnp.dot(
@@ -263,36 +255,36 @@
     sum_ref[...] = parity_sum(0, parts, rows, near_ref, rest_ref, blocks, grads)
 
 
-def update_kernel(parts, rows, near_ref, rest_ref, first_ref, history_ref, spread_ref, table_ref, accum_ref,
-                  sum_ref, blocks, new_table_ref, new_accum_ref, pooled_ref, grads, change, table_vmem, accum_vmem,
-                  pooled_vmem, out_sem):
-    width = first_ref.shape[1]
-    chunks = 8
-    pooled = sum_ref[...]
-    span = blocks.shape[0] // parts
-    for c in range(parts):
-        pooled = pooled + blocks[pl.ds((c + 1) * span - rows, rows), :].astype(jnp.float32)
-    pooled_vmem[...] = pooled
+def spread_kernel(parts, rows, touched_hbm, near_ref, rest_ref, first_ref, blocks, full, grads, summed, touched_ref,
+                  sem):
+    load = pltpu.make_async_copy(touched_hbm, touched_ref, sem)
+    load.start()
+    full[...] = jnp.zeros_like(full)
+    summed[...] = first_ref[...] + parity_sum(1, parts, rows, near_ref, rest_ref, blocks, grads)
+    load.wait()
+
+    def scatter(i, carry):
+        for u in range(32):
+            t = i * 32 + u
+            full[pl.ds(touched_ref[t], 1), :] = summed[pl.ds(t, 1), :]
+        return carry
+
+    lax.fori_loop(0, summed.shape[0] // 32, scatter, 0)
+
+
+def update_kernel(full, table_ref, accum_ref, own_ref, last_ref, new_table_ref, new_accum_ref, pooled_ref,
+                  table_vmem, accum_vmem, pooled_vmem, out_sem):
+    pooled_vmem[...] = own_ref[...] + last_ref[...]
     stores = [pltpu.make_async_copy(pooled_vmem, pooled_ref, out_sem.at[2, 0])]
     stores[0].start()
-    gradient = first_ref[...] + parity_sum(1, parts, rows, near_ref, rest_ref, blocks, grads)
-    square = gradient * gradient
-    step = learn_rate * gradient * lax.rsqrt(history_ref[...] + square)
-    change[:, pl.ds(0, width)] = step.astype(jnp.bfloat16)
-    change[:, pl.ds(width, width)] = square.astype(jnp.bfloat16)
+    chunks = 8
     size = table_vmem.shape[0] // chunks
-
-    def spread(c):
-        return jnp.dot(spread_ref[pl.ds(c * size, size), :], change[...], preferred_element_type=jnp.float32)
-
-    ahead = spread(0)
     for c in range(chunks):
         part = pl.ds(c * size, size)
-        full = ahead
-        if c + 1 < chunks:
-            ahead = spread(c + 1)
-        table_vmem[part, :] = table_ref[part, :] - full[:, :width]
-        accum_vmem[part, :] = accum_ref[part, :] + full[:, width:]
+        change = full[part, :]
+        history = accum_ref[part, :] + change * change
+        table_vmem[part, :] = table_ref[part, :] - learn_rate * change * lax.rsqrt(history)
+        accum_vmem[part, :] = history
         for held, out, s in ((table_vmem, new_table_ref, 0), (accum_vmem, new_accum_ref, 1)):
             store = pltpu.make_async_copy(held.at[part, :], out.at[part, :], out_sem.at[s, c])
             store.start()
@@ -351,44 +343,59 @@
     )(in_hbm(touched_rows), packed, in_hbm(table))
 
     parts = mp // 2
-    payloads = pl.pallas_call(
-        functools.partial(join_kernel, rows, replicas),
-        out_shape=[jax.ShapeDtypeStruct(((replicas + 2) * rows, feature), low)] * parts,
-        in_specs=[vmem()] * (2 + replicas),
-        out_specs=[vmem()] * parts,
+    got = swap(send, "mp", 1)
+    peers = hold(peers, [keep], 1 << 34)
+    joined = pl.pallas_call(
+        functools.partial(join_kernel, rows),
+        out_shape=jax.ShapeDtypeStruct((replicas * rows, feature), low),
+        in_specs=[vmem()] * replicas,
+        out_specs=vmem(),
         compiler_params=params(8),
         name="join",
-    )(keep, send, packed, *peers)
-    far = [swap(payloads[c], "mp", 2 * c) for c in range(1, parts)]
-
-    rest_counts, accum_held, history, spread = pl.pallas_call(
+    )(packed, *peers)
+    far = [swap(joined, "mp", 2 * c) for c in range(1, parts)]
+
+    block = jax.ShapeDtypeStruct((rows, feature), jnp.float32)
+    own_sum, next_sum, across = pl.pallas_call(
+        functools.partial(halves_kernel, rows),
+        out_shape=[block, block, jax.ShapeDtypeStruct((2 * rows, feature), low)],
+        in_specs=[vmem()] * 2,
+        out_specs=[vmem()] * 3,
+        compiler_params=params(8),
+        name="halves",
+    )(keep, got)
+    own_sum, next_sum = pl.pallas_call(
+        functools.partial(fold_kernel, rows),
+        out_shape=[block] * 2,
+        in_specs=[vmem()] * 3,
+        out_specs=[vmem()] * 2,
+        compiler_params=params(8),
+        name="fold",
+    )(own_sum, next_sum, swap(across, "mp", 2))
+    last_sum = swap(next_sum, "mp", 4)
+
+    rest_counts, accum_held = pl.pallas_call(
         functools.partial(counts_kernel, hots),
         out_shape=[
             jax.ShapeDtypeStruct((touch, bags * (replicas - 1)), low),
             jax.ShapeDtypeStruct((table_rows, feature), jnp.float32),
-            jax.ShapeDtypeStruct((touch, feature), jnp.float32),
-            jax.ShapeDtypeStruct((table_rows, touch), low),
         ],
-        in_specs=[hbm(), vmem(), hbm()] + [vmem()] * (replicas - 1),
-        out_specs=[vmem()] * 4,
-        scratch_shapes=[pltpu.VMEM((lookups, LANES), jnp.float32)] * 2
-        + [pltpu.SMEM((touch,), jnp.int32), pltpu.SemaphoreType.DMA((2,))],
+        in_specs=[hbm()] + [vmem()] * (replicas - 1),
+        out_specs=[vmem()] * 2,
+        scratch_shapes=[pltpu.VMEM((lookups, LANES), jnp.float32)] * 2 + [pltpu.SemaphoreType.DMA],
         compiler_params=params(24),
-        cost_estimate=pl.CostEstimate(flops=0, bytes_accessed=1024, transcendentals=0),
+        cost_estimate=pl.CostEstimate(flops=0, bytes_accessed=0, transcendentals=0),
         name="count",
-    )(in_hbm(touched_rows), touched_rows.reshape(touch // LANES, LANES), in_hbm(accum), *peers)
-
-    same, pooled_sum = pl.pallas_call(
-        functools.partial(merge_kernel, rows),
-        out_shape=[
-            jax.ShapeDtypeStruct((parts * (replicas + 1) * rows, feature), low),
-            jax.ShapeDtypeStruct((rows, feature), jnp.float32),
-        ],
-        in_specs=[vmem(), pl.BlockSpec(memory_space=pl.ANY)] + [vmem()] * parts,
-        out_specs=[vmem()] * 2,
+    )(in_hbm(accum), *peers)
+
+    same = pl.pallas_call(
+        merge_kernel,
+        out_shape=jax.ShapeDtypeStruct((parts * replicas * rows, feature), low),
+        in_specs=[pl.BlockSpec(memory_space=pl.ANY)] + [vmem()] * parts,
+        out_specs=vmem(),
         compiler_params=params(8),
         name="merge",
-    )(keep, rest_counts, payloads[0], *far)
+    )(rest_counts, joined, *far)
     other = swap(same, "mp", 1)
 
     first = pl.pallas_call(
@@ -398,28 +405,41 @@
         out_specs=vmem(),
         scratch_shapes=[pltpu.VMEM((bags * replicas // 2, feature), low)],
         compiler_params=params(16),
-        cost_estimate=pl.CostEstimate(flops=0, bytes_accessed=1024, transcendentals=0),
+        cost_estimate=pl.CostEstimate(flops=1 << 34, bytes_accessed=0, transcendentals=0),
         name="gradient",
     )(near_counts, rest_counts, same)
 
+    full = pl.pallas_call(
+        functools.partial(spread_kernel, parts, rows),
+        out_shape=jax.ShapeDtypeStruct((table_rows, feature), jnp.float32),
+        in_specs=[hbm()] + [vmem()] * 4,
+        out_specs=vmem(),
+        scratch_shapes=[
+            pltpu.VMEM((bags * replicas // 2, feature), low),
+            pltpu.VMEM((touch, feature), jnp.float32),
+            pltpu.SMEM((touch,), jnp.int32),
+            pltpu.SemaphoreType.DMA,
+        ],
+        compiler_params=params(16),
+        cost_estimate=pl.CostEstimate(flops=0, bytes_accessed=MIB, transcendentals=0),
+        name="spread",
+    )(in_hbm(touched_rows), near_counts, rest_counts, first, other)
+
     new_table, new_accum, pooled = pl.pallas_call(
-        functools.partial(update_kernel, parts, rows),
-        out_shape=[jax.ShapeDtypeStruct(table.shape, jnp.float32)] * 2
-        + [jax.ShapeDtypeStruct((rows, feature), jnp.float32)],
-        in_specs=[vmem()] * 9,
+        update_kernel,
+        out_shape=[jax.ShapeDtypeStruct(table.shape, jnp.float32)] * 2 + [block],
+        in_specs=[vmem()] * 5,
         out_specs=[hbm()] * 3,
         scratch_shapes=[
-            pltpu.VMEM((bags * replicas // 2, feature), low),
-            pltpu.VMEM((touch, 2 * feature), low),
             pltpu.VMEM((table_rows, feature), jnp.float32),
             pltpu.VMEM((table_rows, feature), jnp.float32),
             pltpu.VMEM((rows, feature), jnp.float32),
             pltpu.SemaphoreType.DMA((3, 8)),
         ],
-        compiler_params=params(24),
+        compiler_params=params(16),
         cost_estimate=pl.CostEstimate(flops=0, bytes_accessed=MIB, transcendentals=0),
         name="update",
-    )(near_counts, rest_counts, first, history, spread, table_held, accum_held, pooled_sum, other)
+    )(full, table_held, accum_held, own_sum, last_sum)
     return (pooled, new_table, new_accum)
 
 
@@ -431,7 +451,7 @@
     rows = pooled_grad.shape[0] // (mp * replicas)
     return (
         powers
-        and 2 <= mp <= 8
+        and mp == 8
         and replicas == 4
         and lookup_slots.shape[0] * touch <= 4096 * 1024
         and touch % 256 == 0

time: 30.5 us -> 28.9 us (0.948)
  Pallas kernels: 17.8 us -> 13.6 us
  starting transfers between devices: 9.38 us -> 11.5 us
  waiting for transfers between devices: 2.34 us -> 2.81 us
    pallas_call x1, Pallas kernels: 7.28 us -> 3.21 us  [per_device_small(): pl.pallas_call(functools.partial(counts_kernel, hots), out_shape=[jax.Sha...]
    ppermute x7 -> x10, starting transfers between devices: 9.38 us -> 11.5 us  [swap(): lax.ppermute(value, axis, [(i, i ^ distance) for i in range(lax.axis_size...]
    ppermute x7 -> x10, waiting for transfers between devices: 2.34 us -> 2.81 us  [swap(): lax.ppermute(value, axis, [(i, i ^ distance) for i in range(lax.axis_size...]
    pallas_call x3 -> x7, Pallas kernels: 5.06 us -> 4.95 us  [the longest x1 2.59 us: per_device_small(): pl.pallas_call(functools.partial(spread_kernel, parts, rows), out_shape=j...]
  transfers between devices with their start and end apart: 7 -> 10, of which waited for: 3 -> 4; matrix products, arithmetic and copies ran while one was open for 0% -> 0% of each run, Pallas kernels for 39% -> 36%
where the time goes in v5:
time: 28.9 us; the launch traced here: 28.7 us
  Pallas kernels  13.6 us (47%)
  starting transfers between devices  11.5 us (40%)
  waiting for transfers between devices  2.81 us (10%)
  between operations  0.74 us (3%)
    ppermute x10, starting transfers between devices, swap(): lax.ppermute(value, axis, [(i, i ^ distance) for i in range(lax.axis_size...  11.5 us
    pallas_call x1, Pallas kernels, per_device_small(): pl.pallas_call(functools.partial(pooled_kernel, hots, mp), out_shape=[jax...  3.28 us
    pallas_call x1, Pallas kernels, per_device_small(): pl.pallas_call(functools.partial(counts_kernel, hots), out_shape=[jax.Sha...  3.21 us
    ppermute x10, waiting for transfers between devices, swap(): lax.ppermute(value, axis, [(i, i ^ distance) for i in range(lax.axis_size...  2.81 us
    pallas_call x1, Pallas kernels, per_device_small(): pl.pallas_call(functools.partial(spread_kernel, parts, rows), out_shape=j...  2.59 us
    pallas_call x1, Pallas kernels, per_device_small(): pl.pallas_call(update_kernel, out_shape=[jax.ShapeDtypeStruct(table.shape...  2.27 us
    pallas_call x1, Pallas kernels, per_device_small(): pl.pallas_call(functools.partial(grad_kernel, parts, rows), out_shape=jax...  1.31 us
    pallas_call x1, Pallas kernels, per_device_small(): pl.pallas_call(pack_kernel, out_shape=jax.ShapeDtypeStruct((rows + 2 * lo...  0.85 us
  transfers between devices with their start and end apart: 10, of which 4 were waited for; matrix products, arithmetic and copies ran while one was open for 0% of the time, Pallas kernels for 36%

profile of v5, /device:TPU:0, one launch (start us, length us, event | category | flops | bytes accessed | tf_op | source)
XLA Modules:
  0.0 28.7 jit_solution(16119571213281411465)
XLA Ops:
  0.6 0.9 %pack.1.packed_ref.refs_0_ = bf16[192,128]{1,0:T(8,128)(2,1)S(1)} custom-call(bf16[128,128]{1,0:T(8,128)(2,1)} %grad_hbm.1, s32[4,1024]{1,0:T(4,128)} %bitcast.2, s32[4,1024]{1,0:T(4,128)} %bitcast.3), custom_call_target="tpu_custom_call" | custom-call | tf_op jit(solution)/shard_map/pack/pallas_call | solution.py:309
  1.5 5.1 %collective-permute-start.2 = (bf16[192,128]{1,0:T(8,128)(2,1)S(1)}, bf16[192,128]{1,0:T(8,128)(2,1)S(1)}, u32[]{:S(2)}, u32[]{:S(2)}) collective-permute-start(bf16[192,128]{1,0:T(8,128)(2,1)S(1)} %pack.1.packed_ref.refs_0_), channel_id=1, source_target_pairs={{0,3},{1,2},{2,1},{3,0},{4,7},{5,6},{6,5},{7,4},{8,11},{9,10},{10,... | collective-permute-start | bytes 147464 | tf_op jit(solution)/shard_map/ppermute | solution.py:307
  6.6 0.0 collective-permute-start.1
  6.6 0.6 %collective-permute-start = (bf16[192,128]{1,0:T(8,128)(2,1)S(1)}, bf16[192,128]{1,0:T(8,128)(2,1)S(1)}, u32[]{:S(2)}, u32[]{:S(2)}) collective-permute-start(bf16[192,128]{1,0:T(8,128)(2,1)S(1)} %pack.1.packed_ref.refs_0_), channel_id=1, source_target_pairs={{0,1},{1,0},{2,3},{3,2},{4,5},{5,4},{6,7},{7,6},{8,9},{9,8},{10,11... | collective-permute-start | bytes 147464 | tf_op jit(solution)/shard_map/ppermute | solution.py:307
  7.2 3.3 %pool.1 = (f32[4,128,128]{2,1,0:T(8,128)S(1)}, f32[4,128,128]{2,1,0:T(8,128)S(1)}, bf16[1024,1024]{1,0:T(8,128)(2,1)S(1)}, f32[4096,128]{1,0:T(8,128)S(1)}) custom-call(s32[1024]{0:T(1024)} %touched_hbm.3, bf16[192,128]{1,0:T(8,128)(2,1)S(1)} %pack.1.packed_ref.refs_0_, f32[4096,128]{1,0:T(8,128)} %table_hbm.1), custom_call_target="tpu_custom_call" | custom-call | flops 268435456 | bytes 8388608 | tf_op jit(solution)/shard_map/pool/pallas_call | solution.py:322
  10.5 0.1 collective-permute-start.7
  10.6 0.0 collective-permute-done.2.refs_2_
  10.6 1.0 %collective-permute-done.1.refs_1_ = bf16[192,128]{1,0:T(8,128)(2,1)S(1)} collective-permute-done((bf16[192,128]{1,0:T(8,128)(2,1)S(1)}, bf16[192,128]{1,0:T(8,128)(2,1)S(1)}, u32[]{:S(2)}, u32[]{:S(2)}) %collective-permute-start.1) | collective-permute-done | bytes 49184 | tf_op jit(solution)/shard_map/ppermute | solution.py:307
  11.6 0.0 collective-permute-done.refs_0_
  11.6 2.5 %collective-permute-start.5 = (bf16[512,128]{1,0:T(8,128)(2,1)S(1)}, bf16[512,128]{1,0:T(8,128)(2,1)S(1)}, u32[]{:S(2)}, u32[]{:S(2)}) collective-permute-start(bf16[512,128]{1,0:T(8,128)(2,1)S(1)} %join.1.refs_0_), channel_id=1, source_target_pairs={{0,24},{4,28},{8,16},{12,20},{16,8},{20,12},{24,0},{28,4},{1,25},{... | collective-permute-start | bytes 393224 | tf_op jit(solution)/shard_map/ppermute | solution.py:307
  14.1 0.5 %collective-permute-start.4 = (bf16[512,128]{1,0:T(8,128)(2,1)S(1)}, bf16[512,128]{1,0:T(8,128)(2,1)S(1)}, u32[]{:S(2)}, u32[]{:S(2)}) collective-permute-start(bf16[512,128]{1,0:T(8,128)(2,1)S(1)} %join.1.refs_0_), channel_id=1, source_target_pairs={{0,16},{4,20},{8,24},{12,28},{16,0},{20,4},{24,8},{28,12},{1,17},{... | collective-permute-start | bytes 393224 | tf_op jit(solution)/shard_map/ppermute | solution.py:307
  14.6 0.5 %collective-permute-start.3 = (bf16[512,128]{1,0:T(8,128)(2,1)S(1)}, bf16[512,128]{1,0:T(8,128)(2,1)S(1)}, u32[]{:S(2)}, u32[]{:S(2)}) collective-permute-start(bf16[512,128]{1,0:T(8,128)(2,1)S(1)} %join.1.refs_0_), channel_id=1, source_target_pairs={{0,8},{4,12},{8,0},{12,4},{16,24},{20,28},{24,16},{28,20},{1,9},{5... | collective-permute-start | bytes 393224 | tf_op jit(solution)/shard_map/ppermute | solution.py:307
  15.2 0.0 collective-permute-done.7.got_ref
  15.2 1.6 %collective-permute-start.8 = (bf16[256,128]{1,0:T(8,128)(2,1)S(1)}, bf16[256,128]{1,0:T(8,128)(2,1)S(1)}, u32[]{:S(2)}, u32[]{:S(2)}) collective-permute-start(bf16[256,128]{1,0:T(8,128)(2,1)S(1)} %get-tuple-element.31), channel_id=1, source_target_pairs={{0,8},{4,12},{8,0},{12,4},{16,24},{20,28},{24,16},{28,20},{1,9},{5... | collective-permute-start | bytes 196616 | tf_op jit(solution)/shard_map/ppermute | solution.py:307
  16.8 3.2 %count.1 = (bf16[1024,3072]{1,0:T(8,128)(2,1)S(1)}, f32[4096,128]{1,0:T(8,128)S(1)}) custom-call(f32[4096,128]{1,0:T(8,128)} %accum_hbm.1, bf16[192,128]{1,0:T(8,128)(2,1)S(1)} %get-tuple-element.22.refs_0_.refs_1_, bf16[192,128]{1,0:T(8,128)(2,1)S(1)} %get-tuple-element.23.refs_1_.refs_2_, bf16[192,128]{1,0:T(8,128)(2,1)S(1)} %get-tuple-element.24.refs_2_.refs_3_), custom_call_target="tpu_custom_call" | custom-call | tf_op jit(solution)/shard_map/count/pallas_call | solution.py:377
  20.0 0.0 collective-permute-done.5.refs_3_
  20.0 0.3 %collective-permute-done.4.refs_2_ = bf16[512,128]{1,0:T(8,128)(2,1)S(1)} collective-permute-done((bf16[512,128]{1,0:T(8,128)(2,1)S(1)}, bf16[512,128]{1,0:T(8,128)(2,1)S(1)}, u32[]{:S(2)}, u32[]{:S(2)}) %collective-permute-start.4) | collective-permute-done | bytes 131104 | tf_op jit(solution)/shard_map/ppermute | solution.py:307
  20.3 0.9 %collective-permute-done.3.refs_1_ = bf16[512,128]{1,0:T(8,128)(2,1)S(1)} collective-permute-done((bf16[512,128]{1,0:T(8,128)(2,1)S(1)}, bf16[512,128]{1,0:T(8,128)(2,1)S(1)}, u32[]{:S(2)}, u32[]{:S(2)}) %collective-permute-start.3) | collective-permute-done | bytes 131104 | tf_op jit(solution)/shard_map/ppermute | solution.py:307
  21.3 0.1 collective-permute-start.6
  21.3 0.6 %collective-permute-done.8.got_ref = bf16[256,128]{1,0:T(8,128)(2,1)S(1)} collective-permute-done((bf16[256,128]{1,0:T(8,128)(2,1)S(1)}, bf16[256,128]{1,0:T(8,128)(2,1)S(1)}, u32[]{:S(2)}, u32[]{:S(2)}) %collective-permute-start.8) | collective-permute-done | bytes 65568 | tf_op jit(solution)/shard_map/ppermute | solution.py:307
  22.0 0.5 %collective-permute-start.9 = (f32[128,128]{1,0:T(8,128)S(1)}, f32[128,128]{1,0:T(8,128)S(1)}, u32[]{:S(2)}, u32[]{:S(2)}) collective-permute-start(f32[128,128]{1,0:T(8,128)S(1)} %get-tuple-element.33), channel_id=1, source_target_pairs={{0,16},{4,20},{8,24},{12,28},{16,0},{20,4},{24,8},{28,12},{1,17},{... | collective-permute-start | bytes 196616 | tf_op jit(solution)/shard_map/ppermute | solution.py:307
  22.4 1.3 %gradient.1.first_ref = f32[1024,128]{1,0:T(8,128)S(1)} custom-call(bf16[1024,1024]{1,0:T(8,128)(2,1)S(1)} %get-tuple-element.20.near_ref, bf16[1024,3072]{1,0:T(8,128)(2,1)S(1)} %get-tuple-element.25.waited_ref.rest_ref, bf16[2048,128]{1,0:T(8,128)(2,1)S(1)} %merge.1.blocks), custom_call_target="tpu_custom_call" | custom-call | flops 17179869184 | tf_op jit(solution)/shard_map/gradient/pallas_call | solution.py:401
  23.8 0.0 collective-permute-done.6.blocks
  23.8 2.6 %spread.1.full = f32[4096,128]{1,0:T(8,128)S(1)} custom-call(s32[1024]{0:T(1024)} %touched_hbm.3, bf16[1024,1024]{1,0:T(8,128)(2,1)S(1)} %get-tuple-element.20.near_ref, bf16[1024,3072]{1,0:T(8,128)(2,1)S(1)} %get-tuple-element.25.waited_ref.rest_ref, f32[1024,128]{1,0:T(8,128)S(1)} %gradient.1.first_ref, bf16[2048,128]{1,0:T(8,128)(2,1)S(1)} %collective-permute-done.6.blocks), custom_call_target="tpu_custom_call" | custom-call | bytes 1048576 | tf_op jit(solution)/shard_map/spread/pallas_call | solution.py:412
  26.4 0.0 collective-permute-done.9.last_ref
  26.4 2.3 %update.1 = (f32[4096,128]{1,0:T(8,128)}, f32[4096,128]{1,0:T(8,128)}, f32[128,128]{1,0:T(8,128)}) custom-call(f32[4096,128]{1,0:T(8,128)S(1)} %spread.1.full, f32[4096,128]{1,0:T(8,128)S(1)} %get-tuple-element.26.table_ref, f32[4096,128]{1,0:T(8,128)S(1)} %get-tuple-element.27.accum_ref, f32[128,128]{1,0:T(8,128)S(1)} %get-tuple-element.32.own_ref, ...), custom_call_target="tpu_custom_call" | custom-call | bytes 1048576 | tf_op jit(solution)/shard_map/update/pallas_call | solution.py:428
  (5 shorter events, 0.1 us)
Async XLA Ops:
  1.5 9.1 %collective-permute-start.2 = (bf16[192,128]{1,0:T(8,128)(2,1)S(1)}, bf16[192,128]{1,0:T(8,128)(2,1)S(1)}, u32[]{:S(2)}, u32[]{:S(2)}) collective-permute-start(bf16[192,128]{1,0:T(8,128)(2,1)S(1)} %pack.1.packed_ref.refs_0_), channel_id=1, source_target_pairs={{0,3},{1,2},{2,1},{3,0},{4,7},{5,6},{6,5},{7,4},{8,11},{9,10},{10,... | collective-permute-start | bytes 147464 | tf_op jit(solution)/shard_map/ppermute | solution.py:307
  6.6 5.0 %collective-permute-start.1 = (bf16[192,128]{1,0:T(8,128)(2,1)S(1)}, bf16[192,128]{1,0:T(8,128)(2,1)S(1)}, u32[]{:S(2)}, u32[]{:S(2)}) collective-permute-start(bf16[192,128]{1,0:T(8,128)(2,1)S(1)} %pack.1.packed_ref.refs_0_), channel_id=1, source_target_pairs={{0,2},{1,3},{2,0},{3,1},{4,6},{5,7},{6,4},{7,5},{8,10},{9,11},{10,... | collective-permute-start | bytes 147464 | tf_op jit(solution)/shard_map/ppermute | solution.py:307
  6.6 5.0 %collective-permute-start = (bf16[192,128]{1,0:T(8,128)(2,1)S(1)}, bf16[192,128]{1,0:T(8,128)(2,1)S(1)}, u32[]{:S(2)}, u32[]{:S(2)}) collective-permute-start(bf16[192,128]{1,0:T(8,128)(2,1)S(1)} %pack.1.packed_ref.refs_0_), channel_id=1, source_target_pairs={{0,1},{1,0},{2,3},{3,2},{4,5},{5,4},{6,7},{7,6},{8,9},{9,8},{10,11... | collective-permute-start | bytes 147464 | tf_op jit(solution)/shard_map/ppermute | solution.py:307
  10.5 4.6 %collective-permute-start.7 = (f32[4,128,128]{2,1,0:T(8,128)S(1)}, f32[4,128,128]{2,1,0:T(8,128)S(1)}, u32[]{:S(2)}, u32[]{:S(2)}) collective-permute-start(f32[4,128,128]{2,1,0:T(8,128)S(1)} %get-tuple-element.28), channel_id=1, source_target_pairs={{0,4},{4,0},{8,12},{12,8},{16,20},{20,16},{24,28},{28,24},{1,5},{5... | collective-permute-start | bytes 786440 | tf_op jit(solution)/shard_map/ppermute | solution.py:307
  11.6 8.4 %collective-permute-start.5 = (bf16[512,128]{1,0:T(8,128)(2,1)S(1)}, bf16[512,128]{1,0:T(8,128)(2,1)S(1)}, u32[]{:S(2)}, u32[]{:S(2)}) collective-permute-start(bf16[512,128]{1,0:T(8,128)(2,1)S(1)} %join.1.refs_0_), channel_id=1, source_target_pairs={{0,24},{4,28},{8,16},{12,20},{16,8},{20,12},{24,0},{28,4},{1,25},{... | collective-permute-start | bytes 393224 | tf_op jit(solution)/shard_map/ppermute | solution.py:307
  14.1 6.2 %collective-permute-start.4 = (bf16[512,128]{1,0:T(8,128)(2,1)S(1)}, bf16[512,128]{1,0:T(8,128)(2,1)S(1)}, u32[]{:S(2)}, u32[]{:S(2)}) collective-permute-start(bf16[512,128]{1,0:T(8,128)(2,1)S(1)} %join.1.refs_0_), channel_id=1, source_target_pairs={{0,16},{4,20},{8,24},{12,28},{16,0},{20,4},{24,8},{28,12},{1,17},{... | collective-permute-start | bytes 393224 | tf_op jit(solution)/shard_map/ppermute | solution.py:307
  14.6 6.6 %collective-permute-start.3 = (bf16[512,128]{1,0:T(8,128)(2,1)S(1)}, bf16[512,128]{1,0:T(8,128)(2,1)S(1)}, u32[]{:S(2)}, u32[]{:S(2)}) collective-permute-start(bf16[512,128]{1,0:T(8,128)(2,1)S(1)} %join.1.refs_0_), channel_id=1, source_target_pairs={{0,8},{4,12},{8,0},{12,4},{16,24},{20,28},{24,16},{28,20},{1,9},{5... | collective-permute-start | bytes 393224 | tf_op jit(solution)/shard_map/ppermute | solution.py:307
  15.2 6.7 %collective-permute-start.8 = (bf16[256,128]{1,0:T(8,128)(2,1)S(1)}, bf16[256,128]{1,0:T(8,128)(2,1)S(1)}, u32[]{:S(2)}, u32[]{:S(2)}) collective-permute-start(bf16[256,128]{1,0:T(8,128)(2,1)S(1)} %get-tuple-element.31), channel_id=1, source_target_pairs={{0,8},{4,12},{8,0},{12,4},{16,24},{20,28},{24,16},{28,20},{1,9},{5... | collective-permute-start | bytes 196616 | tf_op jit(solution)/shard_map/ppermute | solution.py:307
  21.3 2.5 %collective-permute-start.6 = (bf16[2048,128]{1,0:T(8,128)(2,1)S(1)}, bf16[2048,128]{1,0:T(8,128)(2,1)S(1)}, u32[]{:S(2)}, u32[]{:S(2)}) collective-permute-start(bf16[2048,128]{1,0:T(8,128)(2,1)S(1)} %merge.1.blocks), channel_id=1, source_target_pairs={{0,4},{4,0},{8,12},{12,8},{16,20},{20,16},{24,28},{28,24},{1,5},{5... | collective-permute-start | bytes 1572872 | tf_op jit(solution)/shard_map/ppermute | solution.py:307
  22.0 4.4 %collective-permute-start.9 = (f32[128,128]{1,0:T(8,128)S(1)}, f32[128,128]{1,0:T(8,128)S(1)}, u32[]{:S(2)}, u32[]{:S(2)}) collective-permute-start(f32[128,128]{1,0:T(8,128)S(1)} %get-tuple-element.33), channel_id=1, source_target_pairs={{0,16},{4,20},{8,24},{12,28},{16,0},{20,4},{24,8},{28,12},{1,17},{... | collective-permute-start | bytes 196616 | tf_op jit(solution)/shard_map/ppermute | solution.py:307

commit v6 on v5

--- a/solution.py
+++ b/solution.py
@@ -200,7 +200,8 @@
 
 
 def counts_kernel(hots, accum_hbm, *refs):
-    peers, (counts_ref, accum_ref, low_rows, code_rows, sem) = refs[:-5], refs[-5:]
+    peers, (counts_ref, accum_ref, full_ref, low_rows, code_rows, sem) = refs[:-6], refs[-6:]
+    full_ref[...] = jnp.zeros_like(full_ref)
     load = pltpu.make_async_copy(accum_hbm, accum_ref, sem)
     load.start()
     me = lax.axis_index("mp")
@@ -255,21 +256,21 @@
     sum_ref[...] = parity_sum(0, parts, rows, near_ref, rest_ref, blocks, grads)
 
 
-def spread_kernel(parts, rows, touched_hbm, near_ref, rest_ref, first_ref, blocks, full, grads, summed, touched_ref,
-                  sem):
+def spread_kernel(parts, rows, touched_hbm, near_ref, rest_ref, first_ref, blocks, blank_ref, full, grads, summed,
+                  touched_ref, sem):
     load = pltpu.make_async_copy(touched_hbm, touched_ref, sem)
     load.start()
-    full[...] = jnp.zeros_like(full)
+    del blank_ref
     summed[...] = first_ref[...] + parity_sum(1, parts, rows, near_ref, rest_ref, blocks, grads)
     load.wait()
 
     def scatter(i, carry):
-        for u in range(32):
-            t = i * 32 + u
+        for u in range(128):
+            t = i * 128 + u
             full[pl.ds(touched_ref[t], 1), :] = summed[pl.ds(t, 1), :]
         return carry
 
-    lax.fori_loop(0, summed.shape[0] // 32, scatter, 0)
+    lax.fori_loop(0, summed.shape[0] // 128, scatter, 0)
 
 
 def update_kernel(full, table_ref, accum_ref, own_ref, last_ref, new_table_ref, new_accum_ref, pooled_ref,
@@ -374,14 +375,15 @@
     )(own_sum, next_sum, swap(across, "mp", 2))
     last_sum = swap(next_sum, "mp", 4)
 
-    rest_counts, accum_held = pl.pallas_call(
+    rest_counts, accum_held, blank = pl.pallas_call(
         functools.partial(counts_kernel, hots),
         out_shape=[
             jax.ShapeDtypeStruct((touch, bags * (replicas - 1)), low),
             jax.ShapeDtypeStruct((table_rows, feature), jnp.float32),
+            jax.ShapeDtypeStruct((table_rows, feature), jnp.float32),
         ],
         in_specs=[hbm()] + [vmem()] * (replicas - 1),
-        out_specs=[vmem()] * 2,
+        out_specs=[vmem()] * 3,
         scratch_shapes=[pltpu.VMEM((lookups, LANES), jnp.float32)] * 2 + [pltpu.SemaphoreType.DMA],
         compiler_params=params(24),
         cost_estimate=pl.CostEstimate(flops=0, bytes_accessed=0, transcendentals=0),
@@ -412,8 +414,9 @@
     full = pl.pallas_call(
         functools.partial(spread_kernel, parts, rows),
         out_shape=jax.ShapeDtypeStruct((table_rows, feature), jnp.float32),
-        in_specs=[hbm()] + [vmem()] * 4,
+        in_specs=[hbm()] + [vmem()] * 5,
         out_specs=vmem(),
+        input_output_aliases={5: 0},
         scratch_shapes=[
             pltpu.VMEM((bags * replicas // 2, feature), low),
             pltpu.VMEM((touch, feature), jnp.float32),
@@ -423,7 +426,7 @@
         compiler_params=params(16),
         cost_estimate=pl.CostEstimate(flops=0, bytes_accessed=MIB, transcendentals=0),
         name="spread",
-    )(in_hbm(touched_rows), near_counts, rest_counts, first, other)
+    )(in_hbm(touched_rows), near_counts, rest_counts, first, other, blank)
 
     new_table, new_accum, pooled = pl.pallas_call(
         update_kernel,

time: 28.9 us -> 28.8 us (level)
  Pallas kernels: 13.6 us -> 13.3 us
    pallas_call x1, Pallas kernels: 2.59 us -> 2.18 us  [per_device_small(): pl.pallas_call(functools.partial(spread_kernel, parts, rows), out_shape=j...]
  transfers between devices with their start and end apart: 10 -> 10, of which waited for: 4 -> 5; matrix products, arithmetic and copies ran while one was open for 0% -> 0% of each run, Pallas kernels for 36% -> 36%
where the time goes in v6:
time: 28.8 us; the launch traced here: 28.5 us
  Pallas kernels  13.3 us (46%)
  starting transfers between devices  11.5 us (40%)
  waiting for transfers between devices  3 us (10%)
  between operations  0.73 us (3%)
    ppermute x10, starting transfers between devices, swap(): lax.ppermute(value, axis, [(i, i ^ distance) for i in range(lax.axis_size...  11.5 us
    pallas_call x1, Pallas kernels, per_device_small(): pl.pallas_call(functools.partial(counts_kernel, hots), out_shape=[jax.Sha...  3.35 us
    pallas_call x1, Pallas kernels, per_device_small(): pl.pallas_call(functools.partial(pooled_kernel, hots, mp), out_shape=[jax...  3.28 us
    ppermute x10, waiting for transfers between devices, swap(): lax.ppermute(value, axis, [(i, i ^ distance) for i in range(lax.axis_size...  3 us
    pallas_call x1, Pallas kernels, per_device_small(): pl.pallas_call(update_kernel, out_shape=[jax.ShapeDtypeStruct(table.shape...  2.27 us
    pallas_call x1, Pallas kernels, per_device_small(): pl.pallas_call(functools.partial(spread_kernel, parts, rows), out_shape=j...  2.18 us
    pallas_call x1, Pallas kernels, per_device_small(): pl.pallas_call(functools.partial(grad_kernel, parts, rows), out_shape=jax...  1.31 us
    pallas_call x1, Pallas kernels, per_device_small(): pl.pallas_call(pack_kernel, out_shape=jax.ShapeDtypeStruct((rows + 2 * lo...  0.85 us
  transfers between devices with their start and end apart: 10, of which 5 were waited for; matrix products, arithmetic and copies ran while one was open for 0% of the time, Pallas kernels for 36%

profile of v6, /device:TPU:0, one launch (start us, length us, event | category | flops | bytes accessed | tf_op | source)
XLA Modules:
  0.0 28.5 jit_solution(4308895829116425973)
XLA Ops:
  0.6 0.9 %pack.1.packed_ref.refs_0_ = bf16[192,128]{1,0:T(8,128)(2,1)S(1)} custom-call(bf16[128,128]{1,0:T(8,128)(2,1)} %grad_hbm.1, s32[4,1024]{1,0:T(4,128)} %bitcast.2, s32[4,1024]{1,0:T(4,128)} %bitcast.3), custom_call_target="tpu_custom_call" | custom-call | tf_op jit(solution)/shard_map/pack/pallas_call | solution.py:310
  1.5 5.1 %collective-permute-start.2 = (bf16[192,128]{1,0:T(8,128)(2,1)S(1)}, bf16[192,128]{1,0:T(8,128)(2,1)S(1)}, u32[]{:S(2)}, u32[]{:S(2)}) collective-permute-start(bf16[192,128]{1,0:T(8,128)(2,1)S(1)} %pack.1.packed_ref.refs_0_), channel_id=1, source_target_pairs={{0,3},{1,2},{2,1},{3,0},{4,7},{5,6},{6,5},{7,4},{8,11},{9,10},{10,... | collective-permute-start | bytes 147464 | tf_op jit(solution)/shard_map/ppermute | solution.py:308
  6.6 0.0 collective-permute-start.1
  6.6 0.6 %collective-permute-start = (bf16[192,128]{1,0:T(8,128)(2,1)S(1)}, bf16[192,128]{1,0:T(8,128)(2,1)S(1)}, u32[]{:S(2)}, u32[]{:S(2)}) collective-permute-start(bf16[192,128]{1,0:T(8,128)(2,1)S(1)} %pack.1.packed_ref.refs_0_), channel_id=1, source_target_pairs={{0,1},{1,0},{2,3},{3,2},{4,5},{5,4},{6,7},{7,6},{8,9},{9,8},{10,11... | collective-permute-start | bytes 147464 | tf_op jit(solution)/shard_map/ppermute | solution.py:308
  7.2 3.3 %pool.1 = (f32[4,128,128]{2,1,0:T(8,128)S(1)}, f32[4,128,128]{2,1,0:T(8,128)S(1)}, bf16[1024,1024]{1,0:T(8,128)(2,1)S(1)}, f32[4096,128]{1,0:T(8,128)S(1)}) custom-call(s32[1024]{0:T(1024)} %touched_hbm.3, bf16[192,128]{1,0:T(8,128)(2,1)S(1)} %pack.1.packed_ref.refs_0_, f32[4096,128]{1,0:T(8,128)} %table_hbm.1), custom_call_target="tpu_custom_call" | custom-call | flops 268435456 | bytes 8388608 | tf_op jit(solution)/shard_map/pool/pallas_call | solution.py:323
  10.5 0.1 collective-permute-start.7
  10.6 0.0 collective-permute-done.2.refs_2_
  10.6 1.0 %collective-permute-done.1.refs_1_ = bf16[192,128]{1,0:T(8,128)(2,1)S(1)} collective-permute-done((bf16[192,128]{1,0:T(8,128)(2,1)S(1)}, bf16[192,128]{1,0:T(8,128)(2,1)S(1)}, u32[]{:S(2)}, u32[]{:S(2)}) %collective-permute-start.1) | collective-permute-done | bytes 49184 | tf_op jit(solution)/shard_map/ppermute | solution.py:308
  11.6 0.0 collective-permute-done.refs_0_
  11.6 2.5 %collective-permute-start.5 = (bf16[512,128]{1,0:T(8,128)(2,1)S(1)}, bf16[512,128]{1,0:T(8,128)(2,1)S(1)}, u32[]{:S(2)}, u32[]{:S(2)}) collective-permute-start(bf16[512,128]{1,0:T(8,128)(2,1)S(1)} %join.1.refs_0_), channel_id=1, source_target_pairs={{0,24},{4,28},{8,16},{12,20},{16,8},{20,12},{24,0},{28,4},{1,25},{... | collective-permute-start | bytes 393224 | tf_op jit(solution)/shard_map/ppermute | solution.py:308
  14.1 0.5 %collective-permute-start.4 = (bf16[512,128]{1,0:T(8,128)(2,1)S(1)}, bf16[512,128]{1,0:T(8,128)(2,1)S(1)}, u32[]{:S(2)}, u32[]{:S(2)}) collective-permute-start(bf16[512,128]{1,0:T(8,128)(2,1)S(1)} %join.1.refs_0_), channel_id=1, source_target_pairs={{0,16},{4,20},{8,24},{12,28},{16,0},{20,4},{24,8},{28,12},{1,17},{... | collective-permute-start | bytes 393224 | tf_op jit(solution)/shard_map/ppermute | solution.py:308
  14.6 0.5 %collective-permute-start.3 = (bf16[512,128]{1,0:T(8,128)(2,1)S(1)}, bf16[512,128]{1,0:T(8,128)(2,1)S(1)}, u32[]{:S(2)}, u32[]{:S(2)}) collective-permute-start(bf16[512,128]{1,0:T(8,128)(2,1)S(1)} %join.1.refs_0_), channel_id=1, source_target_pairs={{0,8},{4,12},{8,0},{12,4},{16,24},{20,28},{24,16},{28,20},{1,9},{5... | collective-permute-start | bytes 393224 | tf_op jit(solution)/shard_map/ppermute | solution.py:308
  15.2 0.0 collective-permute-done.7.got_ref
  15.2 1.6 %collective-permute-start.8 = (bf16[256,128]{1,0:T(8,128)(2,1)S(1)}, bf16[256,128]{1,0:T(8,128)(2,1)S(1)}, u32[]{:S(2)}, u32[]{:S(2)}) collective-permute-start(bf16[256,128]{1,0:T(8,128)(2,1)S(1)} %get-tuple-element.33), channel_id=1, source_target_pairs={{0,8},{4,12},{8,0},{12,4},{16,24},{20,28},{24,16},{28,20},{1,9},{5... | collective-permute-start | bytes 196616 | tf_op jit(solution)/shard_map/ppermute | solution.py:308
  16.8 3.3 %count.1 = (bf16[1024,3072]{1,0:T(8,128)(2,1)S(1)}, f32[4096,128]{1,0:T(8,128)S(1)}, f32[4096,128]{1,0:T(8,128)S(1)}) custom-call(f32[4096,128]{1,0:T(8,128)} %accum_hbm.1, bf16[192,128]{1,0:T(8,128)(2,1)S(1)} %get-tuple-element.23.refs_0_.refs_1_, bf16[192,128]{1,0:T(8,128)(2,1)S(1)} %get-tuple-element.24.refs_1_.refs_2_, ...), custom_call_target="tpu_custom_call" | custom-call | tf_op jit(solution)/shard_map/count/pallas_call | solution.py:378
  20.1 0.0 collective-permute-done.5.refs_3_
  20.1 0.2 collective-permute-done.4.refs_2_
  20.3 0.9 %collective-permute-done.3.refs_1_ = bf16[512,128]{1,0:T(8,128)(2,1)S(1)} collective-permute-done((bf16[512,128]{1,0:T(8,128)(2,1)S(1)}, bf16[512,128]{1,0:T(8,128)(2,1)S(1)}, u32[]{:S(2)}, u32[]{:S(2)}) %collective-permute-start.3) | collective-permute-done | bytes 131104 | tf_op jit(solution)/shard_map/ppermute | solution.py:308
  21.3 0.1 collective-permute-start.6
  21.3 0.6 %collective-permute-done.8.got_ref = bf16[256,128]{1,0:T(8,128)(2,1)S(1)} collective-permute-done((bf16[256,128]{1,0:T(8,128)(2,1)S(1)}, bf16[256,128]{1,0:T(8,128)(2,1)S(1)}, u32[]{:S(2)}, u32[]{:S(2)}) %collective-permute-start.8) | collective-permute-done | bytes 65568 | tf_op jit(solution)/shard_map/ppermute | solution.py:308
  22.0 0.5 %collective-permute-start.9 = (f32[128,128]{1,0:T(8,128)S(1)}, f32[128,128]{1,0:T(8,128)S(1)}, u32[]{:S(2)}, u32[]{:S(2)}) collective-permute-start(f32[128,128]{1,0:T(8,128)S(1)} %get-tuple-element.35), channel_id=1, source_target_pairs={{0,16},{4,20},{8,24},{12,28},{16,0},{20,4},{24,8},{28,12},{1,17},{... | collective-permute-start | bytes 196616 | tf_op jit(solution)/shard_map/ppermute | solution.py:308
  22.4 1.3 %gradient.1.first_ref = f32[1024,128]{1,0:T(8,128)S(1)} custom-call(bf16[1024,1024]{1,0:T(8,128)(2,1)S(1)} %get-tuple-element.21.near_ref, bf16[1024,3072]{1,0:T(8,128)(2,1)S(1)} %get-tuple-element.26.waited_ref.rest_ref, bf16[2048,128]{1,0:T(8,128)(2,1)S(1)} %merge.1.blocks), custom_call_target="tpu_custom_call" | custom-call | flops 17179869184 | tf_op jit(solution)/shard_map/gradient/pallas_call | solution.py:403
  23.8 0.0 collective-permute-done.6.blocks
  23.8 2.2 %spread.1.full = f32[4096,128]{1,0:T(8,128)S(1)} custom-call(s32[1024]{0:T(1024)} %touched_hbm.3, bf16[1024,1024]{1,0:T(8,128)(2,1)S(1)} %get-tuple-element.21.near_ref, bf16[1024,3072]{1,0:T(8,128)(2,1)S(1)} %get-tuple-element.26.waited_ref.rest_ref, f32[1024,128]{1,0:T(8,128)S(1)} %gradient.1.first_ref, ...), custom_call_target="tpu_custom_call", output_to_operand_aliasing={{}: (5, {})} | custom-call | bytes 1048576 | tf_op jit(solution)/shard_map/spread/pallas_call | solution.py:414
  26.0 0.3 %collective-permute-done.9.last_ref = f32[128,128]{1,0:T(8,128)S(1)} collective-permute-done((f32[128,128]{1,0:T(8,128)S(1)}, f32[128,128]{1,0:T(8,128)S(1)}, u32[]{:S(2)}, u32[]{:S(2)}) %collective-permute-start.9) | collective-permute-done | bytes 65568 | tf_op jit(solution)/shard_map/ppermute | solution.py:308
  26.3 2.3 %update.1 = (f32[4096,128]{1,0:T(8,128)}, f32[4096,128]{1,0:T(8,128)}, f32[128,128]{1,0:T(8,128)}) custom-call(f32[4096,128]{1,0:T(8,128)S(1)} %spread.1.full, f32[4096,128]{1,0:T(8,128)S(1)} %get-tuple-element.28.table_ref, f32[4096,128]{1,0:T(8,128)S(1)} %get-tuple-element.29.accum_ref, f32[128,128]{1,0:T(8,128)S(1)} %get-tuple-element.34.own_ref, ...), custom_call_target="tpu_custom_call" | custom-call | bytes 1048576 | tf_op jit(solution)/shard_map/update/pallas_call | solution.py:431
  (5 shorter events, 0.1 us)
Async XLA Ops:
  1.5 9.1 %collective-permute-start.2 = (bf16[192,128]{1,0:T(8,128)(2,1)S(1)}, bf16[192,128]{1,0:T(8,128)(2,1)S(1)}, u32[]{:S(2)}, u32[]{:S(2)}) collective-permute-start(bf16[192,128]{1,0:T(8,128)(2,1)S(1)} %pack.1.packed_ref.refs_0_), channel_id=1, source_target_pairs={{0,3},{1,2},{2,1},{3,0},{4,7},{5,6},{6,5},{7,4},{8,11},{9,10},{10,... | collective-permute-start | bytes 147464 | tf_op jit(solution)/shard_map/ppermute | solution.py:308
  6.6 5.0 %collective-permute-start.1 = (bf16[192,128]{1,0:T(8,128)(2,1)S(1)}, bf16[192,128]{1,0:T(8,128)(2,1)S(1)}, u32[]{:S(2)}, u32[]{:S(2)}) collective-permute-start(bf16[192,128]{1,0:T(8,128)(2,1)S(1)} %pack.1.packed_ref.refs_0_), channel_id=1, source_target_pairs={{0,2},{1,3},{2,0},{3,1},{4,6},{5,7},{6,4},{7,5},{8,10},{9,11},{10,... | collective-permute-start | bytes 147464 | tf_op jit(solution)/shard_map/ppermute | solution.py:308
  6.6 5.0 %collective-permute-start = (bf16[192,128]{1,0:T(8,128)(2,1)S(1)}, bf16[192,128]{1,0:T(8,128)(2,1)S(1)}, u32[]{:S(2)}, u32[]{:S(2)}) collective-permute-start(bf16[192,128]{1,0:T(8,128)(2,1)S(1)} %pack.1.packed_ref.refs_0_), channel_id=1, source_target_pairs={{0,1},{1,0},{2,3},{3,2},{4,5},{5,4},{6,7},{7,6},{8,9},{9,8},{10,11... | collective-permute-start | bytes 147464 | tf_op jit(solution)/shard_map/ppermute | solution.py:308
  10.5 4.6 %collective-permute-start.7 = (f32[4,128,128]{2,1,0:T(8,128)S(1)}, f32[4,128,128]{2,1,0:T(8,128)S(1)}, u32[]{:S(2)}, u32[]{:S(2)}) collective-permute-start(f32[4,128,128]{2,1,0:T(8,128)S(1)} %get-tuple-element.30), channel_id=1, source_target_pairs={{0,4},{4,0},{8,12},{12,8},{16,20},{20,16},{24,28},{28,24},{1,5},{5... | collective-permute-start | bytes 786440 | tf_op jit(solution)/shard_map/ppermute | solution.py:308
  11.6 8.5 %collective-permute-start.5 = (bf16[512,128]{1,0:T(8,128)(2,1)S(1)}, bf16[512,128]{1,0:T(8,128)(2,1)S(1)}, u32[]{:S(2)}, u32[]{:S(2)}) collective-permute-start(bf16[512,128]{1,0:T(8,128)(2,1)S(1)} %join.1.refs_0_), channel_id=1, source_target_pairs={{0,24},{4,28},{8,16},{12,20},{16,8},{20,12},{24,0},{28,4},{1,25},{... | collective-permute-start | bytes 393224 | tf_op jit(solution)/shard_map/ppermute | solution.py:308
  14.1 6.2 %collective-permute-start.4 = (bf16[512,128]{1,0:T(8,128)(2,1)S(1)}, bf16[512,128]{1,0:T(8,128)(2,1)S(1)}, u32[]{:S(2)}, u32[]{:S(2)}) collective-permute-start(bf16[512,128]{1,0:T(8,128)(2,1)S(1)} %join.1.refs_0_), channel_id=1, source_target_pairs={{0,16},{4,20},{8,24},{12,28},{16,0},{20,4},{24,8},{28,12},{1,17},{... | collective-permute-start | bytes 393224 | tf_op jit(solution)/shard_map/ppermute | solution.py:308
  14.6 6.6 %collective-permute-start.3 = (bf16[512,128]{1,0:T(8,128)(2,1)S(1)}, bf16[512,128]{1,0:T(8,128)(2,1)S(1)}, u32[]{:S(2)}, u32[]{:S(2)}) collective-permute-start(bf16[512,128]{1,0:T(8,128)(2,1)S(1)} %join.1.refs_0_), channel_id=1, source_target_pairs={{0,8},{4,12},{8,0},{12,4},{16,24},{20,28},{24,16},{28,20},{1,9},{5... | collective-permute-start | bytes 393224 | tf_op jit(solution)/shard_map/ppermute | solution.py:308
  15.2 6.7 %collective-permute-start.8 = (bf16[256,128]{1,0:T(8,128)(2,1)S(1)}, bf16[256,128]{1,0:T(8,128)(2,1)S(1)}, u32[]{:S(2)}, u32[]{:S(2)}) collective-permute-start(bf16[256,128]{1,0:T(8,128)(2,1)S(1)} %get-tuple-element.33), channel_id=1, source_target_pairs={{0,8},{4,12},{8,0},{12,4},{16,24},{20,28},{24,16},{28,20},{1,9},{5... | collective-permute-start | bytes 196616 | tf_op jit(solution)/shard_map/ppermute | solution.py:308
  21.3 2.5 %collective-permute-start.6 = (bf16[2048,128]{1,0:T(8,128)(2,1)S(1)}, bf16[2048,128]{1,0:T(8,128)(2,1)S(1)}, u32[]{:S(2)}, u32[]{:S(2)}) collective-permute-start(bf16[2048,128]{1,0:T(8,128)(2,1)S(1)} %merge.1.blocks), channel_id=1, source_target_pairs={{0,4},{4,0},{8,12},{12,8},{16,20},{20,16},{24,28},{28,24},{1,5},{5... | collective-permute-start | bytes 1572872 | tf_op jit(solution)/shard_map/ppermute | solution.py:308
  22.0 4.3 %collective-permute-start.9 = (f32[128,128]{1,0:T(8,128)S(1)}, f32[128,128]{1,0:T(8,128)S(1)}, u32[]{:S(2)}, u32[]{:S(2)}) collective-permute-start(f32[128,128]{1,0:T(8,128)S(1)} %get-tuple-element.35), channel_id=1, source_target_pairs={{0,16},{4,20},{8,24},{12,28},{16,0},{20,4},{24,8},{28,12},{1,17},{... | collective-permute-start | bytes 196616 | tf_op jit(solution)/shard_map/ppermute | solution.py:308

commit v7 on v6

--- a/solution.py
+++ b/solution.py
@@ -10,6 +10,7 @@
 
 learn_rate = 0.5
 LANES = 128
+spots = (0, 3, 1, 2)
 MIB = 1 << 20
 
 
@@ -123,8 +124,15 @@
 
     def one(j, carry):
         distance = jnp.bitwise_xor(j * LANES // rows, me)
-        half = jnp.bitwise_and(distance, 1) * (counts_ref.shape[1] // 2) + place * (blocks * LANES // 2)
-        at_column = half + lax.shift_right_logical(distance, 1) * rows + j * LANES % rows
+        chip = lax.shift_right_logical(distance, 1)
+        spot = jnp.where(chip == 3, 1, jnp.where(chip == 0, 0, chip + 1))
+        at_column = (
+            jnp.bitwise_and(distance, 1) * (counts_ref.shape[1] // 2)
+            + lax.shift_right_logical(spot, 1) * (counts_ref.shape[1] // 4)
+            + place * (2 * rows)
+            + jnp.bitwise_and(spot, 1) * rows
+            + j * LANES % rows
+        )
         columns = pl.ds(pl.multiple_of(at_column, LANES), LANES)
         lows, highs, weights = [], [], []
         for h in range(hots):
@@ -178,7 +186,7 @@
         )
     for half, ref in ((0, keep_ref), (bags // 2, send_ref)):
         for c in range(mp // 2):
-            ref[c] = sum_t[:, pl.ds(half + c * rows, rows)].T
+            ref[c] = sum_t[:, pl.ds(half + spots.index(c) * rows, rows)].T
 
 
 def join_kernel(rows, *refs):
@@ -196,7 +204,7 @@
 
 def fold_kernel(rows, own_ref, next_ref, got_ref, own_out, next_out):
     own_out[...] = own_ref[...] + got_ref[pl.ds(0, rows), :].astype(jnp.float32)
-    next_out[...] = next_ref[...] + got_ref[pl.ds(rows, rows), :].astype(jnp.float32)
+    next_out[...] = (next_ref[...] + got_ref[pl.ds(rows, rows), :].astype(jnp.float32)).astype(next_out.dtype)
 
 
 def counts_kernel(hots, accum_hbm, *refs):
@@ -237,31 +245,42 @@
     )(*values, *others)
 
 
-def parity_sum(odd, parts, rows, near_ref, rest_ref, blocks, grads):
-    span = parts * rows
-    replicas = grads.shape[0] // span
-    for c in range(parts):
+def pair_kernel(group, rows, near_ref, rest_ref, *refs):
+    pair, before, (sum_ref, grads) = refs[:2], refs[2:-2], refs[-2:]
+    replicas = pair[0].shape[0] // rows
+    for d in range(replicas):
+        for p, ref in enumerate(pair):
+            grads[pl.ds((2 * d + p) * rows, rows), :] = ref[pl.ds(d * rows, rows), :]
+    near, rest = near_ref.shape[1] // 4, rest_ref.shape[1] // 4
+    total = jnp.dot(
+        near_ref[:, pl.ds(group * near, near)], grads[pl.ds(0, near), :], preferred_element_type=jnp.float32
+    ) + jnp.dot(
+        rest_ref[:, pl.ds(group * rest, rest)], grads[pl.ds(near, rest), :], preferred_element_type=jnp.float32
+    )
+    for ref in before:
+        total = total + ref[...]
+    sum_ref[...] = total
+
+
+def other_core_sum(rows, near_ref, rest_ref, blocks, grads):
+    replicas = blocks.shape[0] // (len(spots) * rows)
+    near, rest = near_ref.shape[1] // 2, rest_ref.shape[1] // 2
+    for spot, c in enumerate(spots):
         for d in range(replicas):
-            grads[pl.ds(d * span + c * rows, rows), :] = blocks[pl.ds((c * replicas + d) * rows, rows), :]
-    near = near_ref.shape[1] // 2
-    rest = rest_ref.shape[1] // 2
+            group, p = divmod(spot, 2)
+            place = spot * rows if d == 0 else near + ((group * (replicas - 1) + d - 1) * 2 + p) * rows
+            grads[pl.ds(place, rows), :] = blocks[pl.ds((c * replicas + d) * rows, rows), :]
     return jnp.dot(
-        near_ref[:, pl.ds(odd * near, near)], grads[pl.ds(0, near), :], preferred_element_type=jnp.float32
-    ) + jnp.dot(
-        rest_ref[:, pl.ds(odd * rest, rest)], grads[pl.ds(near, rest), :], preferred_element_type=jnp.float32
-    )
-
-
-def grad_kernel(parts, rows, near_ref, rest_ref, blocks, sum_ref, grads):
-    sum_ref[...] = parity_sum(0, parts, rows, near_ref, rest_ref, blocks, grads)
-
-
-def spread_kernel(parts, rows, touched_hbm, near_ref, rest_ref, first_ref, blocks, blank_ref, full, grads, summed,
+        near_ref[:, pl.ds(near, near)], grads[pl.ds(0, near), :], preferred_element_type=jnp.float32
+    ) + jnp.dot(rest_ref[:, pl.ds(rest, rest)], grads[pl.ds(near, rest), :], preferred_element_type=jnp.float32)
+
+
+def spread_kernel(rows, touched_hbm, near_ref, rest_ref, first_ref, blocks, blank_ref, full, grads, summed,
                   touched_ref, sem):
     load = pltpu.make_async_copy(touched_hbm, touched_ref, sem)
     load.start()
     del blank_ref
-    summed[...] = first_ref[...] + parity_sum(1, parts, rows, near_ref, rest_ref, blocks, grads)
+    summed[...] = first_ref[...] + other_core_sum(rows, near_ref, rest_ref, blocks, grads)
     load.wait()
 
     def scatter(i, carry):
@@ -275,7 +294,7 @@
 
 def update_kernel(full, table_ref, accum_ref, own_ref, last_ref, new_table_ref, new_accum_ref, pooled_ref,
                   table_vmem, accum_vmem, pooled_vmem, out_sem):
-    pooled_vmem[...] = own_ref[...] + last_ref[...]
+    pooled_vmem[...] = own_ref[...] + last_ref[...].astype(jnp.float32)
     stores = [pltpu.make_async_copy(pooled_vmem, pooled_ref, out_sem.at[2, 0])]
     stores[0].start()
     chunks = 8
@@ -367,7 +386,7 @@
     )(keep, got)
     own_sum, next_sum = pl.pallas_call(
         functools.partial(fold_kernel, rows),
-        out_shape=[block] * 2,
+        out_shape=[block, jax.ShapeDtypeStruct((rows, feature), low)],
         in_specs=[vmem()] * 3,
         out_specs=[vmem()] * 2,
         compiler_params=params(8),
@@ -390,6 +409,19 @@
         name="count",
     )(in_hbm(accum), *peers)
 
+    def pair_sum(group, pair, before, flops):
+        return pl.pallas_call(
+            functools.partial(pair_kernel, group, rows),
+            out_shape=jax.ShapeDtypeStruct((touch, feature), jnp.float32),
+            in_specs=[vmem()] * (4 + len(before)),
+            out_specs=vmem(),
+            scratch_shapes=[pltpu.VMEM((2 * replicas * rows, feature), low)],
+            compiler_params=params(16),
+            cost_estimate=pl.CostEstimate(flops=flops, bytes_accessed=1, transcendentals=0),
+            name="gradient",
+        )(near_counts, rest_counts, *pair, *before)
+
+    early = pair_sum(0, [joined, far[2]], [], 0)
     same = pl.pallas_call(
         merge_kernel,
         out_shape=jax.ShapeDtypeStruct((parts * replicas * rows, feature), low),
@@ -397,22 +429,13 @@
         out_specs=vmem(),
         compiler_params=params(8),
         name="merge",
-    )(rest_counts, joined, *far)
+    )(early, joined, *far)
     other = swap(same, "mp", 1)
 
-    first = pl.pallas_call(
-        functools.partial(grad_kernel, parts, rows),
-        out_shape=jax.ShapeDtypeStruct((touch, feature), jnp.float32),
-        in_specs=[vmem()] * 3,
-        out_specs=vmem(),
-        scratch_shapes=[pltpu.VMEM((bags * replicas // 2, feature), low)],
-        compiler_params=params(16),
-        cost_estimate=pl.CostEstimate(flops=1 << 34, bytes_accessed=0, transcendentals=0),
-        name="gradient",
-    )(near_counts, rest_counts, same)
+    first = pair_sum(1, far[:2], [early], 1 << 34)
 
     full = pl.pallas_call(
-        functools.partial(spread_kernel, parts, rows),
+        functools.partial(spread_kernel, rows),
         out_shape=jax.ShapeDtypeStruct((table_rows, feature), jnp.float32),
         in_specs=[hbm()] + [vmem()] * 5,
         out_specs=vmem(),

time: 28.8 us -> 28.5 us (0.990)
  waiting for transfers between devices: 3 us -> 2.28 us
    ppermute x10, waiting for transfers between devices: 3 us -> 2.28 us  [swap(): lax.ppermute(value, axis, [(i, i ^ distance) for i in range(lax.axis_size...]
    pallas_call x3 -> x4, Pallas kernels: 3.5 us -> 3.66 us  [the longest x1 2.18 us: per_device_small(): pl.pallas_call(functools.partial(spread_kernel, rows), out_shape=jax.Shap...]
  transfers between devices with their start and end apart: 10 -> 10, of which waited for: 5 -> 4; matrix products, arithmetic and copies ran while one was open for 0% -> 0% of each run, Pallas kernels for 36% -> 37%
where the time goes in v7:
time: 28.5 us; the launch traced here: 28.2 us
  Pallas kernels  13.5 us (47%)
  starting transfers between devices  11.7 us (41%)
  waiting for transfers between devices  2.28 us (8%)
  between operations  0.75 us (3%)
    ppermute x10, starting transfers between devices, swap(): lax.ppermute(value, axis, [(i, i ^ distance) for i in range(lax.axis_size...  11.7 us
    pallas_call x1, Pallas kernels, per_device_small(): pl.pallas_call(functools.partial(counts_kernel, hots), out_shape=[jax.Sha...  3.36 us
    pallas_call x1, Pallas kernels, per_device_small(): pl.pallas_call(functools.partial(pooled_kernel, hots, mp), out_shape=[jax...  3.28 us
    ppermute x10, waiting for transfers between devices, swap(): lax.ppermute(value, axis, [(i, i ^ distance) for i in range(lax.axis_size...  2.28 us
    pallas_call x1, Pallas kernels, per_device_small(): pl.pallas_call(update_kernel, out_shape=[jax.ShapeDtypeStruct(table.shape...  2.27 us
    pallas_call x1, Pallas kernels, per_device_small(): pl.pallas_call(functools.partial(spread_kernel, rows), out_shape=jax.Shap...  2.18 us
    pallas_call x2, Pallas kernels, pair_sum(): pl.pallas_call(functools.partial(pair_kernel, group, rows), out_shape=jax...  1.46 us
    pallas_call x1, Pallas kernels, per_device_small(): pl.pallas_call(pack_kernel, out_shape=jax.ShapeDtypeStruct((rows + 2 * lo...  0.85 us
  transfers between devices with their start and end apart: 10, of which 4 were waited for; matrix products, arithmetic and copies ran while one was open for 0% of the time, Pallas kernels for 37%

profile of v7, /device:TPU:0, one launch (start us, length us, event | category | flops | bytes accessed | tf_op | source)
XLA Modules:
  0.0 28.2 jit_solution(324649101200797935)
XLA Ops:
  0.6 0.9 %pack.1.packed_ref.refs_0_ = bf16[192,128]{1,0:T(8,128)(2,1)S(1)} custom-call(bf16[128,128]{1,0:T(8,128)(2,1)} %grad_hbm.1, s32[4,1024]{1,0:T(4,128)} %bitcast.2, s32[4,1024]{1,0:T(4,128)} %bitcast.3), custom_call_target="tpu_custom_call" | custom-call | tf_op jit(solution)/shard_map/pack/pallas_call | solution.py:329
  1.5 5.1 %collective-permute-start.2 = (bf16[192,128]{1,0:T(8,128)(2,1)S(1)}, bf16[192,128]{1,0:T(8,128)(2,1)S(1)}, u32[]{:S(2)}, u32[]{:S(2)}) collective-permute-start(bf16[192,128]{1,0:T(8,128)(2,1)S(1)} %pack.1.packed_ref.refs_0_), channel_id=1, source_target_pairs={{0,3},{1,2},{2,1},{3,0},{4,7},{5,6},{6,5},{7,4},{8,11},{9,10},{10,... | collective-permute-start | bytes 147464 | tf_op jit(solution)/shard_map/ppermute | solution.py:327
  6.6 0.0 collective-permute-start.1
  6.6 0.6 %collective-permute-start = (bf16[192,128]{1,0:T(8,128)(2,1)S(1)}, bf16[192,128]{1,0:T(8,128)(2,1)S(1)}, u32[]{:S(2)}, u32[]{:S(2)}) collective-permute-start(bf16[192,128]{1,0:T(8,128)(2,1)S(1)} %pack.1.packed_ref.refs_0_), channel_id=1, source_target_pairs={{0,1},{1,0},{2,3},{3,2},{4,5},{5,4},{6,7},{7,6},{8,9},{9,8},{10,11... | collective-permute-start | bytes 147464 | tf_op jit(solution)/shard_map/ppermute | solution.py:327
  7.2 3.3 %pool.1 = (f32[4,128,128]{2,1,0:T(8,128)S(1)}, f32[4,128,128]{2,1,0:T(8,128)S(1)}, bf16[1024,1024]{1,0:T(8,128)(2,1)S(1)}, f32[4096,128]{1,0:T(8,128)S(1)}) custom-call(s32[1024]{0:T(1024)} %touched_hbm.3, bf16[192,128]{1,0:T(8,128)(2,1)S(1)} %pack.1.packed_ref.refs_0_, f32[4096,128]{1,0:T(8,128)} %table_hbm.1), custom_call_target="tpu_custom_call" | custom-call | flops 268435456 | bytes 8388608 | tf_op jit(solution)/shard_map/pool/pallas_call | solution.py:342
  10.5 0.1 collective-permute-start.7
  10.6 0.0 collective-permute-done.2.refs_2_
  10.6 1.0 %collective-permute-done.1.refs_1_ = bf16[192,128]{1,0:T(8,128)(2,1)S(1)} collective-permute-done((bf16[192,128]{1,0:T(8,128)(2,1)S(1)}, bf16[192,128]{1,0:T(8,128)(2,1)S(1)}, u32[]{:S(2)}, u32[]{:S(2)}) %collective-permute-start.1) | collective-permute-done | bytes 49184 | tf_op jit(solution)/shard_map/ppermute | solution.py:327
  11.6 0.0 collective-permute-done.refs_0_
  11.6 2.5 %collective-permute-start.5 = (bf16[512,128]{1,0:T(8,128)(2,1)S(1)}, bf16[512,128]{1,0:T(8,128)(2,1)S(1)}, u32[]{:S(2)}, u32[]{:S(2)}) collective-permute-start(bf16[512,128]{1,0:T(8,128)(2,1)S(1)} %join.1.refs_0_), channel_id=1, source_target_pairs={{0,24},{4,28},{8,16},{12,20},{16,8},{20,12},{24,0},{28,4},{1,25},{... | collective-permute-start | bytes 393224 | tf_op jit(solution)/shard_map/ppermute | solution.py:327
  14.1 0.5 %collective-permute-start.4 = (bf16[512,128]{1,0:T(8,128)(2,1)S(1)}, bf16[512,128]{1,0:T(8,128)(2,1)S(1)}, u32[]{:S(2)}, u32[]{:S(2)}) collective-permute-start(bf16[512,128]{1,0:T(8,128)(2,1)S(1)} %join.1.refs_0_), channel_id=1, source_target_pairs={{0,16},{4,20},{8,24},{12,28},{16,0},{20,4},{24,8},{28,12},{1,17},{... | collective-permute-start | bytes 393224 | tf_op jit(solution)/shard_map/ppermute | solution.py:327
  14.6 0.5 %collective-permute-start.3 = (bf16[512,128]{1,0:T(8,128)(2,1)S(1)}, bf16[512,128]{1,0:T(8,128)(2,1)S(1)}, u32[]{:S(2)}, u32[]{:S(2)}) collective-permute-start(bf16[512,128]{1,0:T(8,128)(2,1)S(1)} %join.1.refs_0_), channel_id=1, source_target_pairs={{0,8},{4,12},{8,0},{12,4},{16,24},{20,28},{24,16},{28,20},{1,9},{5... | collective-permute-start | bytes 393224 | tf_op jit(solution)/shard_map/ppermute | solution.py:327
  15.2 0.0 collective-permute-done.7.got_ref
  15.2 1.6 %collective-permute-start.8 = (bf16[256,128]{1,0:T(8,128)(2,1)S(1)}, bf16[256,128]{1,0:T(8,128)(2,1)S(1)}, u32[]{:S(2)}, u32[]{:S(2)}) collective-permute-start(bf16[256,128]{1,0:T(8,128)(2,1)S(1)} %get-tuple-element.33), channel_id=1, source_target_pairs={{0,8},{4,12},{8,0},{12,4},{16,24},{20,28},{24,16},{28,20},{1,9},{5... | collective-permute-start | bytes 196616 | tf_op jit(solution)/shard_map/ppermute | solution.py:327
  16.8 3.4 %count.1 = (bf16[1024,3072]{1,0:T(8,128)(2,1)S(1)}, f32[4096,128]{1,0:T(8,128)S(1)}, f32[4096,128]{1,0:T(8,128)S(1)}) custom-call(f32[4096,128]{1,0:T(8,128)} %accum_hbm.1, bf16[192,128]{1,0:T(8,128)(2,1)S(1)} %get-tuple-element.23.refs_0_.refs_1_, bf16[192,128]{1,0:T(8,128)(2,1)S(1)} %get-tuple-element.24.refs_1_.refs_2_, ...), custom_call_target="tpu_custom_call" | custom-call | tf_op jit(solution)/shard_map/count/pallas_call | solution.py:397
  20.1 0.0 collective-permute-done.5.refs_1_.refs_3_
  20.1 0.7 %gradient.2.refs_2_.waited_ref = f32[1024,128]{1,0:T(8,128)S(1)} custom-call(bf16[1024,1024]{1,0:T(8,128)(2,1)S(1)} %get-tuple-element.21.near_ref, bf16[1024,3072]{1,0:T(8,128)(2,1)S(1)} %get-tuple-element.26.rest_ref, bf16[512,128]{1,0:T(8,128)(2,1)S(1)} %join.1.refs_0_, bf16[512,128]{1,0:T(8,128)(2,1)S(1)} %collective-permute-done.5.refs_1_.refs_3_), custom_call_target="tpu_custom_call" | custom-call | bytes 1 | tf_op jit(solution)/shard_map/gradient/pallas_call | solution.py:413
  20.9 0.0 collective-permute-done.4.refs_1_.refs_2_
  20.9 0.3 %collective-permute-done.3.refs_0_.refs_1_ = bf16[512,128]{1,0:T(8,128)(2,1)S(1)} collective-permute-done((bf16[512,128]{1,0:T(8,128)(2,1)S(1)}, bf16[512,128]{1,0:T(8,128)(2,1)S(1)}, u32[]{:S(2)}, u32[]{:S(2)}) %collective-permute-start.3) | collective-permute-done | bytes 131104 | tf_op jit(solution)/shard_map/ppermute | solution.py:327
  21.3 0.1 collective-permute-start.6
  21.3 0.6 %collective-permute-done.8.got_ref = bf16[256,128]{1,0:T(8,128)(2,1)S(1)} collective-permute-done((bf16[256,128]{1,0:T(8,128)(2,1)S(1)}, bf16[256,128]{1,0:T(8,128)(2,1)S(1)}, u32[]{:S(2)}, u32[]{:S(2)}) %collective-permute-start.8) | collective-permute-done | bytes 65568 | tf_op jit(solution)/shard_map/ppermute | solution.py:327
  22.0 0.7 %collective-permute-start.9 = (bf16[128,128]{1,0:T(8,128)(2,1)S(1)}, bf16[128,128]{1,0:T(8,128)(2,1)S(1)}, u32[]{:S(2)}, u32[]{:S(2)}) collective-permute-start(bf16[128,128]{1,0:T(8,128)(2,1)S(1)} %get-tuple-element.35), channel_id=1, source_target_pairs={{0,16},{4,20},{8,24},{12,28},{16,0},{20,4},{24,8},{28,12},{1,17},{... | collective-permute-start | bytes 98312 | tf_op jit(solution)/shard_map/ppermute | solution.py:327
  22.6 0.7 %gradient.3.first_ref = f32[1024,128]{1,0:T(8,128)S(1)} custom-call(bf16[1024,1024]{1,0:T(8,128)(2,1)S(1)} %get-tuple-element.21.near_ref, bf16[1024,3072]{1,0:T(8,128)(2,1)S(1)} %get-tuple-element.26.rest_ref, bf16[512,128]{1,0:T(8,128)(2,1)S(1)} %collective-permute-done.3.refs_0_.refs_1_, bf16[512,128]{1,0:T(8,128)(2,1)S(1)} %collective-permute-done.4.refs_1_.refs_2_, ...), custom_call_target="tpu_custom_call" | custom-call | flops 17179869184 | bytes 1 | tf_op jit(solution)/shard_map/gradient/pallas_call | solution.py:413
  23.4 0.0 collective-permute-done.6.blocks
  23.4 2.2 %spread.1.full = f32[4096,128]{1,0:T(8,128)S(1)} custom-call(s32[1024]{0:T(1024)} %touched_hbm.3, bf16[1024,1024]{1,0:T(8,128)(2,1)S(1)} %get-tuple-element.21.near_ref, bf16[1024,3072]{1,0:T(8,128)(2,1)S(1)} %get-tuple-element.26.rest_ref, f32[1024,128]{1,0:T(8,128)S(1)} %gradient.3.first_ref, ...), custom_call_target="tpu_custom_call", output_to_operand_aliasing={{}: (5, {})} | custom-call | bytes 1048576 | tf_op jit(solution)/shard_map/spread/pallas_call | solution.py:437
  25.6 0.4 %collective-permute-done.9.last_ref = bf16[128,128]{1,0:T(8,128)(2,1)S(1)} collective-permute-done((bf16[128,128]{1,0:T(8,128)(2,1)S(1)}, bf16[128,128]{1,0:T(8,128)(2,1)S(1)}, u32[]{:S(2)}, u32[]{:S(2)}) %collective-permute-start.9) | collective-permute-done | bytes 32800 | tf_op jit(solution)/shard_map/ppermute | solution.py:327
  25.9 2.3 %update.1 = (f32[4096,128]{1,0:T(8,128)}, f32[4096,128]{1,0:T(8,128)}, f32[128,128]{1,0:T(8,128)}) custom-call(f32[4096,128]{1,0:T(8,128)S(1)} %spread.1.full, f32[4096,128]{1,0:T(8,128)S(1)} %get-tuple-element.28.table_ref, f32[4096,128]{1,0:T(8,128)S(1)} %get-tuple-element.29.accum_ref, f32[128,128]{1,0:T(8,128)S(1)} %get-tuple-element.34.own_ref, ...), custom_call_target="tpu_custom_call" | custom-call | bytes 1048576 | tf_op jit(solution)/shard_map/update/pallas_call | solution.py:454
  (5 shorter events, 0.1 us)
Async XLA Ops:
  1.5 9.1 %collective-permute-start.2 = (bf16[192,128]{1,0:T(8,128)(2,1)S(1)}, bf16[192,128]{1,0:T(8,128)(2,1)S(1)}, u32[]{:S(2)}, u32[]{:S(2)}) collective-permute-start(bf16[192,128]{1,0:T(8,128)(2,1)S(1)} %pack.1.packed_ref.refs_0_), channel_id=1, source_target_pairs={{0,3},{1,2},{2,1},{3,0},{4,7},{5,6},{6,5},{7,4},{8,11},{9,10},{10,... | collective-permute-start | bytes 147464 | tf_op jit(solution)/shard_map/ppermute | solution.py:327
  6.6 5.0 %collective-permute-start.1 = (bf16[192,128]{1,0:T(8,128)(2,1)S(1)}, bf16[192,128]{1,0:T(8,128)(2,1)S(1)}, u32[]{:S(2)}, u32[]{:S(2)}) collective-permute-start(bf16[192,128]{1,0:T(8,128)(2,1)S(1)} %pack.1.packed_ref.refs_0_), channel_id=1, source_target_pairs={{0,2},{1,3},{2,0},{3,1},{4,6},{5,7},{6,4},{7,5},{8,10},{9,11},{10,... | collective-permute-start | bytes 147464 | tf_op jit(solution)/shard_map/ppermute | solution.py:327
  6.6 5.0 %collective-permute-start = (bf16[192,128]{1,0:T(8,128)(2,1)S(1)}, bf16[192,128]{1,0:T(8,128)(2,1)S(1)}, u32[]{:S(2)}, u32[]{:S(2)}) collective-permute-start(bf16[192,128]{1,0:T(8,128)(2,1)S(1)} %pack.1.packed_ref.refs_0_), channel_id=1, source_target_pairs={{0,1},{1,0},{2,3},{3,2},{4,5},{5,4},{6,7},{7,6},{8,9},{9,8},{10,11... | collective-permute-start | bytes 147464 | tf_op jit(solution)/shard_map/ppermute | solution.py:327
  10.5 4.6 %collective-permute-start.7 = (f32[4,128,128]{2,1,0:T(8,128)S(1)}, f32[4,128,128]{2,1,0:T(8,128)S(1)}, u32[]{:S(2)}, u32[]{:S(2)}) collective-permute-start(f32[4,128,128]{2,1,0:T(8,128)S(1)} %get-tuple-element.30), channel_id=1, source_target_pairs={{0,4},{4,0},{8,12},{12,8},{16,20},{20,16},{24,28},{28,24},{1,5},{5... | collective-permute-start | bytes 786440 | tf_op jit(solution)/shard_map/ppermute | solution.py:327
  11.6 8.5 %collective-permute-start.5 = (bf16[512,128]{1,0:T(8,128)(2,1)S(1)}, bf16[512,128]{1,0:T(8,128)(2,1)S(1)}, u32[]{:S(2)}, u32[]{:S(2)}) collective-permute-start(bf16[512,128]{1,0:T(8,128)(2,1)S(1)} %join.1.refs_0_), channel_id=1, source_target_pairs={{0,24},{4,28},{8,16},{12,20},{16,8},{20,12},{24,0},{28,4},{1,25},{... | collective-permute-start | bytes 393224 | tf_op jit(solution)/shard_map/ppermute | solution.py:327
  14.1 6.8 %collective-permute-start.4 = (bf16[512,128]{1,0:T(8,128)(2,1)S(1)}, bf16[512,128]{1,0:T(8,128)(2,1)S(1)}, u32[]{:S(2)}, u32[]{:S(2)}) collective-permute-start(bf16[512,128]{1,0:T(8,128)(2,1)S(1)} %join.1.refs_0_), channel_id=1, source_target_pairs={{0,16},{4,20},{8,24},{12,28},{16,0},{20,4},{24,8},{28,12},{1,17},{... | collective-permute-start | bytes 393224 | tf_op jit(solution)/shard_map/ppermute | solution.py:327
  14.6 6.6 %collective-permute-start.3 = (bf16[512,128]{1,0:T(8,128)(2,1)S(1)}, bf16[512,128]{1,0:T(8,128)(2,1)S(1)}, u32[]{:S(2)}, u32[]{:S(2)}) collective-permute-start(bf16[512,128]{1,0:T(8,128)(2,1)S(1)} %join.1.refs_0_), channel_id=1, source_target_pairs={{0,8},{4,12},{8,0},{12,4},{16,24},{20,28},{24,16},{28,20},{1,9},{5... | collective-permute-start | bytes 393224 | tf_op jit(solution)/shard_map/ppermute | solution.py:327
  15.2 6.7 %collective-permute-start.8 = (bf16[256,128]{1,0:T(8,128)(2,1)S(1)}, bf16[256,128]{1,0:T(8,128)(2,1)S(1)}, u32[]{:S(2)}, u32[]{:S(2)}) collective-permute-start(bf16[256,128]{1,0:T(8,128)(2,1)S(1)} %get-tuple-element.33), channel_id=1, source_target_pairs={{0,8},{4,12},{8,0},{12,4},{16,24},{20,28},{24,16},{28,20},{1,9},{5... | collective-permute-start | bytes 196616 | tf_op jit(solution)/shard_map/ppermute | solution.py:327
  21.3 2.1 %collective-permute-start.6 = (bf16[2048,128]{1,0:T(8,128)(2,1)S(1)}, bf16[2048,128]{1,0:T(8,128)(2,1)S(1)}, u32[]{:S(2)}, u32[]{:S(2)}) collective-permute-start(bf16[2048,128]{1,0:T(8,128)(2,1)S(1)} %merge.1), channel_id=1, source_target_pairs={{0,4},{4,0},{8,12},{12,8},{16,20},{20,16},{24,28},{28,24},{1,5},{5... | collective-permute-start | bytes 1572872 | tf_op jit(solution)/shard_map/ppermute | solution.py:327
  22.0 4.0 %collective-permute-start.9 = (bf16[128,128]{1,0:T(8,128)(2,1)S(1)}, bf16[128,128]{1,0:T(8,128)(2,1)S(1)}, u32[]{:S(2)}, u32[]{:S(2)}) collective-permute-start(bf16[128,128]{1,0:T(8,128)(2,1)S(1)} %get-tuple-element.35), channel_id=1, source_target_pairs={{0,16},{4,20},{8,24},{12,28},{16,0},{20,4},{24,8},{28,12},{1,17},{... | collective-permute-start | bytes 98312 | tf_op jit(solution)/shard_map/ppermute | solution.py:327

commit v8 on v7

--- a/solution.py
+++ b/solution.py
@@ -173,12 +173,12 @@
         load.wait()
 
     def gather(i, carry):
-        for u in range(16):
-            t = i * 16 + u
+        for u in range(128):
+            t = i * 128 + u
             tile[pl.ds(t, 1), :] = table_vmem[pl.ds(touched_ref[t], 1), :]
         return carry
 
-    lax.fori_loop(0, touch // 16, gather, 0)
+    lax.fori_loop(0, touch // 128, gather, 0)
     tile_t = tile[...].T.astype(jnp.bfloat16)
     for half in (0, 1):
         sum_t[:, pl.ds(half * (bags // 2), bags // 2)] = jnp.dot(
@@ -219,12 +219,15 @@
     load.wait()
 
 
-def merge_kernel(waited_ref, *refs):
+def merge_kernel(rows, waited_ref, *refs):
     del waited_ref
     blocks, merged_ref = refs[:-1], refs[-1]
-    span = merged_ref.shape[0] // len(blocks)
-    for c, ref in enumerate(blocks):
-        merged_ref[pl.ds(c * span, span), :] = ref[...]
+    replicas = blocks[0].shape[0] // rows
+    for spot, c in enumerate(spots):
+        group, p = divmod(spot, 2)
+        for d in range(replicas):
+            place = spot if d == 0 else len(spots) + (group * (replicas - 1) + d - 1) * 2 + p
+            merged_ref[pl.ds(place * rows, rows), :] = blocks[c][pl.ds(d * rows, rows), :]
 
 
 def hold_kernel(*refs):
@@ -262,25 +265,18 @@
     sum_ref[...] = total
 
 
-def other_core_sum(rows, near_ref, rest_ref, blocks, grads):
-    replicas = blocks.shape[0] // (len(spots) * rows)
+def other_core_sum(near_ref, rest_ref, blocks):
     near, rest = near_ref.shape[1] // 2, rest_ref.shape[1] // 2
-    for spot, c in enumerate(spots):
-        for d in range(replicas):
-            group, p = divmod(spot, 2)
-            place = spot * rows if d == 0 else near + ((group * (replicas - 1) + d - 1) * 2 + p) * rows
-            grads[pl.ds(place, rows), :] = blocks[pl.ds((c * replicas + d) * rows, rows), :]
     return jnp.dot(
-        near_ref[:, pl.ds(near, near)], grads[pl.ds(0, near), :], preferred_element_type=jnp.float32
-    ) + jnp.dot(rest_ref[:, pl.ds(rest, rest)], grads[pl.ds(near, rest), :], preferred_element_type=jnp.float32)
-
-
-def spread_kernel(rows, touched_hbm, near_ref, rest_ref, first_ref, blocks, blank_ref, full, grads, summed,
-                  touched_ref, sem):
+        near_ref[:, pl.ds(near, near)], blocks[pl.ds(0, near), :], preferred_element_type=jnp.float32
+    ) + jnp.dot(rest_ref[:, pl.ds(rest, rest)], blocks[pl.ds(near, rest), :], preferred_element_type=jnp.float32)
+
+
+def spread_kernel(touched_hbm, near_ref, rest_ref, first_ref, blocks, blank_ref, full, summed, touched_ref, sem):
     load = pltpu.make_async_copy(touched_hbm, touched_ref, sem)
     load.start()
     del blank_ref
-    summed[...] = first_ref[...] + other_core_sum(rows, near_ref, rest_ref, blocks, grads)
+    summed[...] = first_ref[...] + other_core_sum(near_ref, rest_ref, blocks)
     load.wait()
 
     def scatter(i, carry):
@@ -423,7 +419,7 @@
 
     early = pair_sum(0, [joined, far[2]], [], 0)
     same = pl.pallas_call(
-        merge_kernel,
+        functools.partial(merge_kernel, rows),
         out_shape=jax.ShapeDtypeStruct((parts * replicas * rows, feature), low),
         in_specs=[pl.BlockSpec(memory_space=pl.ANY)] + [vmem()] * parts,
         out_specs=vmem(),
@@ -435,13 +431,12 @@
     first = pair_sum(1, far[:2], [early], 1 << 34)
 
     full = pl.pallas_call(
-        functools.partial(spread_kernel, rows),
+        spread_kernel,
         out_shape=jax.ShapeDtypeStruct((table_rows, feature), jnp.float32),
         in_specs=[hbm()] + [vmem()] * 5,
         out_specs=vmem(),
         input_output_aliases={5: 0},
         scratch_shapes=[
-            pltpu.VMEM((bags * replicas // 2, feature), low),
             pltpu.VMEM((touch, feature), jnp.float32),
             pltpu.SMEM((touch,), jnp.int32),
             pltpu.SemaphoreType.DMA,

time: 28.5 us -> 28.3 us (level)
  Pallas kernels: 13.5 us -> 13.2 us
  transfers between devices with their start and end apart: 10 -> 10, of which waited for: 4 -> 4; matrix products, arithmetic and copies ran while one was open for 0% -> 0% of each run, Pallas kernels for 37% -> 36%
where the time goes in v8:
time: 28.3 us; the launch traced here: 28 us
  Pallas kernels  13.2 us (47%)
  starting transfers between devices  11.9 us (42%)
  waiting for transfers between devices  2.16 us (8%)
  between operations  0.75 us (3%)
    ppermute x10, starting transfers between devices, swap(): lax.ppermute(value, axis, [(i, i ^ distance) for i in range(lax.axis_size...  11.9 us
    pallas_call x1, Pallas kernels, per_device_small(): pl.pallas_call(functools.partial(counts_kernel, hots), out_shape=[jax.Sha...  3.36 us
    pallas_call x1, Pallas kernels, per_device_small(): pl.pallas_call(functools.partial(pooled_kernel, hots, mp), out_shape=[jax...  3.04 us
    pallas_call x1, Pallas kernels, per_device_small(): pl.pallas_call(update_kernel, out_shape=[jax.ShapeDtypeStruct(table.shape...  2.27 us
    ppermute x10, waiting for transfers between devices, swap(): lax.ppermute(value, axis, [(i, i ^ distance) for i in range(lax.axis_size...  2.16 us
    pallas_call x1, Pallas kernels, per_device_small(): pl.pallas_call(spread_kernel, out_shape=jax.ShapeDtypeStruct((table_rows,...  2.12 us
    pallas_call x2, Pallas kernels, pair_sum(): pl.pallas_call(functools.partial(pair_kernel, group, rows), out_shape=jax...  1.46 us
    pallas_call x1, Pallas kernels, per_device_small(): pl.pallas_call(pack_kernel, out_shape=jax.ShapeDtypeStruct((rows + 2 * lo...  0.85 us
  transfers between devices with their start and end apart: 10, of which 4 were waited for; matrix products, arithmetic and copies ran while one was open for 0% of the time, Pallas kernels for 36%

profile of v8, /device:TPU:0, one launch (start us, length us, event | category | flops | bytes accessed | tf_op | source)
XLA Modules:
  0.0 28.0 jit_solution(3316110217271566462)
XLA Ops:
  0.6 0.9 %pack.1.packed_ref.refs_0_ = bf16[192,128]{1,0:T(8,128)(2,1)S(1)} custom-call(bf16[128,128]{1,0:T(8,128)(2,1)} %grad_hbm.1, s32[4,1024]{1,0:T(4,128)} %bitcast.2, s32[4,1024]{1,0:T(4,128)} %bitcast.3), custom_call_target="tpu_custom_call" | custom-call | tf_op jit(solution)/shard_map/pack/pallas_call | solution.py:325
  1.5 5.1 %collective-permute-start.2 = (bf16[192,128]{1,0:T(8,128)(2,1)S(1)}, bf16[192,128]{1,0:T(8,128)(2,1)S(1)}, u32[]{:S(2)}, u32[]{:S(2)}) collective-permute-start(bf16[192,128]{1,0:T(8,128)(2,1)S(1)} %pack.1.packed_ref.refs_0_), channel_id=1, source_target_pairs={{0,3},{1,2},{2,1},{3,0},{4,7},{5,6},{6,5},{7,4},{8,11},{9,10},{10,... | collective-permute-start | bytes 147464 | tf_op jit(solution)/shard_map/ppermute | solution.py:323
  6.6 0.0 collective-permute-start.1
  6.6 0.6 %collective-permute-start = (bf16[192,128]{1,0:T(8,128)(2,1)S(1)}, bf16[192,128]{1,0:T(8,128)(2,1)S(1)}, u32[]{:S(2)}, u32[]{:S(2)}) collective-permute-start(bf16[192,128]{1,0:T(8,128)(2,1)S(1)} %pack.1.packed_ref.refs_0_), channel_id=1, source_target_pairs={{0,1},{1,0},{2,3},{3,2},{4,5},{5,4},{6,7},{7,6},{8,9},{9,8},{10,11... | collective-permute-start | bytes 147464 | tf_op jit(solution)/shard_map/ppermute | solution.py:323
  7.2 3.0 %pool.1 = (f32[4,128,128]{2,1,0:T(8,128)S(1)}, f32[4,128,128]{2,1,0:T(8,128)S(1)}, bf16[1024,1024]{1,0:T(8,128)(2,1)S(1)}, f32[4096,128]{1,0:T(8,128)S(1)}) custom-call(s32[1024]{0:T(1024)} %touched_hbm.3, bf16[192,128]{1,0:T(8,128)(2,1)S(1)} %pack.1.packed_ref.refs_0_, f32[4096,128]{1,0:T(8,128)} %table_hbm.1), custom_call_target="tpu_custom_call" | custom-call | flops 268435456 | bytes 8388608 | tf_op jit(solution)/shard_map/pool/pallas_call | solution.py:338
  10.3 0.1 collective-permute-start.7
  10.4 0.0 collective-permute-done.2.refs_2_
  10.4 1.2 %collective-permute-done.1.refs_1_ = bf16[192,128]{1,0:T(8,128)(2,1)S(1)} collective-permute-done((bf16[192,128]{1,0:T(8,128)(2,1)S(1)}, bf16[192,128]{1,0:T(8,128)(2,1)S(1)}, u32[]{:S(2)}, u32[]{:S(2)}) %collective-permute-start.1) | collective-permute-done | bytes 49184 | tf_op jit(solution)/shard_map/ppermute | solution.py:323
  11.6 0.0 collective-permute-done.refs_0_
  11.6 2.5 %collective-permute-start.5 = (bf16[512,128]{1,0:T(8,128)(2,1)S(1)}, bf16[512,128]{1,0:T(8,128)(2,1)S(1)}, u32[]{:S(2)}, u32[]{:S(2)}) collective-permute-start(bf16[512,128]{1,0:T(8,128)(2,1)S(1)} %join.1.refs_0_), channel_id=1, source_target_pairs={{0,24},{4,28},{8,16},{12,20},{16,8},{20,12},{24,0},{28,4},{1,25},{... | collective-permute-start | bytes 393224 | tf_op jit(solution)/shard_map/ppermute | solution.py:323
  14.1 0.5 %collective-permute-start.4 = (bf16[512,128]{1,0:T(8,128)(2,1)S(1)}, bf16[512,128]{1,0:T(8,128)(2,1)S(1)}, u32[]{:S(2)}, u32[]{:S(2)}) collective-permute-start(bf16[512,128]{1,0:T(8,128)(2,1)S(1)} %join.1.refs_0_), channel_id=1, source_target_pairs={{0,16},{4,20},{8,24},{12,28},{16,0},{20,4},{24,8},{28,12},{1,17},{... | collective-permute-start | bytes 393224 | tf_op jit(solution)/shard_map/ppermute | solution.py:323
  14.6 0.5 %collective-permute-start.3 = (bf16[512,128]{1,0:T(8,128)(2,1)S(1)}, bf16[512,128]{1,0:T(8,128)(2,1)S(1)}, u32[]{:S(2)}, u32[]{:S(2)}) collective-permute-start(bf16[512,128]{1,0:T(8,128)(2,1)S(1)} %join.1.refs_0_), channel_id=1, source_target_pairs={{0,8},{4,12},{8,0},{12,4},{16,24},{20,28},{24,16},{28,20},{1,9},{5... | collective-permute-start | bytes 393224 | tf_op jit(solution)/shard_map/ppermute | solution.py:323
  15.2 0.0 collective-permute-done.7.got_ref
  15.2 1.6 %collective-permute-start.8 = (bf16[256,128]{1,0:T(8,128)(2,1)S(1)}, bf16[256,128]{1,0:T(8,128)(2,1)S(1)}, u32[]{:S(2)}, u32[]{:S(2)}) collective-permute-start(bf16[256,128]{1,0:T(8,128)(2,1)S(1)} %get-tuple-element.33), channel_id=1, source_target_pairs={{0,8},{4,12},{8,0},{12,4},{16,24},{20,28},{24,16},{28,20},{1,9},{5... | collective-permute-start | bytes 196616 | tf_op jit(solution)/shard_map/ppermute | solution.py:323
  16.8 3.4 %count.1 = (bf16[1024,3072]{1,0:T(8,128)(2,1)S(1)}, f32[4096,128]{1,0:T(8,128)S(1)}, f32[4096,128]{1,0:T(8,128)S(1)}) custom-call(f32[4096,128]{1,0:T(8,128)} %accum_hbm.1, bf16[192,128]{1,0:T(8,128)(2,1)S(1)} %get-tuple-element.23.refs_0_.refs_1_, bf16[192,128]{1,0:T(8,128)(2,1)S(1)} %get-tuple-element.24.refs_1_.refs_2_, ...), custom_call_target="tpu_custom_call" | custom-call | tf_op jit(solution)/shard_map/count/pallas_call | solution.py:393
  20.1 0.0 collective-permute-done.5.refs_1_.refs_3_
  20.1 0.7 %gradient.2.refs_2_.waited_ref = f32[1024,128]{1,0:T(8,128)S(1)} custom-call(bf16[1024,1024]{1,0:T(8,128)(2,1)S(1)} %get-tuple-element.21.near_ref, bf16[1024,3072]{1,0:T(8,128)(2,1)S(1)} %get-tuple-element.26.rest_ref, bf16[512,128]{1,0:T(8,128)(2,1)S(1)} %join.1.refs_0_, bf16[512,128]{1,0:T(8,128)(2,1)S(1)} %collective-permute-done.5.refs_1_.refs_3_), custom_call_target="tpu_custom_call" | custom-call | bytes 1 | tf_op jit(solution)/shard_map/gradient/pallas_call | solution.py:409
  20.9 0.0 collective-permute-done.4.refs_1_.refs_2_
  20.9 0.1 collective-permute-done.3.refs_0_.refs_1_
  21.1 0.1 collective-permute-start.6
  21.1 0.6 %collective-permute-done.8.got_ref = bf16[256,128]{1,0:T(8,128)(2,1)S(1)} collective-permute-done((bf16[256,128]{1,0:T(8,128)(2,1)S(1)}, bf16[256,128]{1,0:T(8,128)(2,1)S(1)}, u32[]{:S(2)}, u32[]{:S(2)}) %collective-permute-start.8) | collective-permute-done | bytes 65568 | tf_op jit(solution)/shard_map/ppermute | solution.py:323
  21.7 0.9 %collective-permute-start.9 = (bf16[128,128]{1,0:T(8,128)(2,1)S(1)}, bf16[128,128]{1,0:T(8,128)(2,1)S(1)}, u32[]{:S(2)}, u32[]{:S(2)}) collective-permute-start(bf16[128,128]{1,0:T(8,128)(2,1)S(1)} %get-tuple-element.35), channel_id=1, source_target_pairs={{0,16},{4,20},{8,24},{12,28},{16,0},{20,4},{24,8},{28,12},{1,17},{... | collective-permute-start | bytes 98312 | tf_op jit(solution)/shard_map/ppermute | solution.py:323
  22.6 0.7 %gradient.3.first_ref = f32[1024,128]{1,0:T(8,128)S(1)} custom-call(bf16[1024,1024]{1,0:T(8,128)(2,1)S(1)} %get-tuple-element.21.near_ref, bf16[1024,3072]{1,0:T(8,128)(2,1)S(1)} %get-tuple-element.26.rest_ref, bf16[512,128]{1,0:T(8,128)(2,1)S(1)} %collective-permute-done.3.refs_0_.refs_1_, bf16[512,128]{1,0:T(8,128)(2,1)S(1)} %collective-permute-done.4.refs_1_.refs_2_, ...), custom_call_target="tpu_custom_call" | custom-call | flops 17179869184 | bytes 1 | tf_op jit(solution)/shard_map/gradient/pallas_call | solution.py:409
  23.4 0.0 collective-permute-done.6.blocks
  23.4 2.1 %spread.1.full = f32[4096,128]{1,0:T(8,128)S(1)} custom-call(s32[1024]{0:T(1024)} %touched_hbm.3, bf16[1024,1024]{1,0:T(8,128)(2,1)S(1)} %get-tuple-element.21.near_ref, bf16[1024,3072]{1,0:T(8,128)(2,1)S(1)} %get-tuple-element.26.rest_ref, f32[1024,128]{1,0:T(8,128)S(1)} %gradient.3.first_ref, ...), custom_call_target="tpu_custom_call", output_to_operand_aliasing={{}: (5, {})} | custom-call | bytes 1048576 | tf_op jit(solution)/shard_map/spread/pallas_call | solution.py:433
  25.5 0.2 collective-permute-done.9.last_ref
  25.7 2.3 %update.1 = (f32[4096,128]{1,0:T(8,128)}, f32[4096,128]{1,0:T(8,128)}, f32[128,128]{1,0:T(8,128)}) custom-call(f32[4096,128]{1,0:T(8,128)S(1)} %spread.1.full, f32[4096,128]{1,0:T(8,128)S(1)} %get-tuple-element.28.table_ref, f32[4096,128]{1,0:T(8,128)S(1)} %get-tuple-element.29.accum_ref, f32[128,128]{1,0:T(8,128)S(1)} %get-tuple-element.34.own_ref, ...), custom_call_target="tpu_custom_call" | custom-call | bytes 1048576 | tf_op jit(solution)/shard_map/update/pallas_call | solution.py:449
  (5 shorter events, 0.1 us)
Async XLA Ops:
  1.5 8.9 %collective-permute-start.2 = (bf16[192,128]{1,0:T(8,128)(2,1)S(1)}, bf16[192,128]{1,0:T(8,128)(2,1)S(1)}, u32[]{:S(2)}, u32[]{:S(2)}) collective-permute-start(bf16[192,128]{1,0:T(8,128)(2,1)S(1)} %pack.1.packed_ref.refs_0_), channel_id=1, source_target_pairs={{0,3},{1,2},{2,1},{3,0},{4,7},{5,6},{6,5},{7,4},{8,11},{9,10},{10,... | collective-permute-start | bytes 147464 | tf_op jit(solution)/shard_map/ppermute | solution.py:323
  6.6 5.0 %collective-permute-start.1 = (bf16[192,128]{1,0:T(8,128)(2,1)S(1)}, bf16[192,128]{1,0:T(8,128)(2,1)S(1)}, u32[]{:S(2)}, u32[]{:S(2)}) collective-permute-start(bf16[192,128]{1,0:T(8,128)(2,1)S(1)} %pack.1.packed_ref.refs_0_), channel_id=1, source_target_pairs={{0,2},{1,3},{2,0},{3,1},{4,6},{5,7},{6,4},{7,5},{8,10},{9,11},{10,... | collective-permute-start | bytes 147464 | tf_op jit(solution)/shard_map/ppermute | solution.py:323
  6.6 5.0 %collective-permute-start = (bf16[192,128]{1,0:T(8,128)(2,1)S(1)}, bf16[192,128]{1,0:T(8,128)(2,1)S(1)}, u32[]{:S(2)}, u32[]{:S(2)}) collective-permute-start(bf16[192,128]{1,0:T(8,128)(2,1)S(1)} %pack.1.packed_ref.refs_0_), channel_id=1, source_target_pairs={{0,1},{1,0},{2,3},{3,2},{4,5},{5,4},{6,7},{7,6},{8,9},{9,8},{10,11... | collective-permute-start | bytes 147464 | tf_op jit(solution)/shard_map/ppermute | solution.py:323
  10.3 4.9 %collective-permute-start.7 = (f32[4,128,128]{2,1,0:T(8,128)S(1)}, f32[4,128,128]{2,1,0:T(8,128)S(1)}, u32[]{:S(2)}, u32[]{:S(2)}) collective-permute-start(f32[4,128,128]{2,1,0:T(8,128)S(1)} %get-tuple-element.30), channel_id=1, source_target_pairs={{0,4},{4,0},{8,12},{12,8},{16,20},{20,16},{24,28},{28,24},{1,5},{5... | collective-permute-start | bytes 786440 | tf_op jit(solution)/shard_map/ppermute | solution.py:323
  11.6 8.5 %collective-permute-start.5 = (bf16[512,128]{1,0:T(8,128)(2,1)S(1)}, bf16[512,128]{1,0:T(8,128)(2,1)S(1)}, u32[]{:S(2)}, u32[]{:S(2)}) collective-permute-start(bf16[512,128]{1,0:T(8,128)(2,1)S(1)} %join.1.refs_0_), channel_id=1, source_target_pairs={{0,24},{4,28},{8,16},{12,20},{16,8},{20,12},{24,0},{28,4},{1,25},{... | collective-permute-start | bytes 393224 | tf_op jit(solution)/shard_map/ppermute | solution.py:323
  14.1 6.8 %collective-permute-start.4 = (bf16[512,128]{1,0:T(8,128)(2,1)S(1)}, bf16[512,128]{1,0:T(8,128)(2,1)S(1)}, u32[]{:S(2)}, u32[]{:S(2)}) collective-permute-start(bf16[512,128]{1,0:T(8,128)(2,1)S(1)} %join.1.refs_0_), channel_id=1, source_target_pairs={{0,16},{4,20},{8,24},{12,28},{16,0},{20,4},{24,8},{28,12},{1,17},{... | collective-permute-start | bytes 393224 | tf_op jit(solution)/shard_map/ppermute | solution.py:323
  14.6 6.4 %collective-permute-start.3 = (bf16[512,128]{1,0:T(8,128)(2,1)S(1)}, bf16[512,128]{1,0:T(8,128)(2,1)S(1)}, u32[]{:S(2)}, u32[]{:S(2)}) collective-permute-start(bf16[512,128]{1,0:T(8,128)(2,1)S(1)} %join.1.refs_0_), channel_id=1, source_target_pairs={{0,8},{4,12},{8,0},{12,4},{16,24},{20,28},{24,16},{28,20},{1,9},{5... | collective-permute-start | bytes 393224 | tf_op jit(solution)/shard_map/ppermute | solution.py:323
  15.2 6.5 %collective-permute-start.8 = (bf16[256,128]{1,0:T(8,128)(2,1)S(1)}, bf16[256,128]{1,0:T(8,128)(2,1)S(1)}, u32[]{:S(2)}, u32[]{:S(2)}) collective-permute-start(bf16[256,128]{1,0:T(8,128)(2,1)S(1)} %get-tuple-element.33), channel_id=1, source_target_pairs={{0,8},{4,12},{8,0},{12,4},{16,24},{20,28},{24,16},{28,20},{1,9},{5... | collective-permute-start | bytes 196616 | tf_op jit(solution)/shard_map/ppermute | solution.py:323
  21.1 2.3 %collective-permute-start.6 = (bf16[2048,128]{1,0:T(8,128)(2,1)S(1)}, bf16[2048,128]{1,0:T(8,128)(2,1)S(1)}, u32[]{:S(2)}, u32[]{:S(2)}) collective-permute-start(bf16[2048,128]{1,0:T(8,128)(2,1)S(1)} %merge.1), channel_id=1, source_target_pairs={{0,4},{4,0},{8,12},{12,8},{16,20},{20,16},{24,28},{28,24},{1,5},{5... | collective-permute-start | bytes 1572872 | tf_op jit(solution)/shard_map/ppermute | solution.py:323
  21.7 4.0 %collective-permute-start.9 = (bf16[128,128]{1,0:T(8,128)(2,1)S(1)}, bf16[128,128]{1,0:T(8,128)(2,1)S(1)}, u32[]{:S(2)}, u32[]{:S(2)}) collective-permute-start(bf16[128,128]{1,0:T(8,128)(2,1)S(1)} %get-tuple-element.35), channel_id=1, source_target_pairs={{0,16},{4,20},{8,24},{12,28},{16,0},{20,4},{24,8},{28,12},{1,17},{... | collective-permute-start | bytes 98312 | tf_op jit(solution)/shard_map/ppermute | solution.py:323

commit v9 on v8

--- a/solution.py
+++ b/solution.py
@@ -155,7 +155,7 @@
 
 
 def pooled_kernel(hots, mp, touched_hbm, packed_ref, table_hbm, keep_ref, send_ref, counts_ref,
-                  table_vmem, tile, low_rows, code_rows, sum_t, touched_ref, sem):
+                  table_vmem, blank_ref, tile, low_rows, code_rows, sum_t, touched_ref, sem):
     touch = touched_ref.shape[0]
     bags = counts_ref.shape[1]
     rows = bags // mp
@@ -169,6 +169,7 @@
         load.start()
 
     fill_counts(packed_ref, counts_ref, 0, me, hots, low_rows, code_rows)
+    blank_ref[...] = jnp.zeros_like(blank_ref)
     for load in loads:
         load.wait()
 
@@ -208,8 +209,7 @@
 
 
 def counts_kernel(hots, accum_hbm, *refs):
-    peers, (counts_ref, accum_ref, full_ref, low_rows, code_rows, sem) = refs[:-6], refs[-6:]
-    full_ref[...] = jnp.zeros_like(full_ref)
+    peers, (counts_ref, accum_ref, low_rows, code_rows, sem) = refs[:-5], refs[-5:]
     load = pltpu.make_async_copy(accum_hbm, accum_ref, sem)
     load.start()
     me = lax.axis_index("mp")
@@ -335,16 +335,17 @@
     )(in_hbm(pooled_grad), in_hbm(lookup_slots.T), in_hbm(lookup_weights.T))
     peers = [swap(packed, "replica", d) for d in range(1, replicas)]
 
-    keep, send, near_counts, table_held = pl.pallas_call(
+    keep, send, near_counts, table_held, blank = pl.pallas_call(
         functools.partial(pooled_kernel, hots, mp),
         out_shape=[
             jax.ShapeDtypeStruct((mp // 2, rows, feature), jnp.float32),
             jax.ShapeDtypeStruct((mp // 2, rows, feature), jnp.float32),
             jax.ShapeDtypeStruct((touch, bags), low),
             jax.ShapeDtypeStruct((table_rows, feature), jnp.float32),
+            jax.ShapeDtypeStruct((table_rows, feature), jnp.float32),
         ],
         in_specs=[hbm(), vmem(), hbm()],
-        out_specs=[vmem()] * 4,
+        out_specs=[vmem()] * 5,
         scratch_shapes=[
             pltpu.VMEM((touch, feature), jnp.float32),
             pltpu.VMEM((lookups, LANES), jnp.float32),
@@ -390,15 +391,14 @@
     )(own_sum, next_sum, swap(across, "mp", 2))
     last_sum = swap(next_sum, "mp", 4)
 
-    rest_counts, accum_held, blank = pl.pallas_call(
+    rest_counts, accum_held = pl.pallas_call(
         functools.partial(counts_kernel, hots),
         out_shape=[
             jax.ShapeDtypeStruct((touch, bags * (replicas - 1)), low),
             jax.ShapeDtypeStruct((table_rows, feature), jnp.float32),
-            jax.ShapeDtypeStruct((table_rows, feature), jnp.float32),
         ],
         in_specs=[hbm()] + [vmem()] * (replicas - 1),
-        out_specs=[vmem()] * 3,
+        out_specs=[vmem()] * 2,
         scratch_shapes=[pltpu.VMEM((lookups, LANES), jnp.float32)] * 2 + [pltpu.SemaphoreType.DMA],
         compiler_params=params(24),
         cost_estimate=pl.CostEstimate(flops=0, bytes_accessed=0, transcendentals=0),

time: 28.3 us -> 28.3 us (level)
  transfers between devices with their start and end apart: 10 -> 10, of which waited for: 4 -> 4; matrix products, arithmetic and copies ran while one was open for 0% -> 0% of each run, Pallas kernels for 36% -> 35%
where the time goes in v9:
time: 28.3 us; the launch traced here: 28 us
  Pallas kernels  13.1 us (46%)
  starting transfers between devices  11.8 us (42%)
  waiting for transfers between devices  2.44 us (9%)
  between operations  0.75 us (3%)
    ppermute x10, starting transfers between devices, swap(): lax.ppermute(value, axis, [(i, i ^ distance) for i in range(lax.axis_size...  11.8 us
    pallas_call x1, Pallas kernels, per_device_small(): pl.pallas_call(functools.partial(counts_kernel, hots), out_shape=[jax.Sha...  3.22 us
    pallas_call x1, Pallas kernels, per_device_small(): pl.pallas_call(functools.partial(pooled_kernel, hots, mp), out_shape=[jax...  3.04 us
    ppermute x10, waiting for transfers between devices, swap(): lax.ppermute(value, axis, [(i, i ^ distance) for i in range(lax.axis_size...  2.44 us
    pallas_call x1, Pallas kernels, per_device_small(): pl.pallas_call(update_kernel, out_shape=[jax.ShapeDtypeStruct(table.shape...  2.27 us
    pallas_call x1, Pallas kernels, per_device_small(): pl.pallas_call(spread_kernel, out_shape=jax.ShapeDtypeStruct((table_rows,...  2.12 us
    pallas_call x2, Pallas kernels, pair_sum(): pl.pallas_call(functools.partial(pair_kernel, group, rows), out_shape=jax...  1.46 us
    pallas_call x1, Pallas kernels, per_device_small(): pl.pallas_call(pack_kernel, out_shape=jax.ShapeDtypeStruct((rows + 2 * lo...  0.85 us
  transfers between devices with their start and end apart: 10, of which 4 were waited for; matrix products, arithmetic and copies ran while one was open for 0% of the time, Pallas kernels for 35%

profile of v9, /device:TPU:0, one launch (start us, length us, event | category | flops | bytes accessed | tf_op | source)
XLA Modules:
  0.0 28.0 jit_solution(12689660818777147335)
XLA Ops:
  0.6 0.9 %pack.1.packed_ref.refs_0_ = bf16[192,128]{1,0:T(8,128)(2,1)S(1)} custom-call(bf16[128,128]{1,0:T(8,128)(2,1)} %grad_hbm.1, s32[4,1024]{1,0:T(4,128)} %bitcast.2, s32[4,1024]{1,0:T(4,128)} %bitcast.3), custom_call_target="tpu_custom_call" | custom-call | tf_op jit(solution)/shard_map/pack/pallas_call | solution.py:325
  1.5 5.1 %collective-permute-start.2 = (bf16[192,128]{1,0:T(8,128)(2,1)S(1)}, bf16[192,128]{1,0:T(8,128)(2,1)S(1)}, u32[]{:S(2)}, u32[]{:S(2)}) collective-permute-start(bf16[192,128]{1,0:T(8,128)(2,1)S(1)} %pack.1.packed_ref.refs_0_), channel_id=1, source_target_pairs={{0,3},{1,2},{2,1},{3,0},{4,7},{5,6},{6,5},{7,4},{8,11},{9,10},{10,... | collective-permute-start | bytes 147464 | tf_op jit(solution)/shard_map/ppermute | solution.py:323
  6.6 0.0 collective-permute-start.1
  6.6 0.6 %collective-permute-start = (bf16[192,128]{1,0:T(8,128)(2,1)S(1)}, bf16[192,128]{1,0:T(8,128)(2,1)S(1)}, u32[]{:S(2)}, u32[]{:S(2)}) collective-permute-start(bf16[192,128]{1,0:T(8,128)(2,1)S(1)} %pack.1.packed_ref.refs_0_), channel_id=1, source_target_pairs={{0,1},{1,0},{2,3},{3,2},{4,5},{5,4},{6,7},{7,6},{8,9},{9,8},{10,11... | collective-permute-start | bytes 147464 | tf_op jit(solution)/shard_map/ppermute | solution.py:323
  7.2 3.0 %pool.1 = (f32[4,128,128]{2,1,0:T(8,128)S(1)}, f32[4,128,128]{2,1,0:T(8,128)S(1)}, bf16[1024,1024]{1,0:T(8,128)(2,1)S(1)}, f32[4096,128]{1,0:T(8,128)S(1)}, f32[4096,128]{1,0:T(8,128)S(1)}) custom-call(s32[1024]{0:T(1024)} %touched_hbm.3, bf16[192,128]{1,0:T(8,128)(2,1)S(1)} %pack.1.packed_ref.refs_0_, f32[4096,128]{1,0:T(8,128)} %table_hbm.1), custom_call_target="tpu_custom_call" | custom-call | flops 268435456 | bytes 8388608 | tf_op jit(solution)/shard_map/pool/pallas_call | solution.py:338
  10.3 0.1 collective-permute-start.7
  10.4 0.0 collective-permute-done.2.refs_2_
  10.4 1.2 %collective-permute-done.1.refs_1_ = bf16[192,128]{1,0:T(8,128)(2,1)S(1)} collective-permute-done((bf16[192,128]{1,0:T(8,128)(2,1)S(1)}, bf16[192,128]{1,0:T(8,128)(2,1)S(1)}, u32[]{:S(2)}, u32[]{:S(2)}) %collective-permute-start.1) | collective-permute-done | bytes 49184 | tf_op jit(solution)/shard_map/ppermute | solution.py:323
  11.6 0.0 collective-permute-done.refs_0_
  11.6 2.5 %collective-permute-start.5 = (bf16[512,128]{1,0:T(8,128)(2,1)S(1)}, bf16[512,128]{1,0:T(8,128)(2,1)S(1)}, u32[]{:S(2)}, u32[]{:S(2)}) collective-permute-start(bf16[512,128]{1,0:T(8,128)(2,1)S(1)} %join.1.refs_0_), channel_id=1, source_target_pairs={{0,24},{4,28},{8,16},{12,20},{16,8},{20,12},{24,0},{28,4},{1,25},{... | collective-permute-start | bytes 393224 | tf_op jit(solution)/shard_map/ppermute | solution.py:323
  14.1 0.5 %collective-permute-start.4 = (bf16[512,128]{1,0:T(8,128)(2,1)S(1)}, bf16[512,128]{1,0:T(8,128)(2,1)S(1)}, u32[]{:S(2)}, u32[]{:S(2)}) collective-permute-start(bf16[512,128]{1,0:T(8,128)(2,1)S(1)} %join.1.refs_0_), channel_id=1, source_target_pairs={{0,16},{4,20},{8,24},{12,28},{16,0},{20,4},{24,8},{28,12},{1,17},{... | collective-permute-start | bytes 393224 | tf_op jit(solution)/shard_map/ppermute | solution.py:323
  14.6 0.5 %collective-permute-start.3 = (bf16[512,128]{1,0:T(8,128)(2,1)S(1)}, bf16[512,128]{1,0:T(8,128)(2,1)S(1)}, u32[]{:S(2)}, u32[]{:S(2)}) collective-permute-start(bf16[512,128]{1,0:T(8,128)(2,1)S(1)} %join.1.refs_0_), channel_id=1, source_target_pairs={{0,8},{4,12},{8,0},{12,4},{16,24},{20,28},{24,16},{28,20},{1,9},{5... | collective-permute-start | bytes 393224 | tf_op jit(solution)/shard_map/ppermute | solution.py:323
  15.2 0.0 collective-permute-done.7.got_ref
  15.2 1.6 %collective-permute-start.8 = (bf16[256,128]{1,0:T(8,128)(2,1)S(1)}, bf16[256,128]{1,0:T(8,128)(2,1)S(1)}, u32[]{:S(2)}, u32[]{:S(2)}) collective-permute-start(bf16[256,128]{1,0:T(8,128)(2,1)S(1)} %get-tuple-element.33), channel_id=1, source_target_pairs={{0,8},{4,12},{8,0},{12,4},{16,24},{20,28},{24,16},{28,20},{1,9},{5... | collective-permute-start | bytes 196616 | tf_op jit(solution)/shard_map/ppermute | solution.py:323
  16.8 3.2 %count.1 = (bf16[1024,3072]{1,0:T(8,128)(2,1)S(1)}, f32[4096,128]{1,0:T(8,128)S(1)}) custom-call(f32[4096,128]{1,0:T(8,128)} %accum_hbm.1, bf16[192,128]{1,0:T(8,128)(2,1)S(1)} %get-tuple-element.23.refs_0_.refs_1_, bf16[192,128]{1,0:T(8,128)(2,1)S(1)} %get-tuple-element.24.refs_1_.refs_2_, bf16[192,128]{1,0:T(8,128)(2,1)S(1)} %get-tuple-element.25.refs_2_.refs_3_), custom_call_target="tpu_custom_call" | custom-call | tf_op jit(solution)/shard_map/count/pallas_call | solution.py:394
  20.0 0.0 collective-permute-done.5.refs_1_.refs_3_
  20.0 0.7 %gradient.2.refs_2_.waited_ref = f32[1024,128]{1,0:T(8,128)S(1)} custom-call(bf16[1024,1024]{1,0:T(8,128)(2,1)S(1)} %get-tuple-element.21.near_ref, bf16[1024,3072]{1,0:T(8,128)(2,1)S(1)} %get-tuple-element.26.rest_ref, bf16[512,128]{1,0:T(8,128)(2,1)S(1)} %join.1.refs_0_, bf16[512,128]{1,0:T(8,128)(2,1)S(1)} %collective-permute-done.5.refs_1_.refs_3_), custom_call_target="tpu_custom_call" | custom-call | bytes 1 | tf_op jit(solution)/shard_map/gradient/pallas_call | solution.py:409
  20.7 0.0 collective-permute-done.4.refs_1_.refs_2_
  20.8 0.3 %collective-permute-done.3.refs_0_.refs_1_ = bf16[512,128]{1,0:T(8,128)(2,1)S(1)} collective-permute-done((bf16[512,128]{1,0:T(8,128)(2,1)S(1)}, bf16[512,128]{1,0:T(8,128)(2,1)S(1)}, u32[]{:S(2)}, u32[]{:S(2)}) %collective-permute-start.3) | collective-permute-done | bytes 131104 | tf_op jit(solution)/shard_map/ppermute | solution.py:323
  21.1 0.1 collective-permute-start.6
  21.1 0.6 %collective-permute-done.8.got_ref = bf16[256,128]{1,0:T(8,128)(2,1)S(1)} collective-permute-done((bf16[256,128]{1,0:T(8,128)(2,1)S(1)}, bf16[256,128]{1,0:T(8,128)(2,1)S(1)}, u32[]{:S(2)}, u32[]{:S(2)}) %collective-permute-start.8) | collective-permute-done | bytes 65568 | tf_op jit(solution)/shard_map/ppermute | solution.py:323
  21.8 0.8 %collective-permute-start.9 = (bf16[128,128]{1,0:T(8,128)(2,1)S(1)}, bf16[128,128]{1,0:T(8,128)(2,1)S(1)}, u32[]{:S(2)}, u32[]{:S(2)}) collective-permute-start(bf16[128,128]{1,0:T(8,128)(2,1)S(1)} %get-tuple-element.35), channel_id=1, source_target_pairs={{0,16},{4,20},{8,24},{12,28},{16,0},{20,4},{24,8},{28,12},{1,17},{... | collective-permute-start | bytes 98312 | tf_op jit(solution)/shard_map/ppermute | solution.py:323
  22.5 0.7 %gradient.3.first_ref = f32[1024,128]{1,0:T(8,128)S(1)} custom-call(bf16[1024,1024]{1,0:T(8,128)(2,1)S(1)} %get-tuple-element.21.near_ref, bf16[1024,3072]{1,0:T(8,128)(2,1)S(1)} %get-tuple-element.26.rest_ref, bf16[512,128]{1,0:T(8,128)(2,1)S(1)} %collective-permute-done.3.refs_0_.refs_1_, bf16[512,128]{1,0:T(8,128)(2,1)S(1)} %collective-permute-done.4.refs_1_.refs_2_, ...), custom_call_target="tpu_custom_call" | custom-call | flops 17179869184 | bytes 1 | tf_op jit(solution)/shard_map/gradient/pallas_call | solution.py:409
  23.2 0.0 collective-permute-done.6.blocks
  23.3 2.1 %spread.1.full = f32[4096,128]{1,0:T(8,128)S(1)} custom-call(s32[1024]{0:T(1024)} %touched_hbm.3, bf16[1024,1024]{1,0:T(8,128)(2,1)S(1)} %get-tuple-element.21.near_ref, bf16[1024,3072]{1,0:T(8,128)(2,1)S(1)} %get-tuple-element.26.rest_ref, f32[1024,128]{1,0:T(8,128)S(1)} %gradient.3.first_ref, ...), custom_call_target="tpu_custom_call", output_to_operand_aliasing={{}: (5, {})} | custom-call | bytes 1048576 | tf_op jit(solution)/shard_map/spread/pallas_call | solution.py:433
  25.4 0.3 %collective-permute-done.9.last_ref = bf16[128,128]{1,0:T(8,128)(2,1)S(1)} collective-permute-done((bf16[128,128]{1,0:T(8,128)(2,1)S(1)}, bf16[128,128]{1,0:T(8,128)(2,1)S(1)}, u32[]{:S(2)}, u32[]{:S(2)}) %collective-permute-start.9) | collective-permute-done | bytes 32800 | tf_op jit(solution)/shard_map/ppermute | solution.py:323
  25.7 2.3 %update.1 = (f32[4096,128]{1,0:T(8,128)}, f32[4096,128]{1,0:T(8,128)}, f32[128,128]{1,0:T(8,128)}) custom-call(f32[4096,128]{1,0:T(8,128)S(1)} %spread.1.full, f32[4096,128]{1,0:T(8,128)S(1)} %get-tuple-element.28.table_ref, f32[4096,128]{1,0:T(8,128)S(1)} %get-tuple-element.29.accum_ref, f32[128,128]{1,0:T(8,128)S(1)} %get-tuple-element.34.own_ref, ...), custom_call_target="tpu_custom_call" | custom-call | bytes 1048576 | tf_op jit(solution)/shard_map/update/pallas_call | solution.py:449
  (5 shorter events, 0.1 us)
Async XLA Ops:
  1.5 8.9 %collective-permute-start.2 = (bf16[192,128]{1,0:T(8,128)(2,1)S(1)}, bf16[192,128]{1,0:T(8,128)(2,1)S(1)}, u32[]{:S(2)}, u32[]{:S(2)}) collective-permute-start(bf16[192,128]{1,0:T(8,128)(2,1)S(1)} %pack.1.packed_ref.refs_0_), channel_id=1, source_target_pairs={{0,3},{1,2},{2,1},{3,0},{4,7},{5,6},{6,5},{7,4},{8,11},{9,10},{10,... | collective-permute-start | bytes 147464 | tf_op jit(solution)/shard_map/ppermute | solution.py:323
  6.6 5.0 %collective-permute-start.1 = (bf16[192,128]{1,0:T(8,128)(2,1)S(1)}, bf16[192,128]{1,0:T(8,128)(2,1)S(1)}, u32[]{:S(2)}, u32[]{:S(2)}) collective-permute-start(bf16[192,128]{1,0:T(8,128)(2,1)S(1)} %pack.1.packed_ref.refs_0_), channel_id=1, source_target_pairs={{0,2},{1,3},{2,0},{3,1},{4,6},{5,7},{6,4},{7,5},{8,10},{9,11},{10,... | collective-permute-start | bytes 147464 | tf_op jit(solution)/shard_map/ppermute | solution.py:323
  6.6 5.0 %collective-permute-start = (bf16[192,128]{1,0:T(8,128)(2,1)S(1)}, bf16[192,128]{1,0:T(8,128)(2,1)S(1)}, u32[]{:S(2)}, u32[]{:S(2)}) collective-permute-start(bf16[192,128]{1,0:T(8,128)(2,1)S(1)} %pack.1.packed_ref.refs_0_), channel_id=1, source_target_pairs={{0,1},{1,0},{2,3},{3,2},{4,5},{5,4},{6,7},{7,6},{8,9},{9,8},{10,11... | collective-permute-start | bytes 147464 | tf_op jit(solution)/shard_map/ppermute | solution.py:323
  10.3 4.9 %collective-permute-start.7 = (f32[4,128,128]{2,1,0:T(8,128)S(1)}, f32[4,128,128]{2,1,0:T(8,128)S(1)}, u32[]{:S(2)}, u32[]{:S(2)}) collective-permute-start(f32[4,128,128]{2,1,0:T(8,128)S(1)} %get-tuple-element.30), channel_id=1, source_target_pairs={{0,4},{4,0},{8,12},{12,8},{16,20},{20,16},{24,28},{28,24},{1,5},{5... | collective-permute-start | bytes 786440 | tf_op jit(solution)/shard_map/ppermute | solution.py:323
  11.6 8.4 %collective-permute-start.5 = (bf16[512,128]{1,0:T(8,128)(2,1)S(1)}, bf16[512,128]{1,0:T(8,128)(2,1)S(1)}, u32[]{:S(2)}, u32[]{:S(2)}) collective-permute-start(bf16[512,128]{1,0:T(8,128)(2,1)S(1)} %join.1.refs_0_), channel_id=1, source_target_pairs={{0,24},{4,28},{8,16},{12,20},{16,8},{20,12},{24,0},{28,4},{1,25},{... | collective-permute-start | bytes 393224 | tf_op jit(solution)/shard_map/ppermute | solution.py:323
  14.1 6.6 %collective-permute-start.4 = (bf16[512,128]{1,0:T(8,128)(2,1)S(1)}, bf16[512,128]{1,0:T(8,128)(2,1)S(1)}, u32[]{:S(2)}, u32[]{:S(2)}) collective-permute-start(bf16[512,128]{1,0:T(8,128)(2,1)S(1)} %join.1.refs_0_), channel_id=1, source_target_pairs={{0,16},{4,20},{8,24},{12,28},{16,0},{20,4},{24,8},{28,12},{1,17},{... | collective-permute-start | bytes 393224 | tf_op jit(solution)/shard_map/ppermute | solution.py:323
  14.6 6.4 %collective-permute-start.3 = (bf16[512,128]{1,0:T(8,128)(2,1)S(1)}, bf16[512,128]{1,0:T(8,128)(2,1)S(1)}, u32[]{:S(2)}, u32[]{:S(2)}) collective-permute-start(bf16[512,128]{1,0:T(8,128)(2,1)S(1)} %join.1.refs_0_), channel_id=1, source_target_pairs={{0,8},{4,12},{8,0},{12,4},{16,24},{20,28},{24,16},{28,20},{1,9},{5... | collective-permute-start | bytes 393224 | tf_op jit(solution)/shard_map/ppermute | solution.py:323
  15.2 6.5 %collective-permute-start.8 = (bf16[256,128]{1,0:T(8,128)(2,1)S(1)}, bf16[256,128]{1,0:T(8,128)(2,1)S(1)}, u32[]{:S(2)}, u32[]{:S(2)}) collective-permute-start(bf16[256,128]{1,0:T(8,128)(2,1)S(1)} %get-tuple-element.33), channel_id=1, source_target_pairs={{0,8},{4,12},{8,0},{12,4},{16,24},{20,28},{24,16},{28,20},{1,9},{5... | collective-permute-start | bytes 196616 | tf_op jit(solution)/shard_map/ppermute | solution.py:323
  21.1 2.2 %collective-permute-start.6 = (bf16[2048,128]{1,0:T(8,128)(2,1)S(1)}, bf16[2048,128]{1,0:T(8,128)(2,1)S(1)}, u32[]{:S(2)}, u32[]{:S(2)}) collective-permute-start(bf16[2048,128]{1,0:T(8,128)(2,1)S(1)} %merge.1), channel_id=1, source_target_pairs={{0,4},{4,0},{8,12},{12,8},{16,20},{20,16},{24,28},{28,24},{1,5},{5... | collective-permute-start | bytes 1572872 | tf_op jit(solution)/shard_map/ppermute | solution.py:323
  21.8 4.0 %collective-permute-start.9 = (bf16[128,128]{1,0:T(8,128)(2,1)S(1)}, bf16[128,128]{1,0:T(8,128)(2,1)S(1)}, u32[]{:S(2)}, u32[]{:S(2)}) collective-permute-start(bf16[128,128]{1,0:T(8,128)(2,1)S(1)} %get-tuple-element.35), channel_id=1, source_target_pairs={{0,16},{4,20},{8,24},{12,28},{16,0},{20,4},{24,8},{28,12},{1,17},{... | collective-permute-start | bytes 98312 | tf_op jit(solution)/shard_map/ppermute | solution.py:323
